TPU v7x, 256 devices: a whole 4x4x8 slice. The times are simulated.
256 devices in a mesh: slab: 16 (over x, y_lo, core), dom: 16 (over z, y_hi).
Axes of the slice: x: 4, y: 4 (y_hi: 2, y_lo: 2; y = y_hi * 2 + y_lo), z: 8, core: 2. Of those that a mesh axis runs over, the one named last changes fastest.
Arguments:
- rhs: float32 [6, 16, 24576], P(None, 'slab', 'dom'), may hold values from -6 to 6
- dshift: float32 [16, 24576], P('slab', 'dom'), may hold values from 0.5 to 4
- stiff: bfloat16 [16, 4096, 9216], P('slab', 'dom'), may hold values from -0.15625 to 0.15625
- face_k: bfloat16 [16, 2, 64, 9216], P('slab', None, 'dom'), may hold values from -0.625 to 0.625
- elem_col: int32 [16, 4096], P('slab', 'dom'), may hold values from 0 to 15
- elem_row: int32 [16, 4096], P('slab', 'dom'), may hold values from 0 to 255
- face_rows: int32 [16, 2], P('slab'), may hold values from 96 to 384, as said below
Outputs:
- solution: float32 [6, 16, 24576], P(None, 'slab', 'dom')
- residual: float32 [6, 16, 24576], P(None, 'slab', 'dom')
Inputs may be any that keep to these rules, and one draw needn't show every extreme that they name: `face_rows`: in every draw one slab has a lower face with all 384 rows live.
All inputs are finite; a program needn't handle non-finite values.
Results may differ from a plain program's by a relative error of at most 0.0003.
Values sent between devices are 32-bit elements; how exact they have to be, the bound alone decides.
No kernel may reach another device: no remote copies, remote signals or barrier semaphores. Data moves between devices by JAX's collectives and lax.ppermute only.
A program may use at most 64 MiB of HBM per device.

v0:
```python
import jax
import jax.numpy as jnp
from jax import lax
from jax.sharding import Mesh
from jax.sharding import PartitionSpec as P

BLOCK = 96
CASES = 6
ITERS = 2
DOM = ("dom_0", "dom_1")
SLAB = ("slab_0", "slab_1", "slab_2")
SLAB_DOM = ("slab_0", "slab_1", "slab_2", "dom_0", "dom_1")


highest = lax.Precision.HIGHEST


def with_halo(block, sides, width):
    for axis, dim in sides:
        count = lax.axis_size(axis)
        forward = [(i, i + 1) for i in range(count - 1)]
        forward.append((count - 1, 0))
        backward = [(target, source) for source, target in forward]
        low = lax.ppermute(
            lax.slice_in_dim(block, block.shape[dim] - width, None, axis=dim), axis, forward
        )
        high = lax.ppermute(lax.slice_in_dim(block, 0, width, axis=dim), axis, backward)
        block = jnp.concatenate([low, block, high], axis=dim)
    return block


def split_up(value, dim, length):
    before, after = (value.shape[:dim], value.shape[dim + 1 :])
    return jnp.moveaxis(value.reshape(*before, length, -1, *after), dim, 0)


def sent_and_summed(value, axis, dim):
    pieces = split_up(value, dim, lax.axis_size(axis))
    arrived = lax.all_to_all(pieces, axis, split_axis=0, concat_axis=0, tiled=True)
    return arrived.sum(axis=0)


def joined_along(pieces, dim):
    pieces = jnp.moveaxis(pieces, 0, dim)
    shape = pieces.shape
    return pieces.reshape(*shape[:dim], shape[dim] * shape[dim + 1], *shape[dim + 2 :])


def copy_for_each(value, axis):
    length = lax.axis_size(axis)
    return lax.all_to_all(
        jnp.broadcast_to(value[None], (length, *value.shape)), axis, 0, 0, tiled=True
    )


def gather_directly(value, axis, dim):
    return joined_along(copy_for_each(value, axis), dim)


def by_axis(value, axes):
    for axis in axes:
        value = lax.psum(value, axis)
    return value


def body(rhs, dshift, stiff, face_k, elem_col, elem_row, face_rows):
    span = rhs.shape[2]
    own_blocks = span // BLOCK
    face_blocks = face_k.shape[2]
    face_len = face_blocks * BLOCK
    domains = lax.axis_size(DOM)
    slab_rows = own_blocks * domains
    shift_diag = dshift[0]
    matrices = stiff[0].astype(jnp.float32).reshape(-1, BLOCK, BLOCK)
    coupling = face_k[0].astype(jnp.float32).reshape(2, face_blocks, BLOCK, BLOCK)
    columns = elem_col[0]
    targets = elem_row[0]
    to_columns = (jnp.arange(own_blocks, dtype=jnp.int32)[:, None] == columns[None, :]).astype(
        jnp.float32
    )
    to_rows = (jnp.arange(slab_rows, dtype=jnp.int32)[:, None] == targets[None, :]).astype(
        jnp.float32
    )
    positions = jnp.arange(face_len, dtype=jnp.int32)
    mask_low = (positions < face_rows[0, 0]).astype(jnp.float32).reshape(face_blocks, BLOCK)
    mask_up = (positions < face_rows[0, 1]).astype(jnp.float32).reshape(face_blocks, BLOCK)

    def with_faces(vector, lower_add, upper_add):
        return jnp.concatenate(
            [
                vector[:, :face_len] + lower_add,
                vector[:, face_len : span - face_len],
                vector[:, span - face_len :] + upper_add,
            ],
            axis=1,
        )

    def send_back(stacked):
        return with_halo(stacked, ((SLAB, 1),), 1)

    def apply_operator(vector):
        stacked = jnp.stack([vector[:, :face_len], vector[:, span - face_len :]], axis=1)
        haloed = with_halo(stacked, ((SLAB, 1),), 1)
        from_below = haloed[:, 0].reshape(CASES, face_blocks, BLOCK)
        from_above = haloed[:, 3].reshape(CASES, face_blocks, BLOCK)
        term_low = (
            jnp.einsum("iab,cib->cia", coupling[0], from_below, precision=highest) * mask_low
        ).reshape(CASES, face_len)
        term_up = (
            jnp.einsum("iab,cib->cia", coupling[1], from_above, precision=highest) * mask_up
        ).reshape(CASES, face_len)
        picked = vector.reshape(CASES, own_blocks, BLOCK)[:, columns]
        terms = jnp.einsum("eab,ceb->cea", matrices, picked, precision=highest)
        partial_value = jnp.einsum("re,cea->cra", to_rows, terms, precision=highest)
        partial_value = partial_value.reshape(CASES, partial_value.shape[1] * BLOCK)
        image_own = with_faces(sent_and_summed(partial_value, DOM, 1), term_low, term_up)
        image_full = gather_directly(image_own, DOM, 1)
        gathered_rows = image_full.reshape(CASES, -1, BLOCK)[:, targets]
        back_terms = jnp.einsum("eab,cea->ceb", matrices, gathered_rows, precision=highest)
        adjoint = jnp.einsum("re,ceb->crb", to_columns, back_terms, precision=highest).reshape(
            CASES, span
        )
        low_rows = image_own[:, :face_len].reshape(CASES, face_blocks, BLOCK) * mask_low
        up_rows = image_own[:, span - face_len :].reshape(CASES, face_blocks, BLOCK) * mask_up
        back_low = jnp.einsum("iab,cia->cib", coupling[0], low_rows, precision=highest).reshape(
            CASES, face_len
        )
        back_up = jnp.einsum("iab,cia->cib", coupling[1], up_rows, precision=highest).reshape(
            CASES, face_len
        )
        returned = send_back(jnp.stack([back_low, back_up], axis=1))
        adjoint = with_faces(adjoint, returned[:, 0], returned[:, 3])
        return shift_diag[None] * vector + adjoint

    squares = jnp.sum(matrices * matrices, axis=1)
    inner_diag = jnp.dot(to_columns, squares, precision=highest).reshape(1, span)
    face_sq_low = jnp.sum(coupling[0] * coupling[0] * mask_low[:, :, None], axis=1).reshape(
        face_len
    )
    face_sq_up = jnp.sum(coupling[1] * coupling[1] * mask_up[:, :, None], axis=1).reshape(face_len)
    returned_sq = send_back(jnp.stack([face_sq_low, face_sq_up])[None])
    inverse = 1.0 / (
        shift_diag[None] + with_faces(inner_diag, returned_sq[:, 0], returned_sq[:, 3])
    )
    residual = rhs[:, 0]
    solution = jnp.zeros_like(residual)

    def paired_sums(resid, prec, image):
        return (
            by_axis(jnp.sum(resid * prec, axis=1), SLAB_DOM),
            by_axis(jnp.sum(prec * image, axis=1), SLAB_DOM),
        )

    precond = inverse * residual
    image = apply_operator(precond)
    rz_now, curv_now = paired_sums(residual, precond, image)
    step_size = rz_now / curv_now
    direction = precond
    along = image
    for sweep in range(ITERS):
        solution = solution + step_size[:, None] * direction
        residual = residual - step_size[:, None] * along
        if sweep + 1 < ITERS:
            precond = inverse * residual
            image = apply_operator(precond)
            rz_next, curv_now = paired_sums(residual, precond, image)
            step_ratio = rz_next / rz_now
            step_size = rz_next / (curv_now - step_ratio * rz_next / step_size)
            direction = precond + step_ratio[:, None] * direction
            along = image + step_ratio[:, None] * along
            rz_now = rz_next
    return (solution[:, None, :], residual[:, None, :])


def solution(mesh):
    finer = Mesh(
        mesh.devices.reshape(4, 2, 2, 8, 2), ("slab_0", "slab_1", "slab_2", "dom_0", "dom_1")
    )
    placed = (
        P(None, SLAB, DOM),
        P(SLAB, DOM),
        P(SLAB, DOM, None),
        P(SLAB, None, DOM, None),
        P(SLAB, DOM),
        P(SLAB, DOM),
        P(SLAB, None),
    )
    return jax.shard_map(
        body,
        mesh=finer,
        in_specs=placed,
        out_specs=(P(None, SLAB, DOM), P(None, SLAB, DOM)),
        check_vma=False,
    )
```

profile of v0, /device:TPU:1, one launch (start us, length us, event | category | flops | bytes accessed | tf_op | source)
XLA Modules:
  0.0 264.9 jit_solution(7347345298119890545)
XLA Ops:
  0.6 0.9 convert_element_type.37
  1.8 1.3 fusion.59
  5.0 2.8 %collective-permute-start = (f32[1,1,384]{2,1,0:T(1,128)S(1)}, f32[1,1,384]{2,1,0:T(1,128)S(1)}, u32[]{:S(2)}, u32[]{:S(2)}) collective-permute-start(f32[1,1,384]{2,1,0:T(1,128)S(1)} %get-tuple-element.63), channel_id=1, source_target_pairs={{0,16},{16,32},{32,48},{48,64},{64,80},{80,96},{96,112},{112,128},... | collective-permute-start | bytes 4616 | tf_op jit(solution)/shard_map/ppermute | solution.py:24
  7.8 0.7 collective-permute-start.1
  8.5 6.7 %copy.73 = bf16[1,256,9216]{1,2,0:T(8,128)(2,1)} copy(bf16[1,256,9216]{2,1,0:T(8,128)(2,1)} %param.9) | data formatting | bytes 9437184 | tf_op args[2]
  15.2 3.3 %multiply_reduce_fusion = f32[256,96]{0,1:T(8,128)S(1)} fusion(bf16[256,96,96]{0,2,1:T(8,128)(2,1)} %bitcast.147), kind=kLoop, calls=%fused_computation.4 | loop fusion | flops 7053312 | bytes 4816896 | tf_op jit(solution)/shard_map/reduce_sum | solution.py:135
  18.7 8.4 %copy.75 = bf16[256,96,96]{2,1,0:T(8,128)(2,1)} copy(bf16[256,96,96]{0,2,1:T(8,128)(2,1)} %bitcast.148) | data formatting | bytes 9437184 | tf_op jit(solution)/shard_map/squeeze | solution.py:74
  27.6 1.1 collective-permute-start.2
  28.7 1.0 gather_fusion
  29.8 11.9 %convolution_bitcast_fusion.3 = f32[6,256,96]{2,0,1:T(8,128)S(1)} fusion(bf16[256,96,96]{2,1,0:T(8,128)(2,1)} %copy.75, f32[256,6,96]{2,1,0:T(8,128)S(1)} %gather_fusion), kind=kOutput, calls=%fused_computation.8 | convolution fusion | flops 169869312 | bytes 5898240 | tf_op jit(solution)/shard_map/eab,ceb->cea/dot_general | solution.py:113
  41.6 0.8 convolution_bitcast_fusion.5
  43.1 1.3 copy.78
  44.3 10.6 %all-to-all-start = ((f32[16,6,1536]{2,1,0:T(8,128)}), f32[16,6,1536]{2,1,0:T(8,128)S(1)}, u32[]{:S(2)}, u32[]{:S(2)}) async-start(f32[16,6,1536]{2,1,0:T(8,128)} %copy.78), calls=%async_computation | async-start | bytes 1572864 | tf_op jit(solution)/shard_map/all_to_all | solution.py:39
  55.3 1.6 collective-permute-start.3
  57.3 1.2 collective-permute-done.3
  58.9 17.7 %all-to-all-done = f32[16,6,1536]{2,1,0:T(8,128)S(1)} async-done(((f32[16,6,1536]{2,1,0:T(8,128)}), f32[16,6,1536]{2,1,0:T(8,128)S(1)}, u32[]{:S(2)}, u32[]{:S(2)}) %all-to-all-start) | async-done | bytes 589856 | tf_op jit(solution)/shard_map/all_to_all | solution.py:39
  76.7 1.0 broadcast_in_dim.7
  77.6 5.8 %all-to-all-start.1 = ((f32[16,6,1536]{2,1,0:T(8,128)}), f32[16,6,1536]{2,1,0:T(8,128)S(1)}, u32[]{:S(2)}, u32[]{:S(2)}) async-start(f32[16,6,1536]{2,1,0:T(8,128)} %broadcast_in_dim.7), calls=%async_computation.1 | async-start | bytes 1572864 | tf_op jit(solution)/shard_map/all_to_all | solution.py:51
  84.0 1.0 collective-permute-start.4
  85.7 20.0 %all-to-all-done.1 = f32[16,6,1536]{2,1,0:T(8,128)S(1)} async-done(((f32[16,6,1536]{2,1,0:T(8,128)}), f32[16,6,1536]{2,1,0:T(8,128)S(1)}, u32[]{:S(2)}, u32[]{:S(2)}) %all-to-all-start.1) | async-done | bytes 589856 | tf_op jit(solution)/shard_map/all_to_all | solution.py:51
  106.7 1.0 gather_fusion.1
  107.8 7.0 %convolution_bitcast_fusion.2 = f32[6,256,96]{2,0,1:T(8,128)S(1)} fusion(bf16[256,96,96]{2,1,0:T(8,128)(2,1)} %copy.75, f32[256,6,96]{2,1,0:T(8,128)S(1)} %gather_fusion.1), kind=kOutput, calls=%fused_computation.7 | convolution fusion | flops 169869312 | bytes 5898240 | tf_op jit(solution)/shard_map/eab,cea->ceb/dot_general | solution.py:119
  115.6 7.6 %all-reduce.3 = (f32[6]{0:T(128)S(1)}, f32[6]{0:T(128)S(1)}) all-reduce(f32[6]{0:T(128)S(1)} %get-tuple-element.11, f32[6]{0:T(128)S(1)} %get-tuple-element.10), channel_id=1, replica_groups=mesh['slab_0'=4,'slab_1'=2,'slab_2'=2,'dom_0'=8,'dom_1'=2] {'slab_0'}, use_global_device_ids=true, to_apply=%region_4.0 | all-reduce | flops 12 | bytes 96 | tf_op jit(solution)/shard_map/psum | solution.py:62
  123.2 5.4 %all-reduce.9 = (f32[6]{0:T(128)S(1)}, f32[6]{0:T(128)S(1)}) all-reduce(f32[6]{0:T(128)S(1)} %get-tuple-element.20, f32[6]{0:T(128)S(1)} %get-tuple-element.21), channel_id=1, replica_groups=mesh['slab_0'=4,'slab_1'=2,'slab_2'=2,'dom_0'=8,'dom_1'=2] {'slab_1'}, use_global_device_ids=true, to_apply=%region_5.0 | all-reduce | flops 12 | bytes 96 | tf_op jit(solution)/shard_map/psum | solution.py:62
  128.6 7.4 %all-reduce.7 = (f32[6]{0:T(128)S(1)}, f32[6]{0:T(128)S(1)}) all-reduce(f32[6]{0:T(128)S(1)} %get-tuple-element.32, f32[6]{0:T(128)S(1)} %get-tuple-element.33), channel_id=1, replica_groups=mesh['slab_0'=4,'slab_1'=2,'slab_2'=2,'dom_0'=8,'dom_1'=2] {'slab_2'}, use_global_device_ids=true, to_apply=%region_6.0 | all-reduce | flops 12 | bytes 96 | tf_op jit(solution)/shard_map/psum | solution.py:62
  136.1 10.8 %all-reduce.1 = (f32[6]{0:T(128)S(1)}, f32[6]{0:T(128)S(1)}) all-reduce(f32[6]{0:T(128)S(1)} %get-tuple-element.28, f32[6]{0:T(128)S(1)} %get-tuple-element.29), channel_id=1, replica_groups=mesh['slab_0'=4,'slab_1'=2,'slab_2'=2,'dom_0'=8,'dom_1'=2] {'dom_0'}, use_global_device_ids=true, to_apply=%region_7.0 | all-reduce | flops 12 | bytes 96 | tf_op jit(solution)/shard_map/psum | solution.py:62
  146.8 5.3 %all-reduce.5 = (f32[6]{0:T(128)S(1)}, f32[6]{0:T(128)S(1)}) all-reduce(f32[6]{0:T(128)S(1)} %get-tuple-element.16, f32[6]{0:T(128)S(1)} %get-tuple-element.17), channel_id=1, replica_groups=mesh['slab_0'=4,'slab_1'=2,'slab_2'=2,'dom_0'=8,'dom_1'=2] {'dom_1'}, use_global_device_ids=true, to_apply=%region_8.0 | all-reduce | flops 12 | bytes 96 | tf_op jit(solution)/shard_map/psum | solution.py:62
  152.2 1.0 gather_fusion.2
  153.2 11.8 %convolution_bitcast_fusion.1 = f32[6,256,96]{2,0,1:T(8,128)S(1)} fusion(bf16[256,96,96]{2,1,0:T(8,128)(2,1)} %copy.75, f32[256,6,96]{2,1,0:T(8,128)S(1)} %gather_fusion.2), kind=kOutput, calls=%fused_computation.6 | convolution fusion | flops 169869312 | bytes 5898240 | tf_op jit(solution)/shard_map/eab,ceb->cea/dot_general | solution.py:113
  165.0 0.8 convolution_bitcast_fusion.4
  166.5 1.3 copy.97
  167.7 5.4 %all-to-all-start.2 = ((f32[16,6,1536]{2,1,0:T(8,128)}), f32[16,6,1536]{2,1,0:T(8,128)S(1)}, u32[]{:S(2)}, u32[]{:S(2)}) async-start(f32[16,6,1536]{2,1,0:T(8,128)} %copy.97), calls=%async_computation.2 | async-start | bytes 1572864 | tf_op jit(solution)/shard_map/all_to_all | solution.py:39
  173.2 6.4 %collective-permute-start.6 = (f32[6,1,384]{2,0,1:T(8,128)S(1)}, f32[6,1,384]{2,0,1:T(8,128)S(1)}, u32[]{:S(2)}, u32[]{:S(2)}) collective-permute-start(f32[6,1,384]{2,0,1:T(8,128)S(1)} %get-tuple-element.52), channel_id=1, source_target_pairs={{0,16},{16,32},{32,48},{48,64},{64,80},{80,96},{96,112},{112,128},... | collective-permute-start | bytes 27656 | tf_op jit(solution)/shard_map/ppermute | solution.py:24
  179.6 0.8 collective-permute-done.6
  180.9 2.3 collective-permute-done.7
  183.6 6.7 %all-to-all-done.2 = f32[16,6,1536]{2,1,0:T(8,128)S(1)} async-done(((f32[16,6,1536]{2,1,0:T(8,128)}), f32[16,6,1536]{2,1,0:T(8,128)S(1)}, u32[]{:S(2)}, u32[]{:S(2)}) %all-to-all-start.2) | async-done | bytes 589856 | tf_op jit(solution)/shard_map/all_to_all | solution.py:39
  190.5 1.0 broadcast_in_dim.8
  191.4 6.0 %all-to-all-start.3 = ((f32[16,6,1536]{2,1,0:T(8,128)}), f32[16,6,1536]{2,1,0:T(8,128)S(1)}, u32[]{:S(2)}, u32[]{:S(2)}) async-start(f32[16,6,1536]{2,1,0:T(8,128)} %broadcast_in_dim.8), calls=%async_computation.3 | async-start | bytes 1572864 | tf_op jit(solution)/shard_map/all_to_all | solution.py:51
  197.8 6.8 %collective-permute-start.8 = (f32[6,1,384]{2,0,1:T(8,128)S(1)}, f32[6,1,384]{2,0,1:T(8,128)S(1)}, u32[]{:S(2)}, u32[]{:S(2)}) collective-permute-start(f32[6,1,384]{2,0,1:T(8,128)S(1)} %stack_reshape.22), channel_id=1, source_target_pairs={{0,16},{16,32},{32,48},{48,64},{64,80},{80,96},{96,112},{112,128},... | collective-permute-start | bytes 27656 | tf_op jit(solution)/shard_map/ppermute | solution.py:24
  205.0 9.5 %all-to-all-done.3 = f32[16,6,1536]{2,1,0:T(8,128)S(1)} async-done(((f32[16,6,1536]{2,1,0:T(8,128)}), f32[16,6,1536]{2,1,0:T(8,128)S(1)}, u32[]{:S(2)}, u32[]{:S(2)}) %all-to-all-start.3) | async-done | bytes 589856 | tf_op jit(solution)/shard_map/all_to_all | solution.py:51
  215.6 1.0 gather_fusion.3
  216.6 7.0 %convolution_bitcast_fusion = f32[6,256,96]{2,0,1:T(8,128)S(1)} fusion(bf16[256,96,96]{2,1,0:T(8,128)(2,1)} %copy.75, f32[256,6,96]{2,1,0:T(8,128)S(1)} %gather_fusion.3), kind=kOutput, calls=%fused_computation.5 | convolution fusion | flops 169869312 | bytes 5898240 | tf_op jit(solution)/shard_map/eab,cea->ceb/dot_general | solution.py:119
  224.4 6.0 %all-reduce.2 = (f32[6]{0:T(128)S(1)}, f32[6]{0:T(128)S(1)}) all-reduce(f32[6]{0:T(128)S(1)} %get-tuple-element.9, f32[6]{0:T(128)S(1)} %get-tuple-element.8), channel_id=1, replica_groups=mesh['slab_0'=4,'slab_1'=2,'slab_2'=2,'dom_0'=8,'dom_1'=2] {'slab_0'}, use_global_device_ids=true, to_apply=%region_17.0 | all-reduce | flops 12 | bytes 96 | tf_op jit(solution)/shard_map/psum | solution.py:62
  230.4 3.8 %all-reduce.8 = (f32[6]{0:T(128)S(1)}, f32[6]{0:T(128)S(1)}) all-reduce(f32[6]{0:T(128)S(1)} %get-tuple-element.18, f32[6]{0:T(128)S(1)} %get-tuple-element.19), channel_id=1, replica_groups=mesh['slab_0'=4,'slab_1'=2,'slab_2'=2,'dom_0'=8,'dom_1'=2] {'slab_1'}, use_global_device_ids=true, to_apply=%region_18.0 | all-reduce | flops 12 | bytes 96 | tf_op jit(solution)/shard_map/psum | solution.py:62
  234.2 13.2 %all-reduce.6 = (f32[6]{0:T(128)S(1)}, f32[6]{0:T(128)S(1)}) all-reduce(f32[6]{0:T(128)S(1)} %get-tuple-element.30, f32[6]{0:T(128)S(1)} %get-tuple-element.31), channel_id=1, replica_groups=mesh['slab_0'=4,'slab_1'=2,'slab_2'=2,'dom_0'=8,'dom_1'=2] {'slab_2'}, use_global_device_ids=true, to_apply=%region_19.0 | all-reduce | flops 12 | bytes 96 | tf_op jit(solution)/shard_map/psum | solution.py:62
  247.4 10.8 %all-reduce = (f32[6]{0:T(128)S(1)}, f32[6]{0:T(128)S(1)}) all-reduce(f32[6]{0:T(128)S(1)} %get-tuple-element.26, f32[6]{0:T(128)S(1)} %get-tuple-element.27), channel_id=1, replica_groups=mesh['slab_0'=4,'slab_1'=2,'slab_2'=2,'dom_0'=8,'dom_1'=2] {'dom_0'}, use_global_device_ids=true, to_apply=%region_20.0 | all-reduce | flops 12 | bytes 96 | tf_op jit(solution)/shard_map/psum | solution.py:62
  258.2 5.3 %all-reduce.4 = (f32[6]{0:T(128)S(1)}, f32[6]{0:T(128)S(1)}) all-reduce(f32[6]{0:T(128)S(1)} %get-tuple-element.14, f32[6]{0:T(128)S(1)} %get-tuple-element.15), channel_id=1, replica_groups=mesh['slab_0'=4,'slab_1'=2,'slab_2'=2,'dom_0'=8,'dom_1'=2] {'dom_1'}, use_global_device_ids=true, to_apply=%region_21.0 | all-reduce | flops 12 | bytes 96 | tf_op jit(solution)/shard_map/psum | solution.py:62
  263.6 0.7 copy.111
  (126 shorter events, 12.7 us)
Async XLA Ops:
  5.0 22.3 %collective-permute-start = (f32[1,1,384]{2,1,0:T(1,128)S(1)}, f32[1,1,384]{2,1,0:T(1,128)S(1)}, u32[]{:S(2)}, u32[]{:S(2)}) collective-permute-start(f32[1,1,384]{2,1,0:T(1,128)S(1)} %get-tuple-element.63), channel_id=1, source_target_pairs={{0,16},{16,32},{32,48},{48,64},{64,80},{80,96},{96,112},{112,128},... | collective-permute-start | bytes 4616 | tf_op jit(solution)/shard_map/ppermute | solution.py:24
  7.8 10.7 %copy-start.2 = (s32[1,256]{1,0:T(1,128)S(1)}, s32[1,256]{1,0:T(1,128)}, u32[]{:S(2)}) copy-start(s32[1,256]{1,0:T(1,128)} %param.11) | copy-start | bytes 3076
  7.8 19.6 %collective-permute-start.1 = (f32[1,1,384]{2,1,0:T(1,128)S(1)}, f32[1,1,384]{2,1,0:T(1,128)S(1)}, u32[]{:S(2)}, u32[]{:S(2)}) collective-permute-start(f32[1,1,384]{2,1,0:T(1,128)S(1)} %get-tuple-element.64), channel_id=1, source_target_pairs={{16,0},{32,16},{48,32},{64,48},{80,64},{96,80},{112,96},{128,112},... | collective-permute-start | bytes 4616 | tf_op jit(solution)/shard_map/ppermute | solution.py:27
  18.5 8.7 %copy-start = (f32[6,1,1536]{2,1,0:T(1,128)S(1)}, f32[6,1,1536]{2,1,0:T(1,128)}, u32[]{:S(2)}) copy-start(f32[6,1,1536]{2,1,0:T(1,128)} %param.7) | copy-start | bytes 110596
  18.5 8.9 %copy-start.4 = (f32[1,1536]{1,0:T(1,128)S(1)}, f32[1,1536]{1,0:T(1,128)}, u32[]{:S(2)}) copy-start(f32[1,1536]{1,0:T(1,128)} %param.8) | copy-start | bytes 18436
  27.1 14.5 %copy-start.3 = (s32[1,256]{1,0:T(1,128)S(1)}, s32[1,256]{1,0:T(1,128)}, u32[]{:S(2)}) copy-start(s32[1,256]{1,0:T(1,128)} %param.12) | copy-start | bytes 3076
  27.6 29.3 %collective-permute-start.2 = (f32[6,1,384]{2,0,1:T(8,128)S(1)}, f32[6,1,384]{2,0,1:T(8,128)S(1)}, u32[]{:S(2)}, u32[]{:S(2)}) collective-permute-start(f32[6,1,384]{2,0,1:T(8,128)S(1)} %get-tuple-element.59), channel_id=1, source_target_pairs={{0,16},{16,32},{32,48},{48,64},{64,80},{80,96},{96,112},{112,128},... | collective-permute-start | bytes 27656 | tf_op jit(solution)/shard_map/ppermute | solution.py:24
  29.7 25.2 %copy-start.1 = (bf16[1,2,4,9216]{3,2,1,0:T(4,128)(2,1)S(1)}, bf16[1,2,4,9216]{3,2,1,0:T(4,128)(2,1)}, u32[]{:S(2)}) copy-start(bf16[1,2,4,9216]{3,2,1,0:T(4,128)(2,1)} %param.10) | copy-start | bytes 442372
  44.3 32.2 %all-to-all-start = ((f32[16,6,1536]{2,1,0:T(8,128)}), f32[16,6,1536]{2,1,0:T(8,128)S(1)}, u32[]{:S(2)}, u32[]{:S(2)}) async-start(f32[16,6,1536]{2,1,0:T(8,128)} %copy.78), calls=%async_computation | async-start | bytes 1572864 | tf_op jit(solution)/shard_map/all_to_all | solution.py:39
  55.3 3.2 %collective-permute-start.3 = (f32[6,1,384]{2,0,1:T(8,128)S(1)}, f32[6,1,384]{2,0,1:T(8,128)S(1)}, u32[]{:S(2)}, u32[]{:S(2)}) collective-permute-start(f32[6,1,384]{2,0,1:T(8,128)S(1)} %get-tuple-element.60), channel_id=1, source_target_pairs={{16,0},{32,16},{48,32},{64,48},{80,64},{96,80},{112,96},{128,112},... | collective-permute-start | bytes 27656 | tf_op jit(solution)/shard_map/ppermute | solution.py:27
  77.6 28.0 %all-to-all-start.1 = ((f32[16,6,1536]{2,1,0:T(8,128)}), f32[16,6,1536]{2,1,0:T(8,128)S(1)}, u32[]{:S(2)}, u32[]{:S(2)}) async-start(f32[16,6,1536]{2,1,0:T(8,128)} %broadcast_in_dim.7), calls=%async_computation.1 | async-start | bytes 1572864 | tf_op jit(solution)/shard_map/all_to_all | solution.py:51
  84.0 31.3 %collective-permute-start.4 = (f32[6,1,384]{2,0,1:T(8,128)S(1)}, f32[6,1,384]{2,0,1:T(8,128)S(1)}, u32[]{:S(2)}, u32[]{:S(2)}) collective-permute-start(f32[6,1,384]{2,0,1:T(8,128)S(1)} %stack_reshape.20), channel_id=1, source_target_pairs={{0,16},{16,32},{32,48},{48,64},{64,80},{80,96},{96,112},{112,128},... | collective-permute-start | bytes 27656 | tf_op jit(solution)/shard_map/ppermute | solution.py:24
  85.3 30.1 %collective-permute-start.5 = (f32[6,1,384]{2,0,1:T(8,128)S(1)}, f32[6,1,384]{2,0,1:T(8,128)S(1)}, u32[]{:S(2)}, u32[]{:S(2)}) collective-permute-start(f32[6,1,384]{2,0,1:T(8,128)S(1)} %stack_reshape.21), channel_id=1, source_target_pairs={{16,0},{32,16},{48,32},{64,48},{80,64},{96,80},{112,96},{128,112},... | collective-permute-start | bytes 27656 | tf_op jit(solution)/shard_map/ppermute | solution.py:27
  167.7 22.6 %all-to-all-start.2 = ((f32[16,6,1536]{2,1,0:T(8,128)}), f32[16,6,1536]{2,1,0:T(8,128)S(1)}, u32[]{:S(2)}, u32[]{:S(2)}) async-start(f32[16,6,1536]{2,1,0:T(8,128)} %copy.97), calls=%async_computation.2 | async-start | bytes 1572864 | tf_op jit(solution)/shard_map/all_to_all | solution.py:39
  173.2 7.3 %collective-permute-start.6 = (f32[6,1,384]{2,0,1:T(8,128)S(1)}, f32[6,1,384]{2,0,1:T(8,128)S(1)}, u32[]{:S(2)}, u32[]{:S(2)}) collective-permute-start(f32[6,1,384]{2,0,1:T(8,128)S(1)} %get-tuple-element.52), channel_id=1, source_target_pairs={{0,16},{16,32},{32,48},{48,64},{64,80},{80,96},{96,112},{112,128},... | collective-permute-start | bytes 27656 | tf_op jit(solution)/shard_map/ppermute | solution.py:24
  179.6 3.5 %collective-permute-start.7 = (f32[6,1,384]{2,0,1:T(8,128)S(1)}, f32[6,1,384]{2,0,1:T(8,128)S(1)}, u32[]{:S(2)}, u32[]{:S(2)}) collective-permute-start(f32[6,1,384]{2,0,1:T(8,128)S(1)} %get-tuple-element.53), channel_id=1, source_target_pairs={{16,0},{32,16},{48,32},{64,48},{80,64},{96,80},{112,96},{128,112},... | collective-permute-start | bytes 27656 | tf_op jit(solution)/shard_map/ppermute | solution.py:27
  191.4 23.1 %all-to-all-start.3 = ((f32[16,6,1536]{2,1,0:T(8,128)}), f32[16,6,1536]{2,1,0:T(8,128)S(1)}, u32[]{:S(2)}, u32[]{:S(2)}) async-start(f32[16,6,1536]{2,1,0:T(8,128)} %broadcast_in_dim.8), calls=%async_computation.3 | async-start | bytes 1572864 | tf_op jit(solution)/shard_map/all_to_all | solution.py:51
  197.8 26.4 %collective-permute-start.8 = (f32[6,1,384]{2,0,1:T(8,128)S(1)}, f32[6,1,384]{2,0,1:T(8,128)S(1)}, u32[]{:S(2)}, u32[]{:S(2)}) collective-permute-start(f32[6,1,384]{2,0,1:T(8,128)S(1)} %stack_reshape.22), channel_id=1, source_target_pairs={{0,16},{16,32},{32,48},{48,64},{64,80},{80,96},{96,112},{112,128},... | collective-permute-start | bytes 27656 | tf_op jit(solution)/shard_map/ppermute | solution.py:24
  205.0 19.3 %collective-permute-start.9 = (f32[6,1,384]{2,0,1:T(8,128)S(1)}, f32[6,1,384]{2,0,1:T(8,128)S(1)}, u32[]{:S(2)}, u32[]{:S(2)}) collective-permute-start(f32[6,1,384]{2,0,1:T(8,128)S(1)} %stack_reshape.23), channel_id=1, source_target_pairs={{16,0},{32,16},{48,32},{64,48},{80,64},{96,80},{112,96},{128,112},... | collective-permute-start | bytes 27656 | tf_op jit(solution)/shard_map/ppermute | solution.py:27
where the time goes:
time: 270 us; the launch traced here: 265 us
  blocking collectives  75.5 us (28%)
  waiting for transfers between devices  58.2 us (22%)
  starting transfers between devices  48.6 us (18%)
  matrix products  42.1 us (16%)
  local copies, waits for them, and re-layouts  32.5 us (12%)
  other arithmetic  6.88 us (3%)
    psum x10, blocking collectives, by_axis(): value = lax.psum(value, axis)  75.5 us
    all_to_all x2, waiting for transfers between devices, copy_for_each(): lax.all_to_all(jnp.broadcast_to(value[None], (length, *value.shape)), axi...  29.5 us
    all_to_all x2, waiting for transfers between devices, sent_and_summed(): lax.all_to_all(pieces, axis, split_axis=0, concat_axis=0, tiled=True)  24.4 us
    dot_general x2, matrix products, apply_operator(): terms = jnp.einsum('eab,ceb->cea', matrices, picked, precision=highest)  23.7 us
    ppermute x5, starting transfers between devices, with_halo(): lax.ppermute(lax.slice_in_dim(block, block.shape[dim] - width, None, axis...  18.1 us
    all_to_all x2, starting transfers between devices, sent_and_summed(): lax.all_to_all(pieces, axis, split_axis=0, concat_axis=0, tiled=True)  16 us
    dot_general x2, matrix products, apply_operator(): jnp.einsum('eab,cea->ceb', matrices, gathered_rows, precision=highest)  14.1 us
    all_to_all x2, starting transfers between devices, copy_for_each(): lax.all_to_all(jnp.broadcast_to(value[None], (length, *value.shape)), axi...  11.8 us
  transfers between devices with their start and end apart: 14, of which 7 were waited for; matrix products, arithmetic and copies ran while one was open for 22% of the time, Pallas kernels for 0%

commit v1 on v0

v1 whole, which is shorter than its diff:
```python
import jax
import jax.numpy as jnp
from jax import lax
from jax.experimental import pallas as pl
from jax.experimental.pallas import tpu as pltpu
from jax.sharding import Mesh
from jax.sharding import PartitionSpec as P

BLOCK = 96
CASES = 6
DOM = ("dom_0", "dom_1")
SLAB = ("slab_0", "slab_1", "slab_2")
F32 = jnp.float32
BF16 = jnp.bfloat16
LANES = 128
OWN = 16
STORED = 256
SLAB_ROWS = 256
GROUP = 32
STEPS = STORED // GROUP
CHUNK = 72
TILES = 12
FACE = 4
MIB = 1024 * 1024


def lane(rows):
    return lax.broadcasted_iota(jnp.int32, (rows, LANES), 1)


def spread(t0, t1, t2):
    at = lane(t0.shape[0])
    v0 = t0
    v1 = jnp.where(at < 32, pltpu.roll(t0, 32, 1), pltpu.roll(t1, 32, 1))
    v2 = jnp.where(at < 64, pltpu.roll(t1, 64, 1), pltpu.roll(t2, 64, 1))
    v3 = pltpu.roll(t2, 96, 1)
    return [jnp.where(at < BLOCK, v, 0.0) for v in (v0, v1, v2, v3)]


def packed(v0, v1, v2, v3):
    at = lane(v0.shape[0])
    r1 = pltpu.roll(v1, 96, 1)
    r2 = pltpu.roll(v2, 64, 1)
    r3 = pltpu.roll(v3, 32, 1)
    return (
        jnp.where(at < 96, v0, r1),
        jnp.where(at < 64, r1, r2),
        jnp.where(at < 32, r2, r3),
    )


def halves(v):
    high = v.astype(BF16).astype(F32)
    return jnp.concatenate([high, v - high], axis=0).astype(BF16)


def rows_live(shape, dim, live, block):
    at = lax.broadcasted_iota(jnp.int32, shape, dim)
    row = 4 * (at % 24) + at // 24
    return row + block * BLOCK < live


def eight(ref, start):
    if start + 8 <= ref.shape[0]:
        return ref[start : start + 8, :]
    return pltpu.roll(ref[start - 2 : start + 6, :], 6, 0)


def block_of(held, first, stride):
    parts = [held[pl.ds(first + k * (stride // 3), 24, stride=stride), :] for k in range(3)]
    return jnp.concatenate(spread(*parts), axis=0)


def face_prep(live_ref, x_ref, k_ref, sq_ref, held):
    for t in range(CHUNK):
        held[t * 8 : (t + 1) * 8, :] = x_ref[:, t * LANES : (t + 1) * LANES]
    for k in range(2):
        sums = []
        for i in range(FACE):
            whole = block_of(held, k * FACE + i, 24)
            k_ref[k * FACE + i] = whole.astype(BF16)
            masked = jnp.where(rows_live((BLOCK, LANES), 0, live_ref[k], i), whole, 0.0)
            total = jnp.sum(masked * masked, axis=0, keepdims=True)
            sums.append(jnp.broadcast_to(total, (8, LANES)))
        for t, tile in enumerate(packed(*sums)):
            sq_ref[k, :, t * LANES : (t + 1) * LANES] = tile


def stiff_prep(col_ref, x_ref, k_ref, diag_ref, held, acc):
    step = pl.program_id(0)

    @pl.when(step == 0)
    def _():
        acc[...] = jnp.zeros_like(acc)

    for half in range(GROUP // 16):
        for t in range(CHUNK):
            held[t * 16 : (t + 1) * 16, :] = x_ref[
                half * 16 : (half + 1) * 16, t * LANES : (t + 1) * LANES
            ].astype(F32)
        for e in range(16):
            whole = block_of(held, e, 48)
            k_ref[half * 16 + e] = whole.astype(BF16)
            total = jnp.sum((whole * whole).reshape(12, 8, LANES), axis=0)
            j = col_ref[step * GROUP + half * 16 + e]
            acc[j] = acc[j] + total

    @pl.when(step == STEPS - 1)
    def _():
        for q in range(OWN // 4):
            sums = [
                jnp.broadcast_to(jnp.sum(acc[q * 4 + i], axis=0, keepdims=True), (8, LANES))
                for i in range(4)
            ]
            for t, tile in enumerate(packed(*sums)):
                at = (q * 3 + t) * LANES
                diag_ref[:, at : at + LANES] = tile


def forward(col_ref, row_ref, v_ref, k_ref, out_ref, cols, acc):
    step = pl.program_id(0)

    @pl.when(step == 0)
    def _():
        acc[...] = jnp.zeros_like(acc)
        for q in range(OWN // 4):
            tiles = [v_ref[:, (q * 3 + t) * LANES : (q * 3 + t + 1) * LANES] for t in range(3)]
            for i, v in enumerate(spread(*tiles)):
                cols[q * 4 + i] = halves(v)

    for first in range(0, GROUP, 8):
        terms = []
        for e in range(first, first + 8):
            x = cols[col_ref[step * GROUP + e]]
            out = lax.dot_general(
                x, k_ref[e], (((1,), (1,)), ((), ())), preferred_element_type=F32
            )
            terms.append(out[:8] + out[8:])
        for e in range(first, first + 8):
            r = row_ref[step * GROUP + e]
            acc[r, :, :BLOCK] = acc[r, :, :BLOCK] + terms[e - first]

    @pl.when(step == STEPS - 1)
    def _():
        for g in range(SLAB_ROWS // 4):
            for t, tile in enumerate(packed(*[acc[g * 4 + i] for i in range(4)])):
                at = (g // 4) * CHUNK + ((g % 4) * 3 + t) * CASES
                out_ref[at : at + CASES, :] = tile[:CASES]


def adjoint(
    col_ref, row_ref, y_ref, k_ref, v_ref, shift_ref, low_ref, up_ref, out_ref, rows, acc
):
    step = pl.program_id(0)

    @pl.when(step == 0)
    def _():
        acc[...] = jnp.zeros_like(acc)
        for g in range(SLAB_ROWS // 4):
            at = (g // 4) * CHUNK + (g % 4) * 3 * CASES
            tiles = [eight(y_ref, at + t * CASES) for t in range(3)]
            for i, v in enumerate(spread(*tiles)):
                rows[g * 4 + i] = halves(v)

    for first in range(0, GROUP, 8):
        terms = []
        for e in range(first, first + 8):
            y = rows[row_ref[step * GROUP + e]]
            out = jnp.dot(y[:, :BLOCK], k_ref[e], preferred_element_type=F32)
            terms.append(out[:8] + out[8:])
        for e in range(first, first + 8):
            j = col_ref[step * GROUP + e]
            acc[j] = acc[j] + terms[e - first]

    @pl.when(step == STEPS - 1)
    def _():
        for q in range(OWN // 4):
            for t, tile in enumerate(packed(*[acc[q * 4 + i] for i in range(4)])):
                at = (q * 3 + t) * LANES
                to = slice(at, at + LANES)
                whole = tile + shift_ref[:, to] * v_ref[:, to]
                if q == 0:
                    whole = whole + low_ref[:, to]
                if q == OWN // 4 - 1:
                    whole = whole + up_ref[:, t * LANES : (t + 1) * LANES]
                out_ref[:, to] = whole


def summed(at_ref, live_ref, y_ref, low_ref, up_ref, k_ref, out_ref):
    half = at_ref[0]
    whole = y_ref[0]
    for z in range(1, y_ref.shape[0]):
        whole = whole + y_ref[z]
    out_ref[...] = whole
    for k, face_ref in enumerate((low_ref, up_ref)):
        tiles = [face_ref[:, t * LANES : (t + 1) * LANES] for t in range(3)]
        terms = []
        for i, v in enumerate(spread(*tiles)):
            out = lax.dot_general(
                halves(v), k_ref[k * FACE + i], (((1,), (1,)), ((), ())), preferred_element_type=F32
            )
            term = out[:8] + out[8:]
            term = jnp.where(rows_live((8, BLOCK), 1, live_ref[k], i), term, 0.0)
            terms.append(jnp.concatenate([term, jnp.zeros((8, LANES - BLOCK), F32)], axis=1))
        for t, tile in enumerate(packed(*terms)):
            for h in range(2):
                at = h * CHUNK + (k * 9 + t) * CASES
                added = jnp.where(half == h, tile[:CASES], 0.0)
                out_ref[at : at + CASES, :] = out_ref[at : at + CASES, :] + added


def finished(at_ref, live_ref, a_ref, b_ref, k_ref, out_ref, back_ref, square_ref, held):
    half = at_ref[0]
    both = a_ref[...] + b_ref[...]
    for z in range(out_ref.shape[0]):
        out_ref[z] = both
    own = jnp.where(half == 0, both[:CHUNK], both[CHUNK:])
    held[...] = own
    square = jnp.zeros((8, LANES), F32)
    for t in range(TILES):
        tile = eight(held, t * CASES)
        square = square + tile * tile
    square_ref[...] = square
    for k in range(2):
        tiles = [eight(held, (k * 9 + t) * CASES) for t in range(3)]
        terms = []
        for i, v in enumerate(spread(*tiles)):
            v = jnp.where(rows_live((8, LANES), 1, live_ref[k], i), v, 0.0)
            y = halves(v)
            out = jnp.dot(y[:, :BLOCK], k_ref[k * FACE + i], preferred_element_type=F32)
            terms.append(out[:8] + out[8:])
        for t, tile in enumerate(packed(*terms)):
            back_ref[k, :, t * LANES : (t + 1) * LANES] = tile


SMEM = pl.BlockSpec(memory_space=pltpu.SMEM)
VMEM = pl.BlockSpec(memory_space=pltpu.VMEM)
GIVEN = pltpu.CompilerParams(vmem_limit_bytes=24 * MIB)


def shaped(*shape, dtype=F32):
    return jax.ShapeDtypeStruct(shape, dtype)


def whole_block(*shape):
    return pl.BlockSpec(shape, lambda i, *_: (0,) * len(shape))


def per_step(scalars, ins, outs, out_shape, scratch, kernel):
    return pl.pallas_call(
        kernel,
        grid_spec=pltpu.PrefetchScalarGridSpec(
            num_scalar_prefetch=scalars,
            grid=(STEPS,),
            in_specs=ins,
            out_specs=outs,
            scratch_shapes=scratch,
        ),
        out_shape=out_shape,
        compiler_params=GIVEN,
    )


BLOCKS = pl.BlockSpec((GROUP, BLOCK, LANES), lambda i, *_: (i, 0, 0))


def padded(value):
    return jnp.pad(value, ((0, 2), (0, 0)))


def body(rhs, dshift, stiff, face_k, elem_col, elem_row, face_rows):
    span = rhs.shape[2]
    face_len = FACE * BLOCK
    columns, targets = elem_col[0], elem_row[0]
    live = face_rows[0]
    half = lax.axis_index("dom_1").astype(jnp.int32).reshape(1)
    z_count = lax.axis_size("dom_0")
    slabs = lax.axis_size(SLAB)
    up = [(i, (i + 1) % slabs) for i in range(slabs)]
    down = [(b, a) for a, b in up]

    def to_above(value):
        return lax.ppermute(value, SLAB, up)

    def to_below(value):
        return lax.ppermute(value, SLAB, down)

    def lower(value):
        return value[:, :face_len]

    def upper(value):
        return value[:, span - face_len :]

    faces, face_sq = pl.pallas_call(
        face_prep,
        in_specs=[SMEM, VMEM],
        out_specs=(VMEM, VMEM),
        out_shape=(
            shaped(2 * FACE, BLOCK, LANES, dtype=BF16),
            shaped(2, 8, face_len),
        ),
        scratch_shapes=[pltpu.VMEM((CHUNK * 8, LANES), F32)],
        compiler_params=GIVEN,
    )(live, face_k[0].astype(F32).reshape(2 * FACE, BLOCK * BLOCK))
    sq_above = to_below(face_sq[0, :1])
    sq_below = to_above(face_sq[1, :1])

    blocks, inner = per_step(
        1,
        [pl.BlockSpec((GROUP, BLOCK * BLOCK), lambda i, *_: (i, 0))],
        (BLOCKS, whole_block(8, span)),
        (shaped(STORED, BLOCK, LANES, dtype=BF16), shaped(8, span)),
        [pltpu.VMEM((CHUNK * 16, LANES), F32), pltpu.VMEM((OWN, 8, LANES), F32)],
        stiff_prep,
    )(columns, stiff[0])
    total = dshift + inner[:1]
    total = jnp.concatenate(
        [
            lower(total) + sq_below,
            total[:, face_len : span - face_len],
            upper(total) + sq_above,
        ],
        axis=1,
    )
    inverse = 1.0 / total
    residual = padded(rhs[:, 0])
    direction = inverse * residual

    def all_rows(vector):
        from_below = to_above(upper(vector))
        from_above = to_below(lower(vector))
        parts = per_step(
            2,
            [whole_block(8, span), BLOCKS],
            whole_block(OWN * CHUNK, LANES),
            shaped(OWN * CHUNK, LANES),
            [pltpu.VMEM((OWN, 16, LANES), BF16), pltpu.VMEM((SLAB_ROWS, 8, LANES), F32)],
            forward,
        )(columns, targets, vector, blocks)
        parts = parts.reshape(z_count, 2 * CHUNK, LANES)
        arrived = lax.all_to_all(parts, "dom_0", 0, 0, tiled=True)
        mine = pl.pallas_call(
            summed,
            in_specs=[SMEM, SMEM] + [VMEM] * 4,
            out_specs=VMEM,
            out_shape=shaped(2 * CHUNK, LANES),
            compiler_params=GIVEN,
        )(half, live, arrived, from_below, from_above, faces)
        other = lax.ppermute(mine, "dom_1", [(0, 1), (1, 0)])
        copies, back, square = pl.pallas_call(
            finished,
            in_specs=[SMEM, SMEM] + [VMEM] * 3,
            out_specs=(VMEM, VMEM, VMEM),
            out_shape=(
                shaped(z_count, 2 * CHUNK, LANES),
                shaped(2, 8, face_len),
                shaped(8, LANES),
            ),
            scratch_shapes=[pltpu.VMEM((CHUNK, LANES), F32)],
            compiler_params=GIVEN,
        )(half, live, mine, other, faces)
        full = lax.all_to_all(copies, "dom_0", 0, 0, tiled=True)
        low_add = to_above(back[1])
        up_add = to_below(back[0])
        return full.reshape(OWN * CHUNK, LANES), low_add, up_add, square

    def image_of(vector, made):
        full, low_add, up_add, _ = made
        return per_step(
            2,
            [
                whole_block(OWN * CHUNK, LANES),
                BLOCKS,
                whole_block(8, span),
                whole_block(1, span),
                whole_block(8, face_len),
                whole_block(8, face_len),
            ],
            whole_block(8, span),
            shaped(8, span),
            [pltpu.VMEM((SLAB_ROWS, 16, LANES), BF16), pltpu.VMEM((OWN, 8, LANES), F32)],
            adjoint,
        )(columns, targets, full, blocks, vector, dshift, low_add, up_add)

    def inner_product(first, second):
        return jnp.sum(first[:CASES] * second[:CASES], axis=1)

    def everywhere(value, axis):
        count = lax.axis_size(axis)
        sent = jnp.broadcast_to(value[None], (count, *value.shape))
        return lax.all_to_all(sent, axis, 0, 0, tiled=True).sum(axis=0)

    image = image_of(direction, all_rows(direction))
    second = inverse * image
    made = all_rows(second)
    sums = jnp.stack(
        [
            inner_product(residual, direction),
            inner_product(direction, image),
            inner_product(image, second),
            inner_product(dshift * second, second) + jnp.sum(made[3][:CASES], axis=1),
        ]
    )
    sums = everywhere(everywhere(sums, SLAB), DOM)
    second_image = image_of(second, made)
    rz, curv, cross, last = sums[0], sums[1], sums[2], sums[3]
    step = rz / curv
    ratio = (step * step * cross - rz) / rz
    grown = 1.0 + ratio
    curv_next = grown * grown * curv - 2.0 * grown * step * cross + step * step * last
    step_next = ratio * rz / curv_next
    on_first = (step + step_next * grown)[:, None]
    on_second = (step_next * step)[:, None]
    solution = on_first * direction[:CASES] - on_second * second[:CASES]
    residual = residual[:CASES] - on_first * image[:CASES] + on_second * second_image[:CASES]
    return (solution[:, None, :], residual[:, None, :])


def solution(mesh):
    finer = Mesh(
        mesh.devices.reshape(4, 2, 2, 8, 2), ("slab_0", "slab_1", "slab_2", "dom_0", "dom_1")
    )
    placed = (
        P(None, SLAB, DOM),
        P(SLAB, DOM),
        P(SLAB, DOM, None),
        P(SLAB, None, DOM, None),
        P(SLAB, DOM),
        P(SLAB, DOM),
        P(SLAB, None),
    )
    return jax.shard_map(
        body,
        mesh=finer,
        in_specs=placed,
        out_specs=(P(None, SLAB, DOM), P(None, SLAB, DOM)),
        check_vma=False,
    )
```

time: 270 us -> 180 us (0.67); the launches traced: 265 us -> 179 us
  matrix products: 42.1 us -> 0 us
  blocking collectives: 75.5 us -> 37.9 us
  Pallas kernels: 0 us -> 31 us
  local copies, waits for them, and re-layouts: 32.5 us -> 15.6 us
  waiting for transfers between devices: 58.2 us -> 43 us
  other arithmetic: 6.88 us -> 1.28 us
    psum x10 -> x0, blocking collectives: 75.5 us -> none  [by_axis(): value = lax.psum(value, axis)]
    dot_general x17 -> x0, matrix products: 42.1 us -> none  [the longest x2 23.7 us: apply_operator(): terms = jnp.einsum('eab,ceb->cea', matrices, picked, precision=highest)]
    all_to_all x0 -> x2, blocking collectives: none -> 37.9 us  [everywhere(): return lax.all_to_all(sent, axis, 0, 0, tiled=True).sum(axis=0)]
    pallas_call x0 -> x10, Pallas kernels: none -> 31 us  [the longest x2 12 us: all_rows(): per_step(2, [whole_block(8, span), BLOCKS], whole_block(OWN * CHUNK, LANE...]
    all_to_all x4, waiting for transfers between devices: 53.9 us -> 27.4 us  [the longest x2 16.4 us: all_rows(): full = lax.all_to_all(copies, 'dom_0', 0, 0, tiled=True)]
    ppermute x10 -> x12, waiting for transfers between devices: 4.29 us -> 15.6 us  [the longest x5 8.75 us: to_below(): return lax.ppermute(value, SLAB, down)]
    ppermute x10 -> x12, starting transfers between devices: 20.8 us -> 30.6 us  [the longest x5 22.9 us: to_above(): return lax.ppermute(value, SLAB, up)]
    all_to_all x4, starting transfers between devices: 27.8 us -> 18.9 us  [the longest x2 11.6 us: all_rows(): arrived = lax.all_to_all(parts, 'dom_0', 0, 0, tiled=True)]
  transfers between devices with their start and end apart: 14 -> 16, of which waited for: 7 -> 13; matrix products, arithmetic and copies ran while one was open for 22% -> 1% of each run, Pallas kernels for 0% -> 3%
where the time goes in v1:
time: 180 us; the launch traced here: 179 us
  starting transfers between devices  49.5 us (28%)
  waiting for transfers between devices  43 us (24%)
  blocking collectives  37.9 us (21%)
  Pallas kernels  31 us (17%)
  local copies, waits for them, and re-layouts  15.6 us (9%)
    all_to_all x2, blocking collectives, everywhere(): return lax.all_to_all(sent, axis, 0, 0, tiled=True).sum(axis=0)  37.9 us
    ppermute x5, starting transfers between devices, to_above(): return lax.ppermute(value, SLAB, up)  22.9 us
    all_to_all x2, waiting for transfers between devices, all_rows(): full = lax.all_to_all(copies, 'dom_0', 0, 0, tiled=True)  16.4 us
    unnamed x27, local copies, waits for them, and re-layouts  14.7 us
    pallas_call x2, Pallas kernels, all_rows(): per_step(2, [whole_block(8, span), BLOCKS], whole_block(OWN * CHUNK, LANE...  12 us
    all_to_all x2, starting transfers between devices, all_rows(): arrived = lax.all_to_all(parts, 'dom_0', 0, 0, tiled=True)  11.6 us
    all_to_all x2, waiting for transfers between devices, all_rows(): arrived = lax.all_to_all(parts, 'dom_0', 0, 0, tiled=True)  11 us
    ppermute x5, waiting for transfers between devices, to_below(): return lax.ppermute(value, SLAB, down)  8.75 us
  transfers between devices with their start and end apart: 16, of which 13 were waited for; matrix products, arithmetic and copies ran while one was open for 1% of the time, Pallas kernels for 3%

profile of v1, /device:TPU:1, one launch (start us, length us, event | category | flops | bytes accessed | tf_op | source)
XLA Modules:
  0.0 179.1 jit_solution(10851156530147014114)
XLA Ops:
  0.6 0.9 reshape.140.x_ref
  1.6 0.6 copy-done.9
  2.2 0.8 shard_map.87
  3.0 2.8 %collective-permute-start = (f32[1,384]{1,0:T(1,128)S(1)}, f32[1,384]{1,0:T(1,128)S(1)}, u32[]{:S(2)}, u32[]{:S(2)}) collective-permute-start(f32[1,384]{1,0:T(1,128)S(1)} %get-tuple-element.49), channel_id=1, source_target_pairs={{0,16},{16,32},{32,48},{48,64},{64,80},{80,96},{96,112},{112,128},... | collective-permute-start | bytes 4616 | tf_op jit(solution)/shard_map/ppermute | solution.py:283
  5.8 0.6 collective-permute-start.1
  6.4 2.3 %copy-done.3 = bf16[1,256,9216]{2,1,0:T(8,128)(2,1)S(1)} copy-done((bf16[1,256,9216]{2,1,0:T(8,128)(2,1)S(1)}, bf16[1,256,9216]{2,1,0:T(8,128)(2,1)}, u32[]{:S(2)}) %copy-start.3) | copy-done | bytes 4718616
  8.8 0.7 copy-done.5
  9.5 6.1 %shard_map.86 = (bf16[256,96,128]{2,1,0:T(8,128)(2,1)S(1)}, f32[8,1536]{1,0:T(8,128)S(1)}) custom-call(s32[256]{0:T(256)S(1)} %bitcast.72, bf16[256,9216]{1,0:T(8,128)(2,1)S(1)} %bitcast.69), custom_call_target="tpu_custom_call" | custom-call | tf_op jit(solution)/shard_map/pallas_call | solution.py:308
  15.6 0.8 fusion.11
  16.3 0.8 copy.43
  17.2 0.7 copy-done.7
  17.9 6.0 %shard_map.88 = f32[1152,128]{1,0:T(8,128)} custom-call(s32[256]{0:T(256)S(1)} %bitcast.73, s32[256]{0:T(256)S(1)} %bitcast.77, f32[8,1536]{1,0:T(8,128)S(1)} %pad_multiply_fusion.v_ref, bf16[256,96,128]{2,1,0:T(8,128)(2,1)S(1)} %get-tuple-element.13.k_ref), custom_call_target="tpu_custom_call" | custom-call | tf_op jit(solution)/shard_map/pallas_call | solution.py:332
  23.9 2.6 %copy-done = bf16[256,96,128]{2,1,0:T(8,128)(2,1)} copy-done((bf16[256,96,128]{2,1,0:T(8,128)(2,1)}, bf16[256,96,128]{2,1,0:T(8,128)(2,1)S(1)}, u32[]{:S(2)}) %copy-start) | copy-done | bytes 6291480
  26.5 7.5 %all-to-all-start = ((f32[8,144,128]{2,1,0:T(8,128)}), f32[8,144,128]{2,1,0:T(8,128)S(1)}, u32[]{:S(2)}, u32[]{:S(2)}) async-start(f32[8,144,128]{2,1,0:T(8,128)} %bitcast.8), calls=%async_computation | async-start | bytes 1179648 | tf_op jit(solution)/shard_map/all_to_all | solution.py:341
  34.0 2.1 %collective-permute-start.2 = (f32[8,384]{1,0:T(8,128)S(1)}, f32[8,384]{1,0:T(8,128)S(1)}, u32[]{:S(2)}, u32[]{:S(2)}) collective-permute-start(f32[8,384]{1,0:T(8,128)S(1)} %get-tuple-element.43), channel_id=1, source_target_pairs={{0,16},{16,32},{32,48},{48,64},{64,80},{80,96},{96,112},{112,128},... | collective-permute-start | bytes 36872 | tf_op jit(solution)/shard_map/ppermute | solution.py:283
  36.1 1.0 collective-permute-start.3
  37.7 1.5 collective-permute-done.3.up_ref
  39.3 11.0 %all-to-all-done.y_ref = f32[8,144,128]{2,1,0:T(8,128)S(1)} async-done(((f32[8,144,128]{2,1,0:T(8,128)}), f32[8,144,128]{2,1,0:T(8,128)S(1)}, u32[]{:S(2)}, u32[]{:S(2)}) %all-to-all-start) | async-done | bytes 589856 | tf_op jit(solution)/shard_map/all_to_all | solution.py:341
  50.3 0.9 shard_map.89.a_ref
  51.1 2.6 %collective-permute-start.4 = (f32[144,128]{1,0:T(8,128)S(1)}, f32[144,128]{1,0:T(8,128)S(1)}, u32[]{:S(2)}, u32[]{:S(2)}) collective-permute-start(f32[144,128]{1,0:T(8,128)S(1)} %shard_map.89.a_ref), channel_id=1, source_target_pairs={{0,1},{1,0},{2,3},{3,2},{4,5},{5,4},{6,7},{7,6},{8,9},{9,8},{10,11... | collective-permute-start | bytes 221192 | tf_op jit(solution)/shard_map/ppermute | solution.py:349
  53.7 2.2 %collective-permute-done.4.b_ref = f32[144,128]{1,0:T(8,128)S(1)} collective-permute-done((f32[144,128]{1,0:T(8,128)S(1)}, f32[144,128]{1,0:T(8,128)S(1)}, u32[]{:S(2)}, u32[]{:S(2)}) %collective-permute-start.4) | collective-permute-done | bytes 73760 | tf_op jit(solution)/shard_map/ppermute | solution.py:349
  55.9 1.5 shard_map.90
  57.4 3.5 %all-to-all-start.1 = ((f32[8,144,128]{2,1,0:T(8,128)}), f32[8,144,128]{2,1,0:T(8,128)S(1)}, u32[]{:S(2)}, u32[]{:S(2)}) async-start(f32[8,144,128]{2,1,0:T(8,128)} %get-tuple-element.15), calls=%async_computation.1 | async-start | bytes 1179648 | tf_op jit(solution)/shard_map/all_to_all | solution.py:362
  60.9 5.8 %collective-permute-start.5 = (f32[8,384]{1,0:T(8,128)S(1)}, f32[8,384]{1,0:T(8,128)S(1)}, u32[]{:S(2)}, u32[]{:S(2)}) collective-permute-start(f32[8,384]{1,0:T(8,128)S(1)} %get-tuple-element.47), channel_id=1, source_target_pairs={{0,16},{16,32},{32,48},{48,64},{64,80},{80,96},{96,112},{112,128},... | collective-permute-start | bytes 36872 | tf_op jit(solution)/shard_map/ppermute | solution.py:283
  66.8 0.8 collective-permute-done.5.low_ref
  67.6 2.6 %collective-permute-done.6.up_ref = f32[8,384]{1,0:T(8,128)S(1)} collective-permute-done((f32[8,384]{1,0:T(8,128)S(1)}, f32[8,384]{1,0:T(8,128)S(1)}, u32[]{:S(2)}, u32[]{:S(2)}) %collective-permute-start.6) | collective-permute-done | bytes 12320 | tf_op jit(solution)/shard_map/ppermute | solution.py:286
  70.2 3.3 %all-to-all-done.1 = f32[8,144,128]{2,1,0:T(8,128)S(1)} async-done(((f32[8,144,128]{2,1,0:T(8,128)}), f32[8,144,128]{2,1,0:T(8,128)S(1)}, u32[]{:S(2)}, u32[]{:S(2)}) %all-to-all-start.1) | async-done | bytes 589856 | tf_op jit(solution)/shard_map/all_to_all | solution.py:362
  73.5 2.8 %copy-done.1 = bf16[256,96,128]{2,1,0:T(8,128)(2,1)S(1)} copy-done((bf16[256,96,128]{2,1,0:T(8,128)(2,1)S(1)}, bf16[256,96,128]{2,1,0:T(8,128)(2,1)}, u32[]{:S(2)}) %copy-start.1) | copy-done | bytes 6291480
  76.3 3.7 %shard_map.91 = f32[8,1536]{1,0:T(8,128)S(1)} custom-call(s32[256]{0:T(256)S(1)} %bitcast.74, s32[256]{0:T(256)S(1)} %bitcast.78, f32[1152,128]{1,0:T(8,128)S(1)} %bitcast.71, bf16[256,96,128]{2,1,0:T(8,128)(2,1)S(1)} %copy-done.1, f32[8,1536]{1,0:T(8,128)S(1)} %pad_multiply_fusion.v_ref, f32[1,1536]{1,0:T(1,128)S(1)} %copy-done.4, ...), custom_call_target="tpu_custom_call" | custom-call | tf_op jit(solution)/shard_map/pallas_call | solution.py:369
  80.0 6.0 %shard_map.92 = f32[1152,128]{1,0:T(8,128)} custom-call(s32[256]{0:T(256)S(1)} %bitcast.75, s32[256]{0:T(256)S(1)} %bitcast.79, f32[8,1536]{1,0:T(8,128)S(1)} %broadcast_multiply_fusion.v_ref, bf16[256,96,128]{2,1,0:T(8,128)(2,1)S(1)} %copy-done.1), custom_call_target="tpu_custom_call" | custom-call | tf_op jit(solution)/shard_map/pallas_call | solution.py:332
  86.0 4.1 %all-to-all-start.2 = ((f32[8,144,128]{2,1,0:T(8,128)}), f32[8,144,128]{2,1,0:T(8,128)S(1)}, u32[]{:S(2)}, u32[]{:S(2)}) async-start(f32[8,144,128]{2,1,0:T(8,128)} %bitcast.14), calls=%async_computation.2 | async-start | bytes 1179648 | tf_op jit(solution)/shard_map/all_to_all | solution.py:341
  90.1 10.8 %collective-permute-start.7 = (f32[8,384]{1,0:T(8,128)S(1)}, f32[8,384]{1,0:T(8,128)S(1)}, u32[]{:S(2)}, u32[]{:S(2)}) collective-permute-start(f32[8,384]{1,0:T(8,128)S(1)} %get-tuple-element.41), channel_id=1, source_target_pairs={{0,16},{16,32},{32,48},{48,64},{64,80},{80,96},{96,112},{112,128},... | collective-permute-start | bytes 36872 | tf_op jit(solution)/shard_map/ppermute | solution.py:283
  101.0 0.8 collective-permute-done.7.low_ref
  101.8 2.6 %collective-permute-done.8.up_ref = f32[8,384]{1,0:T(8,128)S(1)} collective-permute-done((f32[8,384]{1,0:T(8,128)S(1)}, f32[8,384]{1,0:T(8,128)S(1)}, u32[]{:S(2)}, u32[]{:S(2)}) %collective-permute-start.8) | collective-permute-done | bytes 12320 | tf_op jit(solution)/shard_map/ppermute | solution.py:286
  104.4 0.9 shard_map.93.a_ref
  105.3 3.0 %collective-permute-start.9 = (f32[144,128]{1,0:T(8,128)S(1)}, f32[144,128]{1,0:T(8,128)S(1)}, u32[]{:S(2)}, u32[]{:S(2)}) collective-permute-start(f32[144,128]{1,0:T(8,128)S(1)} %shard_map.93.a_ref), channel_id=1, source_target_pairs={{0,1},{1,0},{2,3},{3,2},{4,5},{5,4},{6,7},{7,6},{8,9},{9,8},{10,11... | collective-permute-start | bytes 221192 | tf_op jit(solution)/shard_map/ppermute | solution.py:349
  108.4 1.9 %collective-permute-done.9.b_ref = f32[144,128]{1,0:T(8,128)S(1)} collective-permute-done((f32[144,128]{1,0:T(8,128)S(1)}, f32[144,128]{1,0:T(8,128)S(1)}, u32[]{:S(2)}, u32[]{:S(2)}) %collective-permute-start.9) | collective-permute-done | bytes 73760 | tf_op jit(solution)/shard_map/ppermute | solution.py:349
  110.3 1.5 shard_map.94
  111.9 24.3 %all_to_all.30 = f32[16,4,6]{2,1,0:T(4,128)S(1)} all-to-all(f32[16,4,6]{2,1,0:T(4,128)S(1)} %broadcast_in_dim.8), channel_id=1, replica_groups=mesh['slab_0'=4,'slab_1'=2,'slab_2'=2,'dom_0'=8,'dom_1'=2] {'slab_0','sl..., dimensions={0} | all-to-all | bytes 3072 | tf_op jit(solution)/shard_map/all_to_all | solution.py:391
  136.3 13.5 %all_to_all.31 = f32[16,4,6]{2,1,0:T(4,128)S(1)} all-to-all(f32[16,4,6]{2,1,0:T(4,128)S(1)} %broadcast_in_dim.9), channel_id=1, replica_groups=mesh['slab_0'=4,'slab_1'=2,'slab_2'=2,'dom_0'=8,'dom_1'=2] {'dom_0','dom..., dimensions={0} | all-to-all | bytes 3072 | tf_op jit(solution)/shard_map/all_to_all | solution.py:391
  149.8 3.7 %all-to-all-start.5 = ((f32[8,144,128]{2,1,0:T(8,128)}), f32[8,144,128]{2,1,0:T(8,128)S(1)}, u32[]{:S(2)}, u32[]{:S(2)}) async-start(f32[8,144,128]{2,1,0:T(8,128)} %get-tuple-element.18), calls=%async_computation.5 | async-start | bytes 1179648 | tf_op jit(solution)/shard_map/all_to_all | solution.py:362
  153.6 1.4 collective-permute-start.10
  156.0 2.1 %collective-permute-done.11.up_ref = f32[8,384]{1,0:T(8,128)S(1)} collective-permute-done((f32[8,384]{1,0:T(8,128)S(1)}, f32[8,384]{1,0:T(8,128)S(1)}, u32[]{:S(2)}, u32[]{:S(2)}) %collective-permute-start.11) | collective-permute-done | bytes 12320 | tf_op jit(solution)/shard_map/ppermute | solution.py:286
  158.1 13.1 %all-to-all-done.5 = f32[8,144,128]{2,1,0:T(8,128)S(1)} async-done(((f32[8,144,128]{2,1,0:T(8,128)}), f32[8,144,128]{2,1,0:T(8,128)S(1)}, u32[]{:S(2)}, u32[]{:S(2)}) %all-to-all-start.5) | async-done | bytes 589856 | tf_op jit(solution)/shard_map/all_to_all | solution.py:362
  171.2 2.8 %copy-done.2 = bf16[256,96,128]{2,1,0:T(8,128)(2,1)S(1)} copy-done((bf16[256,96,128]{2,1,0:T(8,128)(2,1)S(1)}, bf16[256,96,128]{2,1,0:T(8,128)(2,1)}, u32[]{:S(2)}) %copy-start.2) | copy-done | bytes 6291480
  174.0 3.7 %shard_map.95 = f32[8,1536]{1,0:T(8,128)S(1)} custom-call(s32[256]{0:T(256)S(1)} %bitcast.76, s32[256]{0:T(256)S(1)} %bitcast.80, f32[1152,128]{1,0:T(8,128)S(1)} %bitcast.70, bf16[256,96,128]{2,1,0:T(8,128)(2,1)S(1)} %copy-done.2, f32[8,1536]{1,0:T(8,128)S(1)} %broadcast_multiply_fusion.v_ref, f32[1,1536]{1,0:T(1,128)S(1)} %copy-done.4, ...), custom_call_target="tpu_custom_call" | custom-call | tf_op jit(solution)/shard_map/pallas_call | solution.py:369
  177.8 0.7 copy.25
  178.4 0.7 copy.26
  (47 shorter events, 2.2 us)
Async XLA Ops:
  1.6 0.7 copy-start.9
  3.0 14.1 %collective-permute-start = (f32[1,384]{1,0:T(1,128)S(1)}, f32[1,384]{1,0:T(1,128)S(1)}, u32[]{:S(2)}, u32[]{:S(2)}) collective-permute-start(f32[1,384]{1,0:T(1,128)S(1)} %get-tuple-element.49), channel_id=1, source_target_pairs={{0,16},{16,32},{32,48},{48,64},{64,80},{80,96},{96,112},{112,128},... | collective-permute-start | bytes 4616 | tf_op jit(solution)/shard_map/ppermute | solution.py:283
  5.8 11.3 %collective-permute-start.1 = (f32[1,384]{1,0:T(1,128)S(1)}, f32[1,384]{1,0:T(1,128)S(1)}, u32[]{:S(2)}, u32[]{:S(2)}) collective-permute-start(f32[1,384]{1,0:T(1,128)S(1)} %get-tuple-element.48), channel_id=1, source_target_pairs={{16,0},{32,16},{48,32},{64,48},{80,64},{96,80},{112,96},{128,112},... | collective-permute-start | bytes 4616 | tf_op jit(solution)/shard_map/ppermute | solution.py:286
  6.4 2.3 %copy-start.3 = (bf16[1,256,9216]{2,1,0:T(8,128)(2,1)S(1)}, bf16[1,256,9216]{2,1,0:T(8,128)(2,1)}, u32[]{:S(2)}) copy-start(bf16[1,256,9216]{2,1,0:T(8,128)(2,1)} %param.9) | copy-start | bytes 14155780
  8.8 0.7 copy-start.5
  9.5 40.8 %copy-start.10 = (s32[1,2]{1,0:T(1,128)S(1)}, s32[1,2]{1,0:T(1,128)}, u32[]{:S(2)}) copy-start(s32[1,2]{1,0:T(1,128)} %param.13) | copy-start | bytes 28
  15.5 58.0 %copy-start.4 = (f32[1,1536]{1,0:T(1,128)S(1)}, f32[1,1536]{1,0:T(1,128)}, u32[]{:S(2)}) copy-start(f32[1,1536]{1,0:T(1,128)} %shift_ref.3) | copy-start | bytes 18436
  15.5 58.0 %copy-start.6 = (s32[1,256]{1,0:T(1,128)S(1)}, s32[1,256]{1,0:T(1,128)}, u32[]{:S(2)}) copy-start(s32[1,256]{1,0:T(1,128)} %param.11) | copy-start | bytes 3076
  15.5 57.9 %copy-start.8 = (s32[1,256]{1,0:T(1,128)S(1)}, s32[1,256]{1,0:T(1,128)}, u32[]{:S(2)}) copy-start(s32[1,256]{1,0:T(1,128)} %param.12) | copy-start | bytes 3076
  17.2 0.7 copy-start.7
  23.9 2.6 %copy-start = (bf16[256,96,128]{2,1,0:T(8,128)(2,1)}, bf16[256,96,128]{2,1,0:T(8,128)(2,1)S(1)}, u32[]{:S(2)}) copy-start(bf16[256,96,128]{2,1,0:T(8,128)(2,1)S(1)} %get-tuple-element.13.k_ref) | copy-start | bytes 18874372
  26.5 23.8 %all-to-all-start = ((f32[8,144,128]{2,1,0:T(8,128)}), f32[8,144,128]{2,1,0:T(8,128)S(1)}, u32[]{:S(2)}, u32[]{:S(2)}) async-start(f32[8,144,128]{2,1,0:T(8,128)} %bitcast.8), calls=%async_computation | async-start | bytes 1179648 | tf_op jit(solution)/shard_map/all_to_all | solution.py:341
  34.0 3.7 %collective-permute-start.2 = (f32[8,384]{1,0:T(8,128)S(1)}, f32[8,384]{1,0:T(8,128)S(1)}, u32[]{:S(2)}, u32[]{:S(2)}) collective-permute-start(f32[8,384]{1,0:T(8,128)S(1)} %get-tuple-element.43), channel_id=1, source_target_pairs={{0,16},{16,32},{32,48},{48,64},{64,80},{80,96},{96,112},{112,128},... | collective-permute-start | bytes 36872 | tf_op jit(solution)/shard_map/ppermute | solution.py:283
  36.1 3.1 %collective-permute-start.3 = (f32[8,384]{1,0:T(8,128)S(1)}, f32[8,384]{1,0:T(8,128)S(1)}, u32[]{:S(2)}, u32[]{:S(2)}) collective-permute-start(f32[8,384]{1,0:T(8,128)S(1)} %get-tuple-element.42), channel_id=1, source_target_pairs={{16,0},{32,16},{48,32},{64,48},{80,64},{96,80},{112,96},{128,112},... | collective-permute-start | bytes 36872 | tf_op jit(solution)/shard_map/ppermute | solution.py:286
  51.1 4.8 %collective-permute-start.4 = (f32[144,128]{1,0:T(8,128)S(1)}, f32[144,128]{1,0:T(8,128)S(1)}, u32[]{:S(2)}, u32[]{:S(2)}) collective-permute-start(f32[144,128]{1,0:T(8,128)S(1)} %shard_map.89.a_ref), channel_id=1, source_target_pairs={{0,1},{1,0},{2,3},{3,2},{4,5},{5,4},{6,7},{7,6},{8,9},{9,8},{10,11... | collective-permute-start | bytes 221192 | tf_op jit(solution)/shard_map/ppermute | solution.py:349
  57.4 16.1 %all-to-all-start.1 = ((f32[8,144,128]{2,1,0:T(8,128)}), f32[8,144,128]{2,1,0:T(8,128)S(1)}, u32[]{:S(2)}, u32[]{:S(2)}) async-start(f32[8,144,128]{2,1,0:T(8,128)} %get-tuple-element.15), calls=%async_computation.1 | async-start | bytes 1179648 | tf_op jit(solution)/shard_map/all_to_all | solution.py:362
  60.9 6.7 %collective-permute-start.5 = (f32[8,384]{1,0:T(8,128)S(1)}, f32[8,384]{1,0:T(8,128)S(1)}, u32[]{:S(2)}, u32[]{:S(2)}) collective-permute-start(f32[8,384]{1,0:T(8,128)S(1)} %get-tuple-element.47), channel_id=1, source_target_pairs={{0,16},{16,32},{32,48},{48,64},{64,80},{80,96},{96,112},{112,128},... | collective-permute-start | bytes 36872 | tf_op jit(solution)/shard_map/ppermute | solution.py:283
  66.8 3.4 %collective-permute-start.6 = (f32[8,384]{1,0:T(8,128)S(1)}, f32[8,384]{1,0:T(8,128)S(1)}, u32[]{:S(2)}, u32[]{:S(2)}) collective-permute-start(f32[8,384]{1,0:T(8,128)S(1)} %get-tuple-element.46), channel_id=1, source_target_pairs={{16,0},{32,16},{48,32},{64,48},{80,64},{96,80},{112,96},{128,112},... | collective-permute-start | bytes 36872 | tf_op jit(solution)/shard_map/ppermute | solution.py:286
  73.5 2.8 %copy-start.1 = (bf16[256,96,128]{2,1,0:T(8,128)(2,1)S(1)}, bf16[256,96,128]{2,1,0:T(8,128)(2,1)}, u32[]{:S(2)}) copy-start(bf16[256,96,128]{2,1,0:T(8,128)(2,1)} %copy-done) | copy-start | bytes 18874372
  80.0 28.2 %copy-start.11 = (f32[6,1,1536]{2,1,0:T(1,128)S(1)}, f32[6,1,1536]{2,1,0:T(1,128)}, u32[]{:S(2)}) copy-start(f32[6,1,1536]{2,1,0:T(1,128)} %param.7) | copy-start | bytes 110596
  86.0 18.4 %all-to-all-start.2 = ((f32[8,144,128]{2,1,0:T(8,128)}), f32[8,144,128]{2,1,0:T(8,128)S(1)}, u32[]{:S(2)}, u32[]{:S(2)}) async-start(f32[8,144,128]{2,1,0:T(8,128)} %bitcast.14), calls=%async_computation.2 | async-start | bytes 1179648 | tf_op jit(solution)/shard_map/all_to_all | solution.py:341
  90.1 11.7 %collective-permute-start.7 = (f32[8,384]{1,0:T(8,128)S(1)}, f32[8,384]{1,0:T(8,128)S(1)}, u32[]{:S(2)}, u32[]{:S(2)}) collective-permute-start(f32[8,384]{1,0:T(8,128)S(1)} %get-tuple-element.41), channel_id=1, source_target_pairs={{0,16},{16,32},{32,48},{48,64},{64,80},{80,96},{96,112},{112,128},... | collective-permute-start | bytes 36872 | tf_op jit(solution)/shard_map/ppermute | solution.py:283
  101.0 3.4 %collective-permute-start.8 = (f32[8,384]{1,0:T(8,128)S(1)}, f32[8,384]{1,0:T(8,128)S(1)}, u32[]{:S(2)}, u32[]{:S(2)}) collective-permute-start(f32[8,384]{1,0:T(8,128)S(1)} %get-tuple-element.40), channel_id=1, source_target_pairs={{16,0},{32,16},{48,32},{64,48},{80,64},{96,80},{112,96},{128,112},... | collective-permute-start | bytes 36872 | tf_op jit(solution)/shard_map/ppermute | solution.py:286
  105.3 5.0 %collective-permute-start.9 = (f32[144,128]{1,0:T(8,128)S(1)}, f32[144,128]{1,0:T(8,128)S(1)}, u32[]{:S(2)}, u32[]{:S(2)}) collective-permute-start(f32[144,128]{1,0:T(8,128)S(1)} %shard_map.93.a_ref), channel_id=1, source_target_pairs={{0,1},{1,0},{2,3},{3,2},{4,5},{5,4},{6,7},{7,6},{8,9},{9,8},{10,11... | collective-permute-start | bytes 221192 | tf_op jit(solution)/shard_map/ppermute | solution.py:349
  149.8 21.4 %all-to-all-start.5 = ((f32[8,144,128]{2,1,0:T(8,128)}), f32[8,144,128]{2,1,0:T(8,128)S(1)}, u32[]{:S(2)}, u32[]{:S(2)}) async-start(f32[8,144,128]{2,1,0:T(8,128)} %get-tuple-element.18), calls=%async_computation.5 | async-start | bytes 1179648 | tf_op jit(solution)/shard_map/all_to_all | solution.py:362
  153.6 2.5 %collective-permute-start.10 = (f32[8,384]{1,0:T(8,128)S(1)}, f32[8,384]{1,0:T(8,128)S(1)}, u32[]{:S(2)}, u32[]{:S(2)}) collective-permute-start(f32[8,384]{1,0:T(8,128)S(1)} %get-tuple-element.45), channel_id=1, source_target_pairs={{0,16},{16,32},{32,48},{48,64},{64,80},{80,96},{96,112},{112,128},... | collective-permute-start | bytes 36872 | tf_op jit(solution)/shard_map/ppermute | solution.py:283
  155.0 3.1 %collective-permute-start.11 = (f32[8,384]{1,0:T(8,128)S(1)}, f32[8,384]{1,0:T(8,128)S(1)}, u32[]{:S(2)}, u32[]{:S(2)}) collective-permute-start(f32[8,384]{1,0:T(8,128)S(1)} %get-tuple-element.44), channel_id=1, source_target_pairs={{16,0},{32,16},{48,32},{64,48},{80,64},{96,80},{112,96},{128,112},... | collective-permute-start | bytes 36872 | tf_op jit(solution)/shard_map/ppermute | solution.py:286
  171.2 2.8 %copy-start.2 = (bf16[256,96,128]{2,1,0:T(8,128)(2,1)S(1)}, bf16[256,96,128]{2,1,0:T(8,128)(2,1)}, u32[]{:S(2)}) copy-start(bf16[256,96,128]{2,1,0:T(8,128)(2,1)} %copy-done) | copy-start | bytes 18874372

commit v2 on v1

v2 whole, which is shorter than its diff:
```python
import functools

import jax
import jax.numpy as jnp
from jax import lax
from jax.experimental import pallas as pl
from jax.experimental.pallas import tpu as pltpu
from jax.sharding import Mesh
from jax.sharding import PartitionSpec as P

BLOCK = 96
CASES = 6
DOM = ("dom_0", "dom_1")
SLAB = ("slab_0", "slab_1", "slab_2")
F32 = jnp.float32
BF16 = jnp.bfloat16
LANES = 128
OWN = 16
STORED = 256
SLAB_ROWS = 256
GROUP = 32
STEPS = STORED // GROUP
CHUNK = 72
TILES = 12
FACE = 4
MIB = 1024 * 1024


def lane(rows):
    return lax.broadcasted_iota(jnp.int32, (rows, LANES), 1)


def spread(t0, t1, t2):
    at = lane(t0.shape[0])
    v0 = t0
    v1 = jnp.where(at < 32, pltpu.roll(t0, 32, 1), pltpu.roll(t1, 32, 1))
    v2 = jnp.where(at < 64, pltpu.roll(t1, 64, 1), pltpu.roll(t2, 64, 1))
    v3 = pltpu.roll(t2, 96, 1)
    return [jnp.where(at < BLOCK, v, 0.0) for v in (v0, v1, v2, v3)]


def packed(v0, v1, v2, v3):
    at = lane(v0.shape[0])
    r1 = pltpu.roll(v1, 96, 1)
    r2 = pltpu.roll(v2, 64, 1)
    r3 = pltpu.roll(v3, 32, 1)
    return (
        jnp.where(at < 96, v0, r1),
        jnp.where(at < 64, r1, r2),
        jnp.where(at < 32, r2, r3),
    )


def halves(v):
    high = v.astype(BF16).astype(F32)
    return jnp.concatenate([high, v - high], axis=0).astype(BF16)


def rows_live(shape, dim, live, block):
    at = lax.broadcasted_iota(jnp.int32, shape, dim)
    row = 4 * (at % 24) + at // 24
    return row + block * BLOCK < live


def eight(ref, start):
    if start + 8 <= ref.shape[0]:
        return ref[start : start + 8, :]
    return pltpu.roll(ref[start - 2 : start + 6, :], 6, 0)


def block_of(held, first, stride):
    parts = [held[pl.ds(first + k * (stride // 3), 24, stride=stride), :] for k in range(3)]
    return jnp.concatenate(spread(*parts), axis=0)


def face_prep(live_ref, x_ref, k_ref, sq_ref, held):
    for k in range(2):
        for t in range(CHUNK):
            held[t * 8 + k * FACE : t * 8 + (k + 1) * FACE, :] = x_ref[
                k, :, t * LANES : (t + 1) * LANES
            ].astype(F32)
    for k in range(2):
        sums = []
        for i in range(FACE):
            whole = block_of(held, k * FACE + i, 24)
            k_ref[k * FACE + i] = whole.astype(BF16)
            masked = jnp.where(rows_live((BLOCK, LANES), 0, live_ref[k], i), whole, 0.0)
            total = jnp.sum(masked * masked, axis=0, keepdims=True)
            sums.append(jnp.broadcast_to(total, (8, LANES)))
        for t, tile in enumerate(packed(*sums)):
            sq_ref[k, :, t * LANES : (t + 1) * LANES] = tile


def stiff_prep(col_ref, x_ref, k_ref, diag_ref, held, acc):
    step = pl.program_id(0)

    @pl.when(step == 0)
    def _():
        acc[...] = jnp.zeros_like(acc)

    for half in range(GROUP // 16):
        for t in range(CHUNK):
            held[t * 16 : (t + 1) * 16, :] = x_ref[
                half * 16 : (half + 1) * 16, t * LANES : (t + 1) * LANES
            ].astype(F32)
        for e in range(16):
            whole = block_of(held, e, 48)
            k_ref[half * 16 + e] = whole.astype(BF16)
            total = jnp.sum((whole * whole).reshape(12, 8, LANES), axis=0)
            j = col_ref[step * GROUP + half * 16 + e]
            acc[j] = acc[j] + total

    @pl.when(step == STEPS - 1)
    def _():
        for q in range(OWN // 4):
            sums = [
                jnp.broadcast_to(jnp.sum(acc[q * 4 + i], axis=0, keepdims=True), (8, LANES))
                for i in range(4)
            ]
            for t, tile in enumerate(packed(*sums)):
                diag_ref[:, tile_at(q * 3 + t)] = tile


def tile_at(t):
    return slice(t * LANES, (t + 1) * LANES)


def part(g):
    return pl.ds(g * GROUP, GROUP)


def fetch(k_any, k_ref, sems):
    for g in range(STEPS):
        pltpu.make_async_copy(k_any.at[part(g)], k_ref.at[part(g)], sems.at[g]).start()


def fetched(k_any, k_ref, sems, g):
    pltpu.make_async_copy(k_any.at[part(g)], k_ref.at[part(g)], sems.at[g]).wait()


def forward(col_ref, row_ref, tiles, k_ref, out_ref, cols, acc, wait=None):
    for q in range(OWN // 4):
        for i, v in enumerate(spread(*tiles[q * 3 : q * 3 + 3])):
            cols[q * 4 + i] = halves(v)
    acc[...] = jnp.zeros_like(acc)

    def group(g, carry):
        base = g * GROUP
        if wait is not None:
            wait(g)
        for first in range(0, GROUP, 8):
            terms = []
            for e in range(first, first + 8):
                x = cols[col_ref[base + e]]
                out = lax.dot_general(
                    x, k_ref[base + e], (((1,), (1,)), ((), ())), preferred_element_type=F32
                )
                terms.append(out[:8] + out[8:])
            for e in range(first, first + 8):
                r = row_ref[base + e]
                acc[r, :, :BLOCK] = acc[r, :, :BLOCK] + terms[e - first]
        return carry

    lax.fori_loop(0, STEPS, group, 0)
    for g in range(SLAB_ROWS // 4):
        for t, tile in enumerate(packed(*[acc[g * 4 + i] for i in range(4)])):
            at = (g // 4) * CHUNK + ((g % 4) * 3 + t) * CASES
            out_ref[at : at + CASES, :] = tile[:CASES]


def adjoint(col_ref, row_ref, y_ref, k_ref, rows, acc, wait):
    depth = y_ref.shape[0] // (OWN // 2)
    for g in range(SLAB_ROWS // 4):
        at = (g // 8) * depth + (g // 4 % 2) * CHUNK + (g % 4) * 3 * CASES
        tiles = [eight(y_ref, at + t * CASES) for t in range(3)]
        for i, v in enumerate(spread(*tiles)):
            rows[g * 4 + i] = halves(v)
    acc[...] = jnp.zeros_like(acc)

    def group(g, carry):
        base = g * GROUP
        wait(g)
        for first in range(0, GROUP, 8):
            terms = []
            for e in range(first, first + 8):
                y = rows[row_ref[base + e]]
                out = jnp.dot(y[:, :BLOCK], k_ref[base + e], preferred_element_type=F32)
                terms.append(out[:8] + out[8:])
            for e in range(first, first + 8):
                j = col_ref[base + e]
                acc[j] = acc[j] + terms[e - first]
        return carry

    lax.fori_loop(0, STEPS, group, 0)
    tiles = []
    for q in range(OWN // 4):
        tiles += packed(*[acc[q * 4 + i] for i in range(4)])
    return tiles


def both_sides(core, near_ref, far_ref):
    near = [near_ref[:, tile_at(t)] for t in range(3)]
    far = [far_ref[:, tile_at(t)] for t in range(3)]
    below = [jnp.where(core == 0, f, n) for n, f in zip(near, far)]
    above = [jnp.where(core == 0, n, f) for n, f in zip(near, far)]
    return below, above


def send_sides(core, lower, upper, near_ref, far_ref):
    for t in range(3):
        near_ref[:, tile_at(t)] = jnp.where(core == 0, upper[t], lower[t])
        far_ref[:, tile_at(t)] = jnp.where(core == 0, lower[t], upper[t])


def first_product(
    col_ref, row_ref, at_ref, rhs_ref, shift_ref, diag_ref, near_ref, far_ref, k_any,
    out_ref, inverse_ref, v_ref, near_out, far_out, held, cols, acc, k_ref, sems,
):
    fetch(k_any, k_ref, sems)
    core = at_ref[1]
    held[...] = jnp.zeros_like(held)
    for c in range(CASES):
        held[c : c + 1, :] = rhs_ref[c]
    below, above = both_sides(core, near_ref, far_ref)
    tiles = []
    for t in range(TILES):
        total = diag_ref[:, tile_at(t)] + shift_ref[:, tile_at(t)]
        if t < 3:
            total = total + below[t]
        if t >= 9:
            total = total + above[t - 9]
        inverse = 1.0 / total
        inverse_ref[:, tile_at(t)] = inverse
        tile = inverse * held[:, tile_at(t)]
        v_ref[:, tile_at(t)] = tile
        tiles.append(tile)
    send_sides(core, tiles[:3], tiles[9:], near_out, far_out)
    wait = functools.partial(fetched, k_any, k_ref, sems)
    forward(col_ref, row_ref, tiles, k_ref, out_ref, cols, acc, wait)


def image_tiles(core, tiles, v_ref, shift_ref, near_ref, far_ref):
    below, above = both_sides(core, near_ref, far_ref)
    whole = [
        tile + shift_ref[:, tile_at(t)] * v_ref[:, tile_at(t)] for t, tile in enumerate(tiles)
    ]
    return (
        [whole[t] + below[t] for t in range(3)]
        + whole[3:9]
        + [whole[t + 9] + above[t] for t in range(3)]
    )


def placed_sums(values):
    at = lane(8)
    out = jnp.zeros((8, LANES), F32)
    for n, value in values:
        out = jnp.where(at == n, jnp.sum(value, axis=1, keepdims=True), out)
    return out


def middle_product(
    col_ref, row_ref, at_ref, y_ref, rhs_ref, shift_ref, inverse_ref, v_ref, near_ref, far_ref,
    k_any, out_ref, image_ref, w_ref, sums_ref, near_out, far_out, held, rows, cols, acc,
    k_ref, sems,
):
    fetch(k_any, k_ref, sems)
    core = at_ref[1]
    wait = functools.partial(fetched, k_any, k_ref, sems)
    tiles = adjoint(col_ref, row_ref, y_ref, k_ref, rows, acc, wait)
    tiles = image_tiles(core, tiles, v_ref, shift_ref, near_ref, far_ref)
    held[...] = jnp.zeros_like(held)
    for c in range(CASES):
        held[c : c + 1, :] = rhs_ref[c]
    sums = [jnp.zeros((8, LANES), F32) for _ in range(4)]
    second = []
    for t, image in enumerate(tiles):
        image_ref[:, tile_at(t)] = image
        w = inverse_ref[:, tile_at(t)] * image
        w_ref[:, tile_at(t)] = w
        second.append(w)
        v = v_ref[:, tile_at(t)]
        sums[0] = sums[0] + held[:, tile_at(t)] * v
        sums[1] = sums[1] + v * image
        sums[2] = sums[2] + image * w
        sums[3] = sums[3] + shift_ref[:, tile_at(t)] * w * w
    sums_ref[...] = placed_sums(enumerate(sums))
    send_sides(core, second[:3], second[9:], near_out, far_out)
    forward(col_ref, row_ref, second, k_ref, out_ref, cols, acc)


def last_product(
    col_ref, row_ref, at_ref, y_ref, shift_ref, v_ref, near_ref, far_ref, k_any,
    image_ref, rows, acc, k_ref, sems,
):
    fetch(k_any, k_ref, sems)
    wait = functools.partial(fetched, k_any, k_ref, sems)
    tiles = adjoint(col_ref, row_ref, y_ref, k_ref, rows, acc, wait)
    for t, tile in enumerate(image_tiles(at_ref[1], tiles, v_ref, shift_ref, near_ref, far_ref)):
        image_ref[:, tile_at(t)] = tile


def summed(at_ref, live_ref, y_ref, near_ref, far_ref, k_ref, *rest):
    out_ref = rest[-1]
    half = at_ref[0]
    whole = y_ref[0]
    for z in range(1, y_ref.shape[0]):
        whole = whole + y_ref[z]
    out_ref[: 2 * CHUNK, :] = whole
    if len(rest) > 1:
        out_ref[2 * CHUNK :, :] = rest[0][...]
    for k, face in enumerate(both_sides(at_ref[1], near_ref, far_ref)):
        terms = []
        for i, v in enumerate(spread(*face)):
            out = lax.dot_general(
                halves(v), k_ref[k * FACE + i], (((1,), (1,)), ((), ())), preferred_element_type=F32
            )
            term = out[:8] + out[8:]
            term = jnp.where(rows_live((8, BLOCK), 1, live_ref[k], i), term, 0.0)
            terms.append(jnp.concatenate([term, jnp.zeros((8, LANES - BLOCK), F32)], axis=1))
        for t, tile in enumerate(packed(*terms)):
            for h in range(2):
                at = h * CHUNK + (k * 9 + t) * CASES
                added = jnp.where(half == h, tile[:CASES], 0.0)
                out_ref[at : at + CASES, :] = out_ref[at : at + CASES, :] + added


def finished(at_ref, live_ref, a_ref, b_ref, k_ref, out_ref, near_out, far_out, held):
    half = at_ref[0]
    both = a_ref[...] + b_ref[...]
    if both.shape[0] > 2 * CHUNK:
        square = jnp.zeros((8, LANES), F32)
        for t in range(2 * TILES):
            tile = eight(a_ref, t * CASES) + eight(b_ref, t * CASES)
            square = square + tile * tile
        sums = both[2 * CHUNK :] + placed_sums([(3, square)])
        both = jnp.concatenate([both[: 2 * CHUNK], sums], axis=0)
    for z in range(out_ref.shape[0]):
        out_ref[z] = both
    held[...] = jnp.where(half == 0, both[:CHUNK], both[CHUNK : 2 * CHUNK])
    backs = []
    for k in range(2):
        tiles = [eight(held, (k * 9 + t) * CASES) for t in range(3)]
        terms = []
        for i, v in enumerate(spread(*tiles)):
            v = jnp.where(rows_live((8, LANES), 1, live_ref[k], i), v, 0.0)
            y = halves(v)
            out = jnp.dot(y[:, :BLOCK], k_ref[k * FACE + i], preferred_element_type=F32)
            terms.append(out[:8] + out[8:])
        backs.append(packed(*terms))
    send_sides(at_ref[1], backs[0], backs[1], near_out, far_out)


def combined(sums_ref, rhs_ref, v_ref, image_ref, w_ref, second_ref, sol_ref, res_ref):
    sums = sums_ref[0]
    for s in range(1, sums_ref.shape[0]):
        sums = sums + sums_ref[s]
    rz, curv, cross, last = (sums[:CASES, n : n + 1] for n in range(4))
    step = rz / curv
    ratio = (step * step * cross - rz) / rz
    grown = 1.0 + ratio
    curv_next = grown * grown * curv - 2.0 * grown * step * cross + step * step * last
    step_next = ratio * rz / curv_next
    on_first = step + step_next * grown
    on_second = step_next * step
    v, w = v_ref[:CASES, :], w_ref[:CASES, :]
    sol = on_first * v - on_second * w
    change = on_second * second_ref[:CASES, :] - on_first * image_ref[:CASES, :]
    for c in range(CASES):
        sol_ref[c] = sol[c : c + 1]
        res_ref[c] = rhs_ref[c] + change[c : c + 1]


SMEM = pl.BlockSpec(memory_space=pltpu.SMEM)
VMEM = pl.BlockSpec(memory_space=pltpu.VMEM)


def shaped(*shape, dtype=F32):
    return jax.ShapeDtypeStruct(shape, dtype)


def in_hbm(value):
    return pltpu.with_memory_space_constraint(value, pltpu.HBM)


def call(kernel, scalars, arrays, out_shape, scratch=(), stays=0, limit=20):
    held = len(arrays) - stays
    return pl.pallas_call(
        kernel,
        in_specs=[SMEM] * len(scalars)
        + [VMEM] * held
        + [pl.BlockSpec(memory_space=pltpu.HBM)] * stays,
        out_specs=tuple(VMEM for _ in out_shape),
        out_shape=tuple(out_shape),
        scratch_shapes=list(scratch),
        compiler_params=pltpu.CompilerParams(vmem_limit_bytes=limit * MIB),
    )(*scalars, *arrays)


def body(rhs, dshift, stiff, face_k, elem_col, elem_row, face_rows):
    span = rhs.shape[2]
    face_len = FACE * BLOCK
    columns, targets = in_hbm(elem_col[0]), in_hbm(elem_row[0])
    live = in_hbm(face_rows[0])
    rhs = in_hbm(rhs.reshape(CASES, 1, span))
    dshift = in_hbm(dshift)
    core = lax.axis_index("slab_2")
    place = jnp.stack([lax.axis_index("dom_1"), core]).astype(jnp.int32)
    z_count = lax.axis_size("dom_0")
    slabs = lax.axis_size(SLAB)
    swap = [(0, 1), (1, 0)]
    across = [(s, (s - 1 if s % 2 == 0 else s + 1) % slabs) for s in range(slabs)]
    face = shaped(8, face_len)
    vector = shaped(8, span)

    def exchanged(near, far):
        return lax.ppermute(near, "slab_2", swap), lax.ppermute(far, SLAB, across)

    faces, face_sq = call(
        face_prep,
        [live],
        [in_hbm(face_k[0])],
        [shaped(2 * FACE, BLOCK, LANES, dtype=BF16), shaped(2, 8, face_len)],
        [pltpu.VMEM((CHUNK * 8, LANES), F32)],
    )
    sq_near, sq_far = exchanged(
        jnp.where(core == 0, face_sq[1], face_sq[0]), jnp.where(core == 0, face_sq[0], face_sq[1])
    )

    blocks, inner = pl.pallas_call(
        stiff_prep,
        grid_spec=pltpu.PrefetchScalarGridSpec(
            num_scalar_prefetch=1,
            grid=(STEPS,),
            in_specs=[pl.BlockSpec((GROUP, BLOCK * BLOCK), lambda i, *_: (i, 0))],
            out_specs=(
                pl.BlockSpec((GROUP, BLOCK, LANES), lambda i, *_: (i, 0, 0)),
                pl.BlockSpec((8, span), lambda i, *_: (0, 0)),
            ),
            scratch_shapes=[
                pltpu.VMEM((CHUNK * 16, LANES), F32),
                pltpu.VMEM((OWN, 8, LANES), F32),
            ],
        ),
        out_shape=(pltpu.HBM((STORED, BLOCK, LANES), BF16), vector),
        compiler_params=pltpu.CompilerParams(vmem_limit_bytes=16 * MIB),
    )(columns, in_hbm(stiff[0]))
    blocks = in_hbm(blocks)

    held = pltpu.VMEM((8, span), F32)
    cols = pltpu.VMEM((OWN, 16, LANES), BF16)
    rows = pltpu.VMEM((SLAB_ROWS, 16, LANES), BF16)
    acc = pltpu.VMEM((SLAB_ROWS, 8, LANES), F32)
    stored = [pltpu.VMEM((STORED, BLOCK, LANES), BF16), pltpu.SemaphoreType.DMA((STEPS,))]

    def all_rows(parts, near, far, sums=()):
        near, far = exchanged(near, far)
        parts = parts.reshape(z_count, 2 * CHUNK, LANES)
        arrived = lax.all_to_all(parts, "dom_0", 0, 0, tiled=True)
        depth = 2 * CHUNK + 8 * len(sums)
        (mine,) = call(
            summed,
            [place, live],
            [arrived, near, far, faces, *sums],
            [shaped(depth, LANES)],
        )
        other = lax.ppermute(mine, "dom_1", swap)
        copies, near, far = call(
            finished,
            [place, live],
            [mine, other, faces],
            [shaped(z_count, depth, LANES), face, face],
            [pltpu.VMEM((CHUNK, LANES), F32)],
        )
        full = lax.all_to_all(copies, "dom_0", 0, 0, tiled=True)
        near, far = exchanged(near, far)
        return full, near, far

    parts, inverse, first, near, far = call(
        first_product,
        [columns, targets, place],
        [rhs, dshift, inner, sq_near, sq_far, blocks],
        [shaped(OWN * CHUNK, LANES), vector, vector, face, face],
        [held, cols, acc, *stored],
        stays=1,
    )
    full, near, far = all_rows(parts, near, far)
    parts, image, second, sums, near, far = call(
        middle_product,
        [columns, targets, place],
        [full.reshape(-1, LANES), rhs, dshift, inverse, first, near, far, blocks],
        [shaped(OWN * CHUNK, LANES), vector, vector, shaped(8, LANES), face, face],
        [held, rows, cols, acc, *stored],
        stays=1,
    )
    full, near, far = all_rows(parts, near, far, [sums])
    full, near, far = lax.optimization_barrier((full, near, far))
    sums = jnp.sum(full[:, 2 * CHUNK :], axis=0)
    sums = lax.all_to_all(
        jnp.broadcast_to(sums[None], (slabs, *sums.shape)), SLAB, 0, 0, tiled=True
    )
    (second_image,) = call(
        last_product,
        [columns, targets, place],
        [full.reshape(-1, LANES), dshift, second, near, far, blocks],
        [vector],
        [rows, pltpu.VMEM((OWN, 8, LANES), F32), *stored],
        stays=1,
    )
    out = shaped(CASES, 1, span)
    return call(combined, [], [sums, rhs, first, image, second, second_image], [out, out])


def solution(mesh):
    finer = Mesh(
        mesh.devices.reshape(4, 2, 2, 8, 2), ("slab_0", "slab_1", "slab_2", "dom_0", "dom_1")
    )
    placed = (
        P(None, SLAB, DOM),
        P(SLAB, DOM),
        P(SLAB, DOM, None),
        P(SLAB, None, DOM, None),
        P(SLAB, DOM),
        P(SLAB, DOM),
        P(SLAB, None),
    )
    return jax.shard_map(
        body,
        mesh=finer,
        in_specs=placed,
        out_specs=(P(None, SLAB, DOM), P(None, SLAB, DOM)),
        check_vma=False,
    )
```

time: 180 us -> 156 us (0.87)
  blocking collectives: 37.9 us -> 0 us
  waiting for transfers between devices: 43 us -> 68.5 us
  local copies, waits for them, and re-layouts: 15.6 us -> 0.64 us
  Pallas kernels: 31 us -> 41.4 us
  starting transfers between devices: 49.5 us -> 43.7 us
    all_to_all x2 -> x0, blocking collectives: 37.9 us -> none  [everywhere(): return lax.all_to_all(sent, axis, 0, 0, tiled=True).sum(axis=0)]
    all_to_all x2, waiting for transfers between devices: 11 us -> 27.6 us  [all_rows(): arrived = lax.all_to_all(parts, 'dom_0', 0, 0, tiled=True)]
    unnamed x27 -> x0, local copies, waits for them, and re-layouts: 14.7 us -> none
    ppermute x12, starting transfers between devices: 30.6 us -> 18.2 us  [the longest x10 12.8 us: exchanged(): return (lax.ppermute(near, 'slab_2', swap), lax.ppermute(far, SLAB, across))]
    pallas_call x10, Pallas kernels: 31 us -> 41.4 us  [the longest x9 31.1 us: call(): pl.pallas_call(kernel, in_specs=[SMEM] * len(scalars) + [VMEM] * held + [...]
    all_to_all x0 -> x1, starting transfers between devices: none -> 6.76 us  [body(): lax.all_to_all(jnp.broadcast_to(sums[None], (slabs, *sums.shape)), SLAB,...]
    all_to_all x2, waiting for transfers between devices: 16.4 us -> 22.9 us  [all_rows(): full = lax.all_to_all(copies, 'dom_0', 0, 0, tiled=True)]
  transfers between devices with their start and end apart: 16 -> 17, of which waited for: 13 -> 15; matrix products, arithmetic and copies ran while one was open for 1% -> 0% of each run, Pallas kernels for 3% -> 10%
where the time goes in v2:
time: 156 us; the launch traced here: 155 us
  waiting for transfers between devices  68.5 us (44%)
  starting transfers between devices  43.7 us (28%)
  Pallas kernels  41.4 us (27%)
    pallas_call x9, Pallas kernels, call(): pl.pallas_call(kernel, in_specs=[SMEM] * len(scalars) + [VMEM] * held + [...  31.1 us
    all_to_all x2, waiting for transfers between devices, all_rows(): arrived = lax.all_to_all(parts, 'dom_0', 0, 0, tiled=True)  27.6 us
    all_to_all x2, waiting for transfers between devices, all_rows(): full = lax.all_to_all(copies, 'dom_0', 0, 0, tiled=True)  22.9 us
    ppermute x10, starting transfers between devices, exchanged(): return (lax.ppermute(near, 'slab_2', swap), lax.ppermute(far, SLAB, across))  12.8 us
    ppermute x10, waiting for transfers between devices, exchanged(): return (lax.ppermute(near, 'slab_2', swap), lax.ppermute(far, SLAB, across))  12.8 us
    all_to_all x2, starting transfers between devices, all_rows(): arrived = lax.all_to_all(parts, 'dom_0', 0, 0, tiled=True)  11.7 us
    pallas_call x1, Pallas kernels, body(): pl.pallas_call(stiff_prep, grid_spec=pltpu.PrefetchScalarGridSpec(num_sca...  10.2 us
    all_to_all x2, starting transfers between devices, all_rows(): full = lax.all_to_all(copies, 'dom_0', 0, 0, tiled=True)  7.08 us
  transfers between devices with their start and end apart: 17, of which 15 were waited for; matrix products, arithmetic and copies ran while one was open for 0% of the time, Pallas kernels for 10%

profile of v2, /device:TPU:1, one launch (start us, length us, event | category | flops | bytes accessed | tf_op | source)
XLA Modules:
  0.0 155.0 jit_solution(11973646924447664830)
XLA Ops:
  0.6 1.2 shard_map.87
  1.8 2.8 %collective-permute-start.1 = (f32[8,384]{1,0:T(8,128)S(1)}, f32[8,384]{1,0:T(8,128)S(1)}, u32[]{:S(2)}, u32[]{:S(2)}) collective-permute-start(f32[8,384]{1,0:T(8,128)S(1)} %get-tuple-element.50), channel_id=1, source_target_pairs={{0,240},{16,32},{32,16},{48,64},{64,48},{80,96},{96,80},{112,128},... | collective-permute-start | bytes 36872 | tf_op jit(solution)/shard_map/ppermute | solution.py:417
  4.6 2.0 %collective-permute-start = (f32[8,384]{1,0:T(8,128)S(1)}, f32[8,384]{1,0:T(8,128)S(1)}, u32[]{:S(2)}, u32[]{:S(2)}) collective-permute-start(f32[8,384]{1,0:T(8,128)S(1)} %get-tuple-element.51), channel_id=1, source_target_pairs={{0,16},{16,0},{1,17},{17,1},{2,18},{18,2},{3,19},{19,3},{4,20},{20... | collective-permute-start | bytes 36872 | tf_op jit(solution)/shard_map/ppermute | solution.py:417
  6.6 0.1 pad_add_fusion.at_ref
  6.7 10.2 %shard_map.86 = (bf16[256,96,128]{2,1,0:T(8,128)(2,1)}, f32[8,1536]{1,0:T(8,128)S(1)}) custom-call(s32[256]{0:T(256)} %bitcast.19, bf16[256,9216]{1,0:T(8,128)(2,1)} %bitcast.17), custom_call_target="tpu_custom_call" | custom-call | tf_op jit(solution)/shard_map/pallas_call | solution.py:430
  17.0 0.0 collective-permute-done.1.far_ref
  17.0 0.0 collective-permute-done.near_ref
  17.0 7.4 %shard_map.88 = (f32[1152,128]{1,0:T(8,128)}, f32[8,1536]{1,0:T(8,128)S(1)}, f32[8,1536]{1,0:T(8,128)S(1)}, f32[8,384]{1,0:T(8,128)S(1)}, f32[8,384]{1,0:T(8,128)S(1)}) custom-call(s32[256]{0:T(256)} %bitcast.20, s32[256]{0:T(256)} %bitcast.28, s32[2]{0:T(128)S(1)} %pad_add_fusion.at_ref, f32[6,1,1536]{2,1,0:T(1,128)} %rhs_ref.5, f32[1,1536]{1,0:T(1,128)} %shift_ref.5, ...), custom_call_target="tpu_custom_call" | custom-call | tf_op jit(solution)/shard_map/pallas_call | solution.py:388
  24.4 8.2 %all-to-all-start = ((f32[8,144,128]{2,1,0:T(8,128)}), f32[8,144,128]{2,1,0:T(8,128)S(1)}, u32[]{:S(2)}, u32[]{:S(2)}) async-start(f32[8,144,128]{2,1,0:T(8,128)} %bitcast.9), calls=%async_computation | async-start | bytes 1179648 | tf_op jit(solution)/shard_map/all_to_all | solution.py:459
  32.6 0.3 collective-permute-start.2
  32.9 0.0 collective-permute-start.3
  32.9 0.9 collective-permute-done.2.near_ref
  33.8 2.5 %collective-permute-done.3.far_ref = f32[8,384]{1,0:T(8,128)S(1)} collective-permute-done((f32[8,384]{1,0:T(8,128)S(1)}, f32[8,384]{1,0:T(8,128)S(1)}, u32[]{:S(2)}, u32[]{:S(2)}) %collective-permute-start.3) | collective-permute-done | bytes 12320 | tf_op jit(solution)/shard_map/ppermute | solution.py:417
  36.3 15.7 %all-to-all-done.y_ref = f32[8,144,128]{2,1,0:T(8,128)S(1)} async-done(((f32[8,144,128]{2,1,0:T(8,128)}), f32[8,144,128]{2,1,0:T(8,128)S(1)}, u32[]{:S(2)}, u32[]{:S(2)}) %all-to-all-start) | async-done | bytes 589856 | tf_op jit(solution)/shard_map/all_to_all | solution.py:459
  52.0 1.0 shard_map.89.a_ref
  53.0 2.7 %collective-permute-start.4 = (f32[144,128]{1,0:T(8,128)S(1)}, f32[144,128]{1,0:T(8,128)S(1)}, u32[]{:S(2)}, u32[]{:S(2)}) collective-permute-start(f32[144,128]{1,0:T(8,128)S(1)} %shard_map.89.a_ref), channel_id=1, source_target_pairs={{0,1},{1,0},{2,3},{3,2},{4,5},{5,4},{6,7},{7,6},{8,9},{9,8},{10,11... | collective-permute-start | bytes 221192 | tf_op jit(solution)/shard_map/ppermute | solution.py:467
  55.7 2.1 %collective-permute-done.4.b_ref = f32[144,128]{1,0:T(8,128)S(1)} collective-permute-done((f32[144,128]{1,0:T(8,128)S(1)}, f32[144,128]{1,0:T(8,128)S(1)}, u32[]{:S(2)}, u32[]{:S(2)}) %collective-permute-start.4) | collective-permute-done | bytes 73760 | tf_op jit(solution)/shard_map/ppermute | solution.py:467
  57.8 1.6 %shard_map.90 = (f32[8,144,128]{2,1,0:T(8,128)}, f32[8,384]{1,0:T(8,128)S(1)}, f32[8,384]{1,0:T(8,128)S(1)}) custom-call(s32[2]{0:T(128)S(1)} %pad_add_fusion.at_ref, s32[2]{0:T(128)} %bitcast.25, f32[144,128]{1,0:T(8,128)S(1)} %shard_map.89.a_ref, f32[144,128]{1,0:T(8,128)S(1)} %collective-permute-done.4.b_ref, bf16[8,96,128]{2,1,0:T(8,128)(2,1)S(1)} %get-tuple-element.32.k_ref), custom_call_target="tpu_custom_call" | custom-call | tf_op jit(solution)/shard_map/pallas_call | solution.py:388
  59.4 3.5 %all-to-all-start.1 = ((f32[8,144,128]{2,1,0:T(8,128)}), f32[8,144,128]{2,1,0:T(8,128)S(1)}, u32[]{:S(2)}, u32[]{:S(2)}) async-start(f32[8,144,128]{2,1,0:T(8,128)} %get-tuple-element.33), calls=%async_computation.1 | async-start | bytes 1179648 | tf_op jit(solution)/shard_map/all_to_all | solution.py:475
  63.0 1.7 %collective-permute-start.5 = (f32[8,384]{1,0:T(8,128)S(1)}, f32[8,384]{1,0:T(8,128)S(1)}, u32[]{:S(2)}, u32[]{:S(2)}) collective-permute-start(f32[8,384]{1,0:T(8,128)S(1)} %get-tuple-element.36), channel_id=1, source_target_pairs={{0,16},{16,0},{1,17},{17,1},{2,18},{18,2},{3,19},{19,3},{4,20},{20... | collective-permute-start | bytes 36872 | tf_op jit(solution)/shard_map/ppermute | solution.py:417
  64.7 0.0 collective-permute-start.6
  64.7 0.8 collective-permute-done.5.near_ref
  65.5 2.3 %collective-permute-done.6.far_ref = f32[8,384]{1,0:T(8,128)S(1)} collective-permute-done((f32[8,384]{1,0:T(8,128)S(1)}, f32[8,384]{1,0:T(8,128)S(1)}, u32[]{:S(2)}, u32[]{:S(2)}) %collective-permute-start.6) | collective-permute-done | bytes 12320 | tf_op jit(solution)/shard_map/ppermute | solution.py:417
  67.8 12.9 %all-to-all-done.1 = f32[8,144,128]{2,1,0:T(8,128)S(1)} async-done(((f32[8,144,128]{2,1,0:T(8,128)}), f32[8,144,128]{2,1,0:T(8,128)S(1)}, u32[]{:S(2)}, u32[]{:S(2)}) %all-to-all-start.1) | async-done | bytes 589856 | tf_op jit(solution)/shard_map/all_to_all | solution.py:475
  80.7 10.5 %shard_map.91 = (f32[1152,128]{1,0:T(8,128)}, f32[8,1536]{1,0:T(8,128)S(1)}, f32[8,1536]{1,0:T(8,128)S(1)}, f32[8,128]{1,0:T(8,128)S(1)}, f32[8,384]{1,0:T(8,128)S(1)}, /*index=5*/f32[8,384]{1,0:T(8,128)S(1)}) custom-call(s32[256]{0:T(256)} %bitcast.21, s32[256]{0:T(256)} %bitcast.29, s32[2]{0:T(128)S(1)} %pad_add_fusion.at_ref, f32[1152,128]{1,0:T(8,128)S(1)} %bitcast.16, ...), custom_call_target="tpu_custom_call" | custom-call | tf_op jit(solution)/shard_map/pallas_call | solution.py:388
  91.2 3.5 %all-to-all-start.2 = ((f32[8,144,128]{2,1,0:T(8,128)}), f32[8,144,128]{2,1,0:T(8,128)S(1)}, u32[]{:S(2)}, u32[]{:S(2)}) async-start(f32[8,144,128]{2,1,0:T(8,128)} %bitcast.11), calls=%async_computation.2 | async-start | bytes 1179648 | tf_op jit(solution)/shard_map/all_to_all | solution.py:459
  94.8 2.1 %collective-permute-start.7 = (f32[8,384]{1,0:T(8,128)S(1)}, f32[8,384]{1,0:T(8,128)S(1)}, u32[]{:S(2)}, u32[]{:S(2)}) collective-permute-start(f32[8,384]{1,0:T(8,128)S(1)} %get-tuple-element.39), channel_id=1, source_target_pairs={{0,16},{16,0},{1,17},{17,1},{2,18},{18,2},{3,19},{19,3},{4,20},{20... | collective-permute-start | bytes 36872 | tf_op jit(solution)/shard_map/ppermute | solution.py:417
  96.9 0.0 collective-permute-start.8
  96.9 0.8 collective-permute-done.7.near_ref
  97.8 2.3 %collective-permute-done.8.far_ref = f32[8,384]{1,0:T(8,128)S(1)} collective-permute-done((f32[8,384]{1,0:T(8,128)S(1)}, f32[8,384]{1,0:T(8,128)S(1)}, u32[]{:S(2)}, u32[]{:S(2)}) %collective-permute-start.8) | collective-permute-done | bytes 12320 | tf_op jit(solution)/shard_map/ppermute | solution.py:417
  100.0 11.9 %all-to-all-done.2.y_ref = f32[8,144,128]{2,1,0:T(8,128)S(1)} async-done(((f32[8,144,128]{2,1,0:T(8,128)}), f32[8,144,128]{2,1,0:T(8,128)S(1)}, u32[]{:S(2)}, u32[]{:S(2)}) %all-to-all-start.2) | async-done | bytes 589856 | tf_op jit(solution)/shard_map/all_to_all | solution.py:459
  111.9 1.0 shard_map.92.a_ref
  112.9 2.7 %collective-permute-start.9 = (f32[152,128]{1,0:T(8,128)S(1)}, f32[152,128]{1,0:T(8,128)S(1)}, u32[]{:S(2)}, u32[]{:S(2)}) collective-permute-start(f32[152,128]{1,0:T(8,128)S(1)} %shard_map.92.a_ref), channel_id=1, source_target_pairs={{0,1},{1,0},{2,3},{3,2},{4,5},{5,4},{6,7},{7,6},{8,9},{9,8},{10,11... | collective-permute-start | bytes 233480 | tf_op jit(solution)/shard_map/ppermute | solution.py:467
  115.6 2.1 %collective-permute-done.9.b_ref = f32[152,128]{1,0:T(8,128)S(1)} collective-permute-done((f32[152,128]{1,0:T(8,128)S(1)}, f32[152,128]{1,0:T(8,128)S(1)}, u32[]{:S(2)}, u32[]{:S(2)}) %collective-permute-start.9) | collective-permute-done | bytes 77856 | tf_op jit(solution)/shard_map/ppermute | solution.py:467
  117.7 1.8 %shard_map.93 = (f32[8,152,128]{2,1,0:T(8,128)}, f32[8,384]{1,0:T(8,128)S(1)}, f32[8,384]{1,0:T(8,128)S(1)}) custom-call(s32[2]{0:T(128)S(1)} %pad_add_fusion.at_ref, s32[2]{0:T(128)} %bitcast.27, f32[152,128]{1,0:T(8,128)S(1)} %shard_map.92.a_ref, f32[152,128]{1,0:T(8,128)S(1)} %collective-permute-done.9.b_ref, bf16[8,96,128]{2,1,0:T(8,128)(2,1)S(1)} %get-tuple-element.32.k_ref), custom_call_target="tpu_custom_call" | custom-call | tf_op jit(solution)/shard_map/pallas_call | solution.py:388
  119.5 3.5 %all-to-all-start.3 = ((f32[8,152,128]{2,1,0:T(8,128)}), f32[8,152,128]{2,1,0:T(8,128)S(1)}, u32[]{:S(2)}, u32[]{:S(2)}) async-start(f32[8,152,128]{2,1,0:T(8,128)} %get-tuple-element.42), calls=%async_computation.3 | async-start | bytes 1245184 | tf_op jit(solution)/shard_map/all_to_all | solution.py:475
  123.1 3.9 %collective-permute-start.10 = (f32[8,384]{1,0:T(8,128)S(1)}, f32[8,384]{1,0:T(8,128)S(1)}, u32[]{:S(2)}, u32[]{:S(2)}) collective-permute-start(f32[8,384]{1,0:T(8,128)S(1)} %get-tuple-element.43), channel_id=1, source_target_pairs={{0,16},{16,0},{1,17},{17,1},{2,18},{18,2},{3,19},{19,3},{4,20},{20... | collective-permute-start | bytes 36872 | tf_op jit(solution)/shard_map/ppermute | solution.py:417
  126.9 0.0 collective-permute-start.11
  126.9 0.8 collective-permute-done.10.near_ref
  127.8 2.3 %collective-permute-done.11.far_ref = f32[8,384]{1,0:T(8,128)S(1)} collective-permute-done((f32[8,384]{1,0:T(8,128)S(1)}, f32[8,384]{1,0:T(8,128)S(1)}, u32[]{:S(2)}, u32[]{:S(2)}) %collective-permute-start.11) | collective-permute-done | bytes 12320 | tf_op jit(solution)/shard_map/ppermute | solution.py:417
  130.1 10.0 %all-to-all-done.3 = f32[8,152,128]{2,1,0:T(8,128)S(1)} async-done(((f32[8,152,128]{2,1,0:T(8,128)}), f32[8,152,128]{2,1,0:T(8,128)S(1)}, u32[]{:S(2)}, u32[]{:S(2)}) %all-to-all-start.3) | async-done | bytes 622624 | tf_op jit(solution)/shard_map/all_to_all | solution.py:475
  140.1 0.6 broadcast_in_dim.2
  140.7 6.8 %all-to-all-start.4 = ((f32[16,8,128]{2,1,0:T(8,128)}), f32[16,8,128]{2,1,0:T(8,128)S(1)}, u32[]{:S(2)}, u32[]{:S(2)}) async-start(f32[16,8,128]{2,1,0:T(8,128)} %broadcast_in_dim.2), calls=%async_computation.4 | async-start | bytes 131072 | tf_op jit(solution)/shard_map/all_to_all | solution.py:499
  147.5 5.0 %shard_map.94.second_ref = f32[8,1536]{1,0:T(8,128)S(1)} custom-call(s32[256]{0:T(256)} %bitcast.22, s32[256]{0:T(256)} %bitcast.30, s32[2]{0:T(128)S(1)} %pad_add_fusion.at_ref, f32[1216,128]{1,0:T(8,128)S(1)} %bitcast.15, f32[1,1536]{1,0:T(1,128)} %shift_ref.5, f32[8,1536]{1,0:T(8,128)S(1)} %get-tuple-element.47.v_ref.w_ref, ...), custom_call_target="tpu_custom_call" | custom-call | tf_op jit(solution)/shard_map/pallas_call | solution.py:388
  152.5 0.9 all-to-all-done.4.sums_ref
  153.4 1.6 %shard_map.95 = (f32[6,1,1536]{2,1,0:T(1,128)}, f32[6,1,1536]{2,1,0:T(1,128)}) custom-call(f32[16,8,128]{2,1,0:T(8,128)S(1)} %all-to-all-done.4.sums_ref, f32[6,1,1536]{2,1,0:T(1,128)} %rhs_ref.5, f32[8,1536]{1,0:T(8,128)S(1)} %get-tuple-element.35.v_ref, f32[8,1536]{1,0:T(8,128)S(1)} %get-tuple-element.46.image_ref, ...), custom_call_target="tpu_custom_call" | custom-call | tf_op jit(solution)/shard_map/pallas_call | solution.py:388
  (2 shorter events, 0.0 us)
Async XLA Ops:
  1.8 15.1 %collective-permute-start.1 = (f32[8,384]{1,0:T(8,128)S(1)}, f32[8,384]{1,0:T(8,128)S(1)}, u32[]{:S(2)}, u32[]{:S(2)}) collective-permute-start(f32[8,384]{1,0:T(8,128)S(1)} %get-tuple-element.50), channel_id=1, source_target_pairs={{0,240},{16,32},{32,16},{48,64},{64,48},{80,96},{96,80},{112,128},... | collective-permute-start | bytes 36872 | tf_op jit(solution)/shard_map/ppermute | solution.py:417
  4.6 12.4 %collective-permute-start = (f32[8,384]{1,0:T(8,128)S(1)}, f32[8,384]{1,0:T(8,128)S(1)}, u32[]{:S(2)}, u32[]{:S(2)}) collective-permute-start(f32[8,384]{1,0:T(8,128)S(1)} %get-tuple-element.51), channel_id=1, source_target_pairs={{0,16},{16,0},{1,17},{17,1},{2,18},{18,2},{3,19},{19,3},{4,20},{20... | collective-permute-start | bytes 36872 | tf_op jit(solution)/shard_map/ppermute | solution.py:417
  24.4 27.6 %all-to-all-start = ((f32[8,144,128]{2,1,0:T(8,128)}), f32[8,144,128]{2,1,0:T(8,128)S(1)}, u32[]{:S(2)}, u32[]{:S(2)}) async-start(f32[8,144,128]{2,1,0:T(8,128)} %bitcast.9), calls=%async_computation | async-start | bytes 1179648 | tf_op jit(solution)/shard_map/all_to_all | solution.py:459
  32.6 1.2 collective-permute-start.2
  32.9 3.4 %collective-permute-start.3 = (f32[8,384]{1,0:T(8,128)S(1)}, f32[8,384]{1,0:T(8,128)S(1)}, u32[]{:S(2)}, u32[]{:S(2)}) collective-permute-start(f32[8,384]{1,0:T(8,128)S(1)} %get-tuple-element.31), channel_id=1, source_target_pairs={{0,240},{16,32},{32,16},{48,64},{64,48},{80,96},{96,80},{112,128},... | collective-permute-start | bytes 36872 | tf_op jit(solution)/shard_map/ppermute | solution.py:417
  53.0 4.8 %collective-permute-start.4 = (f32[144,128]{1,0:T(8,128)S(1)}, f32[144,128]{1,0:T(8,128)S(1)}, u32[]{:S(2)}, u32[]{:S(2)}) collective-permute-start(f32[144,128]{1,0:T(8,128)S(1)} %shard_map.89.a_ref), channel_id=1, source_target_pairs={{0,1},{1,0},{2,3},{3,2},{4,5},{5,4},{6,7},{7,6},{8,9},{9,8},{10,11... | collective-permute-start | bytes 221192 | tf_op jit(solution)/shard_map/ppermute | solution.py:467
  59.4 21.3 %all-to-all-start.1 = ((f32[8,144,128]{2,1,0:T(8,128)}), f32[8,144,128]{2,1,0:T(8,128)S(1)}, u32[]{:S(2)}, u32[]{:S(2)}) async-start(f32[8,144,128]{2,1,0:T(8,128)} %get-tuple-element.33), calls=%async_computation.1 | async-start | bytes 1179648 | tf_op jit(solution)/shard_map/all_to_all | solution.py:475
  63.0 2.5 %collective-permute-start.5 = (f32[8,384]{1,0:T(8,128)S(1)}, f32[8,384]{1,0:T(8,128)S(1)}, u32[]{:S(2)}, u32[]{:S(2)}) collective-permute-start(f32[8,384]{1,0:T(8,128)S(1)} %get-tuple-element.36), channel_id=1, source_target_pairs={{0,16},{16,0},{1,17},{17,1},{2,18},{18,2},{3,19},{19,3},{4,20},{20... | collective-permute-start | bytes 36872 | tf_op jit(solution)/shard_map/ppermute | solution.py:417
  64.7 3.1 %collective-permute-start.6 = (f32[8,384]{1,0:T(8,128)S(1)}, f32[8,384]{1,0:T(8,128)S(1)}, u32[]{:S(2)}, u32[]{:S(2)}) collective-permute-start(f32[8,384]{1,0:T(8,128)S(1)} %get-tuple-element.37), channel_id=1, source_target_pairs={{0,240},{16,32},{32,16},{48,64},{64,48},{80,96},{96,80},{112,128},... | collective-permute-start | bytes 36872 | tf_op jit(solution)/shard_map/ppermute | solution.py:417
  91.2 20.7 %all-to-all-start.2 = ((f32[8,144,128]{2,1,0:T(8,128)}), f32[8,144,128]{2,1,0:T(8,128)S(1)}, u32[]{:S(2)}, u32[]{:S(2)}) async-start(f32[8,144,128]{2,1,0:T(8,128)} %bitcast.11), calls=%async_computation.2 | async-start | bytes 1179648 | tf_op jit(solution)/shard_map/all_to_all | solution.py:459
  94.8 3.0 %collective-permute-start.7 = (f32[8,384]{1,0:T(8,128)S(1)}, f32[8,384]{1,0:T(8,128)S(1)}, u32[]{:S(2)}, u32[]{:S(2)}) collective-permute-start(f32[8,384]{1,0:T(8,128)S(1)} %get-tuple-element.39), channel_id=1, source_target_pairs={{0,16},{16,0},{1,17},{17,1},{2,18},{18,2},{3,19},{19,3},{4,20},{20... | collective-permute-start | bytes 36872 | tf_op jit(solution)/shard_map/ppermute | solution.py:417
  96.9 3.1 %collective-permute-start.8 = (f32[8,384]{1,0:T(8,128)S(1)}, f32[8,384]{1,0:T(8,128)S(1)}, u32[]{:S(2)}, u32[]{:S(2)}) collective-permute-start(f32[8,384]{1,0:T(8,128)S(1)} %get-tuple-element.40), channel_id=1, source_target_pairs={{0,240},{16,32},{32,16},{48,64},{64,48},{80,96},{96,80},{112,128},... | collective-permute-start | bytes 36872 | tf_op jit(solution)/shard_map/ppermute | solution.py:417
  112.9 4.8 %collective-permute-start.9 = (f32[152,128]{1,0:T(8,128)S(1)}, f32[152,128]{1,0:T(8,128)S(1)}, u32[]{:S(2)}, u32[]{:S(2)}) collective-permute-start(f32[152,128]{1,0:T(8,128)S(1)} %shard_map.92.a_ref), channel_id=1, source_target_pairs={{0,1},{1,0},{2,3},{3,2},{4,5},{5,4},{6,7},{7,6},{8,9},{9,8},{10,11... | collective-permute-start | bytes 233480 | tf_op jit(solution)/shard_map/ppermute | solution.py:467
  119.5 20.6 %all-to-all-start.3 = ((f32[8,152,128]{2,1,0:T(8,128)}), f32[8,152,128]{2,1,0:T(8,128)S(1)}, u32[]{:S(2)}, u32[]{:S(2)}) async-start(f32[8,152,128]{2,1,0:T(8,128)} %get-tuple-element.42), calls=%async_computation.3 | async-start | bytes 1245184 | tf_op jit(solution)/shard_map/all_to_all | solution.py:475
  123.1 4.7 %collective-permute-start.10 = (f32[8,384]{1,0:T(8,128)S(1)}, f32[8,384]{1,0:T(8,128)S(1)}, u32[]{:S(2)}, u32[]{:S(2)}) collective-permute-start(f32[8,384]{1,0:T(8,128)S(1)} %get-tuple-element.43), channel_id=1, source_target_pairs={{0,16},{16,0},{1,17},{17,1},{2,18},{18,2},{3,19},{19,3},{4,20},{20... | collective-permute-start | bytes 36872 | tf_op jit(solution)/shard_map/ppermute | solution.py:417
  126.9 3.1 %collective-permute-start.11 = (f32[8,384]{1,0:T(8,128)S(1)}, f32[8,384]{1,0:T(8,128)S(1)}, u32[]{:S(2)}, u32[]{:S(2)}) collective-permute-start(f32[8,384]{1,0:T(8,128)S(1)} %get-tuple-element.44), channel_id=1, source_target_pairs={{0,240},{16,32},{32,16},{48,64},{64,48},{80,96},{96,80},{112,128},... | collective-permute-start | bytes 36872 | tf_op jit(solution)/shard_map/ppermute | solution.py:417
  140.7 12.7 %all-to-all-start.4 = ((f32[16,8,128]{2,1,0:T(8,128)}), f32[16,8,128]{2,1,0:T(8,128)S(1)}, u32[]{:S(2)}, u32[]{:S(2)}) async-start(f32[16,8,128]{2,1,0:T(8,128)} %broadcast_in_dim.2), calls=%async_computation.4 | async-start | bytes 131072 | tf_op jit(solution)/shard_map/all_to_all | solution.py:499

commit v3 on v2

--- a/solution.py
+++ b/solution.py
@@ -212,11 +212,10 @@
         far_ref[:, tile_at(t)] = jnp.where(core == 0, lower[t], upper[t])
 
 
-def first_product(
-    col_ref, row_ref, at_ref, rhs_ref, shift_ref, diag_ref, near_ref, far_ref, k_any,
-    out_ref, inverse_ref, v_ref, near_out, far_out, held, cols, acc, k_ref, sems,
+def first_vector(
+    at_ref, rhs_ref, shift_ref, diag_ref, near_ref, far_ref,
+    inverse_ref, v_ref, near_out, far_out, held,
 ):
-    fetch(k_any, k_ref, sems)
     core = at_ref[1]
     held[...] = jnp.zeros_like(held)
     for c in range(CASES):
@@ -235,14 +234,27 @@
         v_ref[:, tile_at(t)] = tile
         tiles.append(tile)
     send_sides(core, tiles[:3], tiles[9:], near_out, far_out)
+
+
+def forward_product(col_ref, row_ref, v_ref, k_any, out_ref, cols, acc, k_ref, sems):
+    fetch(k_any, k_ref, sems)
     wait = functools.partial(fetched, k_any, k_ref, sems)
+    tiles = [v_ref[:, tile_at(t)] for t in range(TILES)]
     forward(col_ref, row_ref, tiles, k_ref, out_ref, cols, acc, wait)
 
 
-def image_tiles(core, tiles, v_ref, shift_ref, near_ref, far_ref):
+def adjoint_product(col_ref, row_ref, y_ref, k_any, out_ref, rows, acc, k_ref, sems):
+    fetch(k_any, k_ref, sems)
+    wait = functools.partial(fetched, k_any, k_ref, sems)
+    for t, tile in enumerate(adjoint(col_ref, row_ref, y_ref, k_ref, rows, acc, wait)):
+        out_ref[:, tile_at(t)] = tile
+
+
+def image_tiles(core, part_ref, v_ref, shift_ref, near_ref, far_ref):
     below, above = both_sides(core, near_ref, far_ref)
     whole = [
-        tile + shift_ref[:, tile_at(t)] * v_ref[:, tile_at(t)] for t, tile in enumerate(tiles)
+        part_ref[:, tile_at(t)] + shift_ref[:, tile_at(t)] * v_ref[:, tile_at(t)]
+        for t in range(TILES)
     ]
     return (
         [whole[t] + below[t] for t in range(3)]
@@ -259,21 +271,17 @@
     return out
 
 
-def middle_product(
-    col_ref, row_ref, at_ref, y_ref, rhs_ref, shift_ref, inverse_ref, v_ref, near_ref, far_ref,
-    k_any, out_ref, image_ref, w_ref, sums_ref, near_out, far_out, held, rows, cols, acc,
-    k_ref, sems,
+def second_vector(
+    at_ref, part_ref, rhs_ref, shift_ref, inverse_ref, v_ref, near_ref, far_ref,
+    image_ref, w_ref, sums_ref, near_out, far_out, held,
 ):
-    fetch(k_any, k_ref, sems)
     core = at_ref[1]
-    wait = functools.partial(fetched, k_any, k_ref, sems)
-    tiles = adjoint(col_ref, row_ref, y_ref, k_ref, rows, acc, wait)
-    tiles = image_tiles(core, tiles, v_ref, shift_ref, near_ref, far_ref)
     held[...] = jnp.zeros_like(held)
     for c in range(CASES):
         held[c : c + 1, :] = rhs_ref[c]
     sums = [jnp.zeros((8, LANES), F32) for _ in range(4)]
     second = []
+    tiles = image_tiles(core, part_ref, v_ref, shift_ref, near_ref, far_ref)
     for t, image in enumerate(tiles):
         image_ref[:, tile_at(t)] = image
         w = inverse_ref[:, tile_at(t)] * image
@@ -286,18 +294,6 @@
         sums[3] = sums[3] + shift_ref[:, tile_at(t)] * w * w
     sums_ref[...] = placed_sums(enumerate(sums))
     send_sides(core, second[:3], second[9:], near_out, far_out)
-    forward(col_ref, row_ref, second, k_ref, out_ref, cols, acc)
-
-
-def last_product(
-    col_ref, row_ref, at_ref, y_ref, shift_ref, v_ref, near_ref, far_ref, k_any,
-    image_ref, rows, acc, k_ref, sems,
-):
-    fetch(k_any, k_ref, sems)
-    wait = functools.partial(fetched, k_any, k_ref, sems)
-    tiles = adjoint(col_ref, row_ref, y_ref, k_ref, rows, acc, wait)
-    for t, tile in enumerate(image_tiles(at_ref[1], tiles, v_ref, shift_ref, near_ref, far_ref)):
-        image_ref[:, tile_at(t)] = tile
 
 
 def summed(at_ref, live_ref, y_ref, near_ref, far_ref, k_ref, *rest):
@@ -351,11 +347,14 @@
     send_sides(at_ref[1], backs[0], backs[1], near_out, far_out)
 
 
-def combined(sums_ref, rhs_ref, v_ref, image_ref, w_ref, second_ref, sol_ref, res_ref):
+def combined(
+    at_ref, sums_ref, rhs_ref, shift_ref, v_ref, image_ref, w_ref, part_ref, near_ref, far_ref,
+    sol_ref, res_ref,
+):
     sums = sums_ref[0]
     for s in range(1, sums_ref.shape[0]):
         sums = sums + sums_ref[s]
-    rz, curv, cross, last = (sums[:CASES, n : n + 1] for n in range(4))
+    rz, curv, cross, last = (sums[:, n : n + 1] for n in range(4))
     step = rz / curv
     ratio = (step * step * cross - rz) / rz
     grown = 1.0 + ratio
@@ -363,12 +362,14 @@
     step_next = ratio * rz / curv_next
     on_first = step + step_next * grown
     on_second = step_next * step
-    v, w = v_ref[:CASES, :], w_ref[:CASES, :]
-    sol = on_first * v - on_second * w
-    change = on_second * second_ref[:CASES, :] - on_first * image_ref[:CASES, :]
-    for c in range(CASES):
-        sol_ref[c] = sol[c : c + 1]
-        res_ref[c] = rhs_ref[c] + change[c : c + 1]
+    tiles = image_tiles(at_ref[1], part_ref, w_ref, shift_ref, near_ref, far_ref)
+    for t, second in enumerate(tiles):
+        to = tile_at(t)
+        sol = on_first * v_ref[:, to] - on_second * w_ref[:, to]
+        change = on_second * second - on_first * image_ref[:, to]
+        for c in range(CASES):
+            sol_ref[c, :, to] = sol[c : c + 1]
+            res_ref[c, :, to] = rhs_ref[c, :, to] + change[c : c + 1]
 
 
 SMEM = pl.BlockSpec(memory_space=pltpu.SMEM)
@@ -453,9 +454,18 @@
     acc = pltpu.VMEM((SLAB_ROWS, 8, LANES), F32)
     stored = [pltpu.VMEM((STORED, BLOCK, LANES), BF16), pltpu.SemaphoreType.DMA((STEPS,))]
 
-    def all_rows(parts, near, far, sums=()):
+    def all_rows(vector, near, far, sums=()):
         near, far = exchanged(near, far)
+        (parts,) = call(
+            forward_product,
+            [columns, targets],
+            [vector, blocks],
+            [shaped(OWN * CHUNK, LANES)],
+            [cols, acc, *stored],
+            stays=1,
+        )
         parts = parts.reshape(z_count, 2 * CHUNK, LANES)
+        parts, near, far = lax.optimization_barrier((parts, near, far))
         arrived = lax.all_to_all(parts, "dom_0", 0, 0, tiled=True)
         depth = 2 * CHUNK + 8 * len(sums)
         (mine,) = call(
@@ -473,42 +483,48 @@
             [pltpu.VMEM((CHUNK, LANES), F32)],
         )
         full = lax.all_to_all(copies, "dom_0", 0, 0, tiled=True)
+        full, near, far = lax.optimization_barrier((full, near, far))
         near, far = exchanged(near, far)
         return full, near, far
 
-    parts, inverse, first, near, far = call(
-        first_product,
-        [columns, targets, place],
-        [rhs, dshift, inner, sq_near, sq_far, blocks],
-        [shaped(OWN * CHUNK, LANES), vector, vector, face, face],
-        [held, cols, acc, *stored],
-        stays=1,
-    )
-    full, near, far = all_rows(parts, near, far)
-    parts, image, second, sums, near, far = call(
-        middle_product,
-        [columns, targets, place],
-        [full.reshape(-1, LANES), rhs, dshift, inverse, first, near, far, blocks],
-        [shaped(OWN * CHUNK, LANES), vector, vector, shaped(8, LANES), face, face],
-        [held, rows, cols, acc, *stored],
-        stays=1,
-    )
-    full, near, far = all_rows(parts, near, far, [sums])
-    full, near, far = lax.optimization_barrier((full, near, far))
+    def adjoint_part(full):
+        return call(
+            adjoint_product,
+            [columns, targets],
+            [full.reshape(-1, LANES), blocks],
+            [vector],
+            [rows, pltpu.VMEM((OWN, 8, LANES), F32), *stored],
+            stays=1,
+        )[0]
+
+    inverse, first, near, far = call(
+        first_vector,
+        [place],
+        [rhs, dshift, inner, sq_near, sq_far],
+        [vector, vector, face, face],
+        [held],
+    )
+    full, near, far = all_rows(first, near, far)
+    part_of = adjoint_part(full)
+    image, second, sums, near, far = call(
+        second_vector,
+        [place],
+        [part_of, rhs, dshift, inverse, first, near, far],
+        [vector, vector, shaped(8, LANES), face, face],
+        [held],
+    )
+    full, near, far = all_rows(second, near, far, [sums])
     sums = jnp.sum(full[:, 2 * CHUNK :], axis=0)
     sums = lax.all_to_all(
         jnp.broadcast_to(sums[None], (slabs, *sums.shape)), SLAB, 0, 0, tiled=True
     )
-    (second_image,) = call(
-        last_product,
-        [columns, targets, place],
-        [full.reshape(-1, LANES), dshift, second, near, far, blocks],
-        [vector],
-        [rows, pltpu.VMEM((OWN, 8, LANES), F32), *stored],
-        stays=1,
-    )
     out = shaped(CASES, 1, span)
-    return call(combined, [], [sums, rhs, first, image, second, second_image], [out, out])
+    return call(
+        combined,
+        [place],
+        [sums, rhs, dshift, first, image, second, adjoint_part(full), near, far],
+        [out, out],
+    )
 
 
 def solution(mesh):

time: 156 us -> 163 us (1.045)
  blocking collectives: 0 us -> 84 us
  waiting for transfers between devices: 68.5 us -> 4.52 us
  starting transfers between devices: 43.7 us -> 29.8 us
    all_to_all x0 -> x4, blocking collectives: none -> 84 us  [the longest x2 46.8 us: all_rows(): arrived = lax.all_to_all(parts, 'dom_0', 0, 0, tiled=True)]
    all_to_all x4 -> x0, waiting for transfers between devices: 50.5 us -> none  [the longest x2 27.6 us: all_rows(): arrived = lax.all_to_all(parts, 'dom_0', 0, 0, tiled=True)]
    all_to_all x4 -> x0, starting transfers between devices: 18.8 us -> none  [the longest x2 11.7 us: all_rows(): arrived = lax.all_to_all(parts, 'dom_0', 0, 0, tiled=True)]
    ppermute x10, waiting for transfers between devices: 12.8 us -> 0.03 us  [exchanged(): return (lax.ppermute(near, 'slab_2', swap), lax.ppermute(far, SLAB, across))]
    ppermute x10, starting transfers between devices: 12.8 us -> 18.3 us  [exchanged(): return (lax.ppermute(near, 'slab_2', swap), lax.ppermute(far, SLAB, across))]
    pallas_call x9 -> x12, Pallas kernels: 31.1 us -> 31.4 us  [call(): pl.pallas_call(kernel, in_specs=[SMEM] * len(scalars) + [VMEM] * held + [...]
  transfers between devices with their start and end apart: 17 -> 13, of which waited for: 15 -> 2; matrix products, arithmetic and copies ran while one was open for 0% -> 0% of each run, Pallas kernels for 10% -> 20%
where the time goes in v3:
time: 163 us; the launch traced here: 161 us
  blocking collectives  84 us (52%)
  Pallas kernels  41.6 us (26%)
  starting transfers between devices  29.8 us (18%)
  waiting for transfers between devices  4.52 us (3%)
    all_to_all x2, blocking collectives, all_rows(): arrived = lax.all_to_all(parts, 'dom_0', 0, 0, tiled=True)  46.8 us
    all_to_all x2, blocking collectives, all_rows(): full = lax.all_to_all(copies, 'dom_0', 0, 0, tiled=True)  37.2 us
    pallas_call x12, Pallas kernels, call(): pl.pallas_call(kernel, in_specs=[SMEM] * len(scalars) + [VMEM] * held + [...  31.4 us
    ppermute x10, starting transfers between devices, exchanged(): return (lax.ppermute(near, 'slab_2', swap), lax.ppermute(far, SLAB, across))  18.3 us
    pallas_call x1, Pallas kernels, body(): pl.pallas_call(stiff_prep, grid_spec=pltpu.PrefetchScalarGridSpec(num_sca...  10.2 us
    all_to_all x1, starting transfers between devices, body(): lax.all_to_all(jnp.broadcast_to(sums[None], (slabs, *sums.shape)), SLAB,...  6.38 us
    ppermute x2, starting transfers between devices, all_rows(): other = lax.ppermute(mine, 'dom_1', swap)  5.06 us
    ppermute x2, waiting for transfers between devices, all_rows(): other = lax.ppermute(mine, 'dom_1', swap)  4.5 us
  transfers between devices with their start and end apart: 13, of which 2 were waited for; matrix products, arithmetic and copies ran while one was open for 0% of the time, Pallas kernels for 20%

profile of v3, /device:TPU:1, one launch (start us, length us, event | category | flops | bytes accessed | tf_op | source)
XLA Modules:
  0.0 161.3 jit_solution(14023525697454898222)
XLA Ops:
  0.6 1.2 shard_map.87
  1.8 2.8 %collective-permute-start.1 = (f32[8,384]{1,0:T(8,128)S(1)}, f32[8,384]{1,0:T(8,128)S(1)}, u32[]{:S(2)}, u32[]{:S(2)}) collective-permute-start(f32[8,384]{1,0:T(8,128)S(1)} %get-tuple-element.64), channel_id=1, source_target_pairs={{0,240},{16,32},{32,16},{48,64},{64,48},{80,96},{96,80},{112,128},... | collective-permute-start | bytes 36872 | tf_op jit(solution)/shard_map/ppermute | solution.py:418
  4.6 2.0 %collective-permute-start = (f32[8,384]{1,0:T(8,128)S(1)}, f32[8,384]{1,0:T(8,128)S(1)}, u32[]{:S(2)}, u32[]{:S(2)}) collective-permute-start(f32[8,384]{1,0:T(8,128)S(1)} %get-tuple-element.65), channel_id=1, source_target_pairs={{0,16},{16,0},{1,17},{17,1},{2,18},{18,2},{3,19},{19,3},{4,20},{20... | collective-permute-start | bytes 36872 | tf_op jit(solution)/shard_map/ppermute | solution.py:418
  6.6 0.1 pad_add_fusion.at_ref
  6.7 10.2 %shard_map.86 = (bf16[256,96,128]{2,1,0:T(8,128)(2,1)}, f32[8,1536]{1,0:T(8,128)S(1)}) custom-call(s32[256]{0:T(256)} %bitcast.21, bf16[256,9216]{1,0:T(8,128)(2,1)} %bitcast.19), custom_call_target="tpu_custom_call" | custom-call | tf_op jit(solution)/shard_map/pallas_call | solution.py:431
  17.0 0.0 collective-permute-done.1.far_ref
  17.0 0.0 collective-permute-done.near_ref
  17.0 0.8 shard_map.88
  17.8 0.1 collective-permute-start.2
  17.9 0.1 collective-permute-start.3
  18.0 6.4 %shard_map.89 = f32[1152,128]{1,0:T(8,128)S(1)} custom-call(s32[256]{0:T(256)} %bitcast.22, s32[256]{0:T(256)} %bitcast.26, f32[8,1536]{1,0:T(8,128)S(1)} %get-tuple-element.35.v_ref, bf16[256,96,128]{2,1,0:T(8,128)(2,1)} %get-tuple-element.36.k_any), custom_call_target="tpu_custom_call" | custom-call | tf_op jit(solution)/shard_map/pallas_call | solution.py:389
  24.4 0.0 collective-permute-done.2.near_ref
  24.4 0.0 collective-permute-done.3.far_ref
  24.4 25.0 %all_to_all.25.y_ref = f32[8,144,128]{2,1,0:T(8,128)S(1)} all-to-all(f32[8,144,128]{2,1,0:T(8,128)S(1)} %bitcast.17), channel_id=1, replica_groups=mesh['slab_0'=4,'slab_1'=2,'slab_2'=2,'dom_0'=8,'dom_1'=2] {'dom_0'}, dimensions={0} | all-to-all | bytes 1179648 | tf_op jit(solution)/shard_map/all_to_all | solution.py:469
  49.5 1.0 shard_map.90.a_ref
  50.5 2.4 %collective-permute-start.4 = (f32[144,128]{1,0:T(8,128)S(1)}, f32[144,128]{1,0:T(8,128)S(1)}, u32[]{:S(2)}, u32[]{:S(2)}) collective-permute-start(f32[144,128]{1,0:T(8,128)S(1)} %shard_map.90.a_ref), channel_id=1, source_target_pairs={{0,1},{1,0},{2,3},{3,2},{4,5},{5,4},{6,7},{7,6},{8,9},{9,8},{10,11... | collective-permute-start | bytes 221192 | tf_op jit(solution)/shard_map/ppermute | solution.py:477
  52.9 2.4 %collective-permute-done.4.b_ref = f32[144,128]{1,0:T(8,128)S(1)} collective-permute-done((f32[144,128]{1,0:T(8,128)S(1)}, f32[144,128]{1,0:T(8,128)S(1)}, u32[]{:S(2)}, u32[]{:S(2)}) %collective-permute-start.4) | collective-permute-done | bytes 73760 | tf_op jit(solution)/shard_map/ppermute | solution.py:477
  55.3 1.0 shard_map.91
  56.2 17.3 %all_to_all.26 = f32[8,144,128]{2,1,0:T(8,128)S(1)} all-to-all(f32[8,144,128]{2,1,0:T(8,128)S(1)} %get-tuple-element.43), channel_id=1, replica_groups=mesh['slab_0'=4,'slab_1'=2,'slab_2'=2,'dom_0'=8,'dom_1'=2] {'dom_0'}, dimensions={0} | all-to-all | bytes 1179648 | tf_op jit(solution)/shard_map/all_to_all | solution.py:485
  73.5 5.7 %collective-permute-start.5 = (f32[8,384]{1,0:T(8,128)S(1)}, f32[8,384]{1,0:T(8,128)S(1)}, u32[]{:S(2)}, u32[]{:S(2)}) collective-permute-start(f32[8,384]{1,0:T(8,128)S(1)} %get-tuple-element.48), channel_id=1, source_target_pairs={{0,16},{16,0},{1,17},{17,1},{2,18},{18,2},{3,19},{19,3},{4,20},{20... | collective-permute-start | bytes 36872 | tf_op jit(solution)/shard_map/ppermute | solution.py:418
  79.2 0.6 collective-permute-start.6
  79.7 5.0 %shard_map.92.part_ref = f32[8,1536]{1,0:T(8,128)S(1)} custom-call(s32[256]{0:T(256)} %bitcast.23, s32[256]{0:T(256)} %bitcast.27, f32[1152,128]{1,0:T(8,128)S(1)} %bitcast.16, bf16[256,96,128]{2,1,0:T(8,128)(2,1)} %get-tuple-element.36.k_any), custom_call_target="tpu_custom_call" | custom-call | tf_op jit(solution)/shard_map/pallas_call | solution.py:389
  84.7 0.0 collective-permute-done.5.near_ref
  84.7 0.0 collective-permute-done.6.far_ref
  84.7 0.9 shard_map.93
  85.6 5.3 %collective-permute-start.7 = (f32[8,384]{1,0:T(8,128)S(1)}, f32[8,384]{1,0:T(8,128)S(1)}, u32[]{:S(2)}, u32[]{:S(2)}) collective-permute-start(f32[8,384]{1,0:T(8,128)S(1)} %get-tuple-element.51), channel_id=1, source_target_pairs={{0,16},{16,0},{1,17},{17,1},{2,18},{18,2},{3,19},{19,3},{4,20},{20... | collective-permute-start | bytes 36872 | tf_op jit(solution)/shard_map/ppermute | solution.py:418
  91.0 0.0 collective-permute-start.8
  91.0 6.4 %shard_map.94 = f32[1152,128]{1,0:T(8,128)S(1)} custom-call(s32[256]{0:T(256)} %bitcast.24, s32[256]{0:T(256)} %bitcast.28, f32[8,1536]{1,0:T(8,128)S(1)} %get-tuple-element.50.v_ref.w_ref, bf16[256,96,128]{2,1,0:T(8,128)(2,1)} %get-tuple-element.36.k_any), custom_call_target="tpu_custom_call" | custom-call | tf_op jit(solution)/shard_map/pallas_call | solution.py:389
  97.4 0.0 collective-permute-done.7.near_ref
  97.4 0.0 collective-permute-done.8.far_ref
  97.4 21.8 %all_to_all.27.y_ref = f32[8,144,128]{2,1,0:T(8,128)S(1)} all-to-all(f32[8,144,128]{2,1,0:T(8,128)S(1)} %bitcast.18), channel_id=1, replica_groups=mesh['slab_0'=4,'slab_1'=2,'slab_2'=2,'dom_0'=8,'dom_1'=2] {'dom_0'}, dimensions={0} | all-to-all | bytes 1179648 | tf_op jit(solution)/shard_map/all_to_all | solution.py:469
  119.2 1.0 shard_map.95.a_ref
  120.2 2.7 %collective-permute-start.9 = (f32[152,128]{1,0:T(8,128)S(1)}, f32[152,128]{1,0:T(8,128)S(1)}, u32[]{:S(2)}, u32[]{:S(2)}) collective-permute-start(f32[152,128]{1,0:T(8,128)S(1)} %shard_map.95.a_ref), channel_id=1, source_target_pairs={{0,1},{1,0},{2,3},{3,2},{4,5},{5,4},{6,7},{7,6},{8,9},{9,8},{10,11... | collective-permute-start | bytes 233480 | tf_op jit(solution)/shard_map/ppermute | solution.py:477
  122.9 2.1 %collective-permute-done.9.b_ref = f32[152,128]{1,0:T(8,128)S(1)} collective-permute-done((f32[152,128]{1,0:T(8,128)S(1)}, f32[152,128]{1,0:T(8,128)S(1)}, u32[]{:S(2)}, u32[]{:S(2)}) %collective-permute-start.9) | collective-permute-done | bytes 77856 | tf_op jit(solution)/shard_map/ppermute | solution.py:477
  125.0 1.0 shard_map.96
  126.0 19.9 %all_to_all.28 = f32[8,152,128]{2,1,0:T(8,128)S(1)} all-to-all(f32[8,152,128]{2,1,0:T(8,128)S(1)} %get-tuple-element.57), channel_id=1, replica_groups=mesh['slab_0'=4,'slab_1'=2,'slab_2'=2,'dom_0'=8,'dom_1'=2] {'dom_0'}, dimensions={0} | all-to-all | bytes 1245184 | tf_op jit(solution)/shard_map/all_to_all | solution.py:485
  145.9 0.6 broadcast_in_dim.2
  146.5 6.4 %all-to-all-start.4 = ((f32[16,8,128]{2,1,0:T(8,128)}), f32[16,8,128]{2,1,0:T(8,128)S(1)}, u32[]{:S(2)}, u32[]{:S(2)}) async-start(f32[16,8,128]{2,1,0:T(8,128)} %broadcast_in_dim.2), calls=%async_computation.4 | async-start | bytes 131072 | tf_op jit(solution)/shard_map/all_to_all | solution.py:518
  152.9 0.2 collective-permute-start.10
  153.1 1.5 collective-permute-start.11
  154.7 5.0 %shard_map.97.part_ref = f32[8,1536]{1,0:T(8,128)S(1)} custom-call(s32[256]{0:T(256)} %bitcast.25, s32[256]{0:T(256)} %bitcast.29, f32[1216,128]{1,0:T(8,128)S(1)} %bitcast.15, bf16[256,96,128]{2,1,0:T(8,128)(2,1)} %get-tuple-element.36.k_any), custom_call_target="tpu_custom_call" | custom-call | tf_op jit(solution)/shard_map/pallas_call | solution.py:389
  159.7 0.0 collective-permute-done.10.near_ref
  159.7 0.0 collective-permute-done.11.far_ref
  159.7 0.0 all-to-all-done.4.sums_ref
  159.7 1.6 %shard_map.98 = (f32[6,1,1536]{2,1,0:T(1,128)}, f32[6,1,1536]{2,1,0:T(1,128)}) custom-call(s32[2]{0:T(128)S(1)} %pad_add_fusion.at_ref, f32[16,8,128]{2,1,0:T(8,128)S(1)} %all-to-all-done.4.sums_ref, f32[6,1,1536]{2,1,0:T(1,128)} %rhs_ref.5, f32[1,1536]{1,0:T(1,128)} %shift_ref.5, f32[8,1536]{1,0:T(8,128)S(1)} %get-tuple-element.35.v_ref, ...), custom_call_target="tpu_custom_call" | custom-call | tf_op jit(solution)/shard_map/pallas_call | solution.py:389
  (2 shorter events, 0.0 us)
Async XLA Ops:
  1.8 15.1 %collective-permute-start.1 = (f32[8,384]{1,0:T(8,128)S(1)}, f32[8,384]{1,0:T(8,128)S(1)}, u32[]{:S(2)}, u32[]{:S(2)}) collective-permute-start(f32[8,384]{1,0:T(8,128)S(1)} %get-tuple-element.64), channel_id=1, source_target_pairs={{0,240},{16,32},{32,16},{48,64},{64,48},{80,96},{96,80},{112,128},... | collective-permute-start | bytes 36872 | tf_op jit(solution)/shard_map/ppermute | solution.py:418
  4.6 12.3 %collective-permute-start = (f32[8,384]{1,0:T(8,128)S(1)}, f32[8,384]{1,0:T(8,128)S(1)}, u32[]{:S(2)}, u32[]{:S(2)}) collective-permute-start(f32[8,384]{1,0:T(8,128)S(1)} %get-tuple-element.65), channel_id=1, source_target_pairs={{0,16},{16,0},{1,17},{17,1},{2,18},{18,2},{3,19},{19,3},{4,20},{20... | collective-permute-start | bytes 36872 | tf_op jit(solution)/shard_map/ppermute | solution.py:418
  17.8 6.6 %collective-permute-start.2 = (f32[8,384]{1,0:T(8,128)S(1)}, f32[8,384]{1,0:T(8,128)S(1)}, u32[]{:S(2)}, u32[]{:S(2)}) collective-permute-start(f32[8,384]{1,0:T(8,128)S(1)} %get-tuple-element.37), channel_id=1, source_target_pairs={{0,16},{16,0},{1,17},{17,1},{2,18},{18,2},{3,19},{19,3},{4,20},{20... | collective-permute-start | bytes 36872 | tf_op jit(solution)/shard_map/ppermute | solution.py:418
  17.9 6.6 %collective-permute-start.3 = (f32[8,384]{1,0:T(8,128)S(1)}, f32[8,384]{1,0:T(8,128)S(1)}, u32[]{:S(2)}, u32[]{:S(2)}) collective-permute-start(f32[8,384]{1,0:T(8,128)S(1)} %get-tuple-element.38), channel_id=1, source_target_pairs={{0,240},{16,32},{32,16},{48,64},{64,48},{80,96},{96,80},{112,128},... | collective-permute-start | bytes 36872 | tf_op jit(solution)/shard_map/ppermute | solution.py:418
  50.5 4.8 %collective-permute-start.4 = (f32[144,128]{1,0:T(8,128)S(1)}, f32[144,128]{1,0:T(8,128)S(1)}, u32[]{:S(2)}, u32[]{:S(2)}) collective-permute-start(f32[144,128]{1,0:T(8,128)S(1)} %shard_map.90.a_ref), channel_id=1, source_target_pairs={{0,1},{1,0},{2,3},{3,2},{4,5},{5,4},{6,7},{7,6},{8,9},{9,8},{10,11... | collective-permute-start | bytes 221192 | tf_op jit(solution)/shard_map/ppermute | solution.py:477
  73.5 11.2 %collective-permute-start.5 = (f32[8,384]{1,0:T(8,128)S(1)}, f32[8,384]{1,0:T(8,128)S(1)}, u32[]{:S(2)}, u32[]{:S(2)}) collective-permute-start(f32[8,384]{1,0:T(8,128)S(1)} %get-tuple-element.48), channel_id=1, source_target_pairs={{0,16},{16,0},{1,17},{17,1},{2,18},{18,2},{3,19},{19,3},{4,20},{20... | collective-permute-start | bytes 36872 | tf_op jit(solution)/shard_map/ppermute | solution.py:418
  79.2 5.6 %collective-permute-start.6 = (f32[8,384]{1,0:T(8,128)S(1)}, f32[8,384]{1,0:T(8,128)S(1)}, u32[]{:S(2)}, u32[]{:S(2)}) collective-permute-start(f32[8,384]{1,0:T(8,128)S(1)} %get-tuple-element.49), channel_id=1, source_target_pairs={{0,240},{16,32},{32,16},{48,64},{64,48},{80,96},{96,80},{112,128},... | collective-permute-start | bytes 36872 | tf_op jit(solution)/shard_map/ppermute | solution.py:418
  85.6 11.8 %collective-permute-start.7 = (f32[8,384]{1,0:T(8,128)S(1)}, f32[8,384]{1,0:T(8,128)S(1)}, u32[]{:S(2)}, u32[]{:S(2)}) collective-permute-start(f32[8,384]{1,0:T(8,128)S(1)} %get-tuple-element.51), channel_id=1, source_target_pairs={{0,16},{16,0},{1,17},{17,1},{2,18},{18,2},{3,19},{19,3},{4,20},{20... | collective-permute-start | bytes 36872 | tf_op jit(solution)/shard_map/ppermute | solution.py:418
  91.0 6.5 %collective-permute-start.8 = (f32[8,384]{1,0:T(8,128)S(1)}, f32[8,384]{1,0:T(8,128)S(1)}, u32[]{:S(2)}, u32[]{:S(2)}) collective-permute-start(f32[8,384]{1,0:T(8,128)S(1)} %get-tuple-element.52), channel_id=1, source_target_pairs={{0,240},{16,32},{32,16},{48,64},{64,48},{80,96},{96,80},{112,128},... | collective-permute-start | bytes 36872 | tf_op jit(solution)/shard_map/ppermute | solution.py:418
  120.2 4.8 %collective-permute-start.9 = (f32[152,128]{1,0:T(8,128)S(1)}, f32[152,128]{1,0:T(8,128)S(1)}, u32[]{:S(2)}, u32[]{:S(2)}) collective-permute-start(f32[152,128]{1,0:T(8,128)S(1)} %shard_map.95.a_ref), channel_id=1, source_target_pairs={{0,1},{1,0},{2,3},{3,2},{4,5},{5,4},{6,7},{7,6},{8,9},{9,8},{10,11... | collective-permute-start | bytes 233480 | tf_op jit(solution)/shard_map/ppermute | solution.py:477
  146.5 13.2 %all-to-all-start.4 = ((f32[16,8,128]{2,1,0:T(8,128)}), f32[16,8,128]{2,1,0:T(8,128)S(1)}, u32[]{:S(2)}, u32[]{:S(2)}) async-start(f32[16,8,128]{2,1,0:T(8,128)} %broadcast_in_dim.2), calls=%async_computation.4 | async-start | bytes 131072 | tf_op jit(solution)/shard_map/all_to_all | solution.py:518
  152.9 6.8 %collective-permute-start.10 = (f32[8,384]{1,0:T(8,128)S(1)}, f32[8,384]{1,0:T(8,128)S(1)}, u32[]{:S(2)}, u32[]{:S(2)}) collective-permute-start(f32[8,384]{1,0:T(8,128)S(1)} %get-tuple-element.62), channel_id=1, source_target_pairs={{0,16},{16,0},{1,17},{17,1},{2,18},{18,2},{3,19},{19,3},{4,20},{20... | collective-permute-start | bytes 36872 | tf_op jit(solution)/shard_map/ppermute | solution.py:418
  153.1 6.5 %collective-permute-start.11 = (f32[8,384]{1,0:T(8,128)S(1)}, f32[8,384]{1,0:T(8,128)S(1)}, u32[]{:S(2)}, u32[]{:S(2)}) collective-permute-start(f32[8,384]{1,0:T(8,128)S(1)} %get-tuple-element.63), channel_id=1, source_target_pairs={{0,240},{16,32},{32,16},{48,64},{64,48},{80,96},{96,80},{112,128},... | collective-permute-start | bytes 36872 | tf_op jit(solution)/shard_map/ppermute | solution.py:418

commit v4 on v2

--- a/solution.py
+++ b/solution.py
@@ -91,34 +91,44 @@
             sq_ref[k, :, t * LANES : (t + 1) * LANES] = tile
 
 
-def stiff_prep(col_ref, x_ref, k_ref, diag_ref, held, acc):
-    step = pl.program_id(0)
-
-    @pl.when(step == 0)
-    def _():
-        acc[...] = jnp.zeros_like(acc)
-
-    for half in range(GROUP // 16):
-        for t in range(CHUNK):
-            held[t * 16 : (t + 1) * 16, :] = x_ref[
-                half * 16 : (half + 1) * 16, t * LANES : (t + 1) * LANES
-            ].astype(F32)
-        for e in range(16):
-            whole = block_of(held, e, 48)
-            k_ref[half * 16 + e] = whole.astype(BF16)
-            total = jnp.sum((whole * whole).reshape(12, 8, LANES), axis=0)
-            j = col_ref[step * GROUP + half * 16 + e]
-            acc[j] = acc[j] + total
-
-    @pl.when(step == STEPS - 1)
-    def _():
-        for q in range(OWN // 4):
-            sums = [
-                jnp.broadcast_to(jnp.sum(acc[q * 4 + i], axis=0, keepdims=True), (8, LANES))
-                for i in range(4)
-            ]
-            for t, tile in enumerate(packed(*sums)):
-                diag_ref[:, tile_at(q * 3 + t)] = tile
+def stiff_prep(col_ref, x_any, k_any, diag_ref, x_ref, k_ref, held, acc, came, left):
+    def arriving(g):
+        return pltpu.make_async_copy(x_any.at[part(g)], x_ref.at[part(g)], came.at[g])
+
+    def leaving(g):
+        return pltpu.make_async_copy(k_ref.at[part(g)], k_any.at[part(g)], left.at[g])
+
+    for g in range(STEPS):
+        arriving(g).start()
+    acc[...] = jnp.zeros_like(acc)
+
+    def group(g, carry):
+        arriving(g).wait()
+        for half in range(GROUP // 16):
+            base = g * GROUP + half * 16
+            for t in range(CHUNK):
+                held[t * 16 : (t + 1) * 16, :] = x_ref[
+                    pl.ds(pl.multiple_of(base, 16), 16), tile_at(t)
+                ].astype(F32)
+            for e in range(16):
+                whole = block_of(held, e, 48)
+                k_ref[base + e] = whole.astype(BF16)
+                total = jnp.sum((whole * whole).reshape(12, 8, LANES), axis=0)
+                j = col_ref[base + e]
+                acc[j] = acc[j] + total
+        leaving(g).start()
+        return carry
+
+    lax.fori_loop(0, STEPS, group, 0)
+    for q in range(OWN // 4):
+        sums = [
+            jnp.broadcast_to(jnp.sum(acc[q * 4 + i], axis=0, keepdims=True), (8, LANES))
+            for i in range(4)
+        ]
+        for t, tile in enumerate(packed(*sums)):
+            diag_ref[:, tile_at(q * 3 + t)] = tile
+    for g in range(STEPS):
+        leaving(g).wait()
 
 
 def tile_at(t):
@@ -129,13 +139,17 @@
     return pl.ds(g * GROUP, GROUP)
 
 
+def brought(k_any, k_ref, sems, g):
+    return pltpu.make_async_copy(k_any.at[part(g)], k_ref.at[part(g), pl.ds(0, BLOCK)], sems.at[g])
+
+
 def fetch(k_any, k_ref, sems):
     for g in range(STEPS):
-        pltpu.make_async_copy(k_any.at[part(g)], k_ref.at[part(g)], sems.at[g]).start()
+        brought(k_any, k_ref, sems, g).start()
 
 
 def fetched(k_any, k_ref, sems, g):
-    pltpu.make_async_copy(k_any.at[part(g)], k_ref.at[part(g)], sems.at[g]).wait()
+    brought(k_any, k_ref, sems, g).wait()
 
 
 def forward(col_ref, row_ref, tiles, k_ref, out_ref, cols, acc, wait=None):
@@ -150,12 +164,15 @@
             wait(g)
         for first in range(0, GROUP, 8):
             terms = []
-            for e in range(first, first + 8):
-                x = cols[col_ref[base + e]]
+            for e in range(first, first + 8, 2):
+                x = jnp.concatenate([cols[col_ref[base + e]], cols[col_ref[base + e + 1]]], axis=0)
+                two = k_ref[pl.ds(base + e, 2)].reshape(2 * LANES, LANES)
                 out = lax.dot_general(
-                    x, k_ref[base + e], (((1,), (1,)), ((), ())), preferred_element_type=F32
+                    x, two, (((1,), (1,)), ((), ())), preferred_element_type=F32
                 )
-                terms.append(out[:8] + out[8:])
+                terms.append(out[:8, :BLOCK] + out[8:16, :BLOCK])
+                other = slice(LANES, LANES + BLOCK)
+                terms.append(out[16:24, other] + out[24:, other])
             for e in range(first, first + 8):
                 r = row_ref[base + e]
                 acc[r, :, :BLOCK] = acc[r, :, :BLOCK] + terms[e - first]
@@ -169,9 +186,9 @@
 
 
 def adjoint(col_ref, row_ref, y_ref, k_ref, rows, acc, wait):
-    depth = y_ref.shape[0] // (OWN // 2)
+    depth = y_ref.shape[0] // (SLAB_ROWS // OWN)
     for g in range(SLAB_ROWS // 4):
-        at = (g // 8) * depth + (g // 4 % 2) * CHUNK + (g % 4) * 3 * CASES
+        at = (g // 4) * depth + (g % 4) * 3 * CASES
         tiles = [eight(y_ref, at + t * CASES) for t in range(3)]
         for i, v in enumerate(spread(*tiles)):
             rows[g * 4 + i] = halves(v)
@@ -182,10 +199,12 @@
         wait(g)
         for first in range(0, GROUP, 8):
             terms = []
-            for e in range(first, first + 8):
-                y = rows[row_ref[base + e]]
-                out = jnp.dot(y[:, :BLOCK], k_ref[base + e], preferred_element_type=F32)
-                terms.append(out[:8] + out[8:])
+            for e in range(first, first + 8, 2):
+                y = jnp.concatenate([rows[row_ref[base + e]], rows[row_ref[base + e + 1]]], axis=0)
+                two = jnp.concatenate([k_ref[base + e, :BLOCK], k_ref[base + e + 1, :BLOCK]], axis=1)
+                out = jnp.dot(y[:, :BLOCK], two, preferred_element_type=F32)
+                terms.append(out[:8, :LANES] + out[8:16, :LANES])
+                terms.append(out[16:24, LANES:] + out[24:, LANES:])
             for e in range(first, first + 8):
                 j = col_ref[base + e]
                 acc[j] = acc[j] + terms[e - first]
@@ -217,7 +236,7 @@
     out_ref, inverse_ref, v_ref, near_out, far_out, held, cols, acc, k_ref, sems,
 ):
     fetch(k_any, k_ref, sems)
-    core = at_ref[1]
+    core = at_ref[0]
     held[...] = jnp.zeros_like(held)
     for c in range(CASES):
         held[c : c + 1, :] = rhs_ref[c]
@@ -265,7 +284,7 @@
     k_ref, sems,
 ):
     fetch(k_any, k_ref, sems)
-    core = at_ref[1]
+    core = at_ref[0]
     wait = functools.partial(fetched, k_any, k_ref, sems)
     tiles = adjoint(col_ref, row_ref, y_ref, k_ref, rows, acc, wait)
     tiles = image_tiles(core, tiles, v_ref, shift_ref, near_ref, far_ref)
@@ -296,20 +315,17 @@
     fetch(k_any, k_ref, sems)
     wait = functools.partial(fetched, k_any, k_ref, sems)
     tiles = adjoint(col_ref, row_ref, y_ref, k_ref, rows, acc, wait)
-    for t, tile in enumerate(image_tiles(at_ref[1], tiles, v_ref, shift_ref, near_ref, far_ref)):
+    for t, tile in enumerate(image_tiles(at_ref[0], tiles, v_ref, shift_ref, near_ref, far_ref)):
         image_ref[:, tile_at(t)] = tile
 
 
-def summed(at_ref, live_ref, y_ref, near_ref, far_ref, k_ref, *rest):
-    out_ref = rest[-1]
-    half = at_ref[0]
+def settled(at_ref, live_ref, y_ref, near_ref, far_ref, k_ref, *rest):
+    out_ref, near_out, far_out, held = rest[-4:]
     whole = y_ref[0]
-    for z in range(1, y_ref.shape[0]):
-        whole = whole + y_ref[z]
-    out_ref[: 2 * CHUNK, :] = whole
-    if len(rest) > 1:
-        out_ref[2 * CHUNK :, :] = rest[0][...]
-    for k, face in enumerate(both_sides(at_ref[1], near_ref, far_ref)):
+    for d in range(1, y_ref.shape[0]):
+        whole = whole + y_ref[d]
+    held[...] = whole
+    for k, face in enumerate(both_sides(at_ref[0], near_ref, far_ref)):
         terms = []
         for i, v in enumerate(spread(*face)):
             out = lax.dot_general(
@@ -319,25 +335,19 @@
             term = jnp.where(rows_live((8, BLOCK), 1, live_ref[k], i), term, 0.0)
             terms.append(jnp.concatenate([term, jnp.zeros((8, LANES - BLOCK), F32)], axis=1))
         for t, tile in enumerate(packed(*terms)):
-            for h in range(2):
-                at = h * CHUNK + (k * 9 + t) * CASES
-                added = jnp.where(half == h, tile[:CASES], 0.0)
-                out_ref[at : at + CASES, :] = out_ref[at : at + CASES, :] + added
-
-
-def finished(at_ref, live_ref, a_ref, b_ref, k_ref, out_ref, near_out, far_out, held):
-    half = at_ref[0]
-    both = a_ref[...] + b_ref[...]
-    if both.shape[0] > 2 * CHUNK:
+            at = (k * 9 + t) * CASES
+            held[at : at + CASES, :] = held[at : at + CASES, :] + tile[:CASES]
+    own = held[...]
+    for d in range(out_ref.shape[0]):
+        out_ref[d, :CHUNK] = own
+    if len(rest) > 4:
         square = jnp.zeros((8, LANES), F32)
-        for t in range(2 * TILES):
-            tile = eight(a_ref, t * CASES) + eight(b_ref, t * CASES)
+        for t in range(TILES):
+            tile = eight(held, t * CASES)
             square = square + tile * tile
-        sums = both[2 * CHUNK :] + placed_sums([(3, square)])
-        both = jnp.concatenate([both[: 2 * CHUNK], sums], axis=0)
-    for z in range(out_ref.shape[0]):
-        out_ref[z] = both
-    held[...] = jnp.where(half == 0, both[:CHUNK], both[CHUNK : 2 * CHUNK])
+        sums = rest[0][...] + placed_sums([(3, square)])
+        for d in range(out_ref.shape[0]):
+            out_ref[d, CHUNK:] = sums
     backs = []
     for k in range(2):
         tiles = [eight(held, (k * 9 + t) * CASES) for t in range(3)]
@@ -348,7 +358,7 @@
             out = jnp.dot(y[:, :BLOCK], k_ref[k * FACE + i], preferred_element_type=F32)
             terms.append(out[:8] + out[8:])
         backs.append(packed(*terms))
-    send_sides(at_ref[1], backs[0], backs[1], near_out, far_out)
+    send_sides(at_ref[0], backs[0], backs[1], near_out, far_out)
 
 
 def combined(sums_ref, rhs_ref, v_ref, image_ref, w_ref, second_ref, sol_ref, res_ref):
@@ -405,8 +415,8 @@
     rhs = in_hbm(rhs.reshape(CASES, 1, span))
     dshift = in_hbm(dshift)
     core = lax.axis_index("slab_2")
-    place = jnp.stack([lax.axis_index("dom_1"), core]).astype(jnp.int32)
-    z_count = lax.axis_size("dom_0")
+    place = core.astype(jnp.int32).reshape(1)
+    domains = lax.axis_size(DOM)
     slabs = lax.axis_size(SLAB)
     swap = [(0, 1), (1, 0)]
     across = [(s, (s - 1 if s % 2 == 0 else s + 1) % slabs) for s in range(slabs)]
@@ -427,23 +437,21 @@
         jnp.where(core == 0, face_sq[1], face_sq[0]), jnp.where(core == 0, face_sq[0], face_sq[1])
     )
 
+    hbm = pl.BlockSpec(memory_space=pltpu.HBM)
     blocks, inner = pl.pallas_call(
         stiff_prep,
-        grid_spec=pltpu.PrefetchScalarGridSpec(
-            num_scalar_prefetch=1,
-            grid=(STEPS,),
-            in_specs=[pl.BlockSpec((GROUP, BLOCK * BLOCK), lambda i, *_: (i, 0))],
-            out_specs=(
-                pl.BlockSpec((GROUP, BLOCK, LANES), lambda i, *_: (i, 0, 0)),
-                pl.BlockSpec((8, span), lambda i, *_: (0, 0)),
-            ),
-            scratch_shapes=[
-                pltpu.VMEM((CHUNK * 16, LANES), F32),
-                pltpu.VMEM((OWN, 8, LANES), F32),
-            ],
-        ),
+        in_specs=[SMEM, hbm],
+        out_specs=(hbm, VMEM),
         out_shape=(pltpu.HBM((STORED, BLOCK, LANES), BF16), vector),
-        compiler_params=pltpu.CompilerParams(vmem_limit_bytes=16 * MIB),
+        scratch_shapes=[
+            pltpu.VMEM((STORED, BLOCK * BLOCK), BF16),
+            pltpu.VMEM((STORED, BLOCK, LANES), BF16),
+            pltpu.VMEM((CHUNK * 16, LANES), F32),
+            pltpu.VMEM((OWN, 8, LANES), F32),
+            pltpu.SemaphoreType.DMA((STEPS,)),
+            pltpu.SemaphoreType.DMA((STEPS,)),
+        ],
+        compiler_params=pltpu.CompilerParams(vmem_limit_bytes=20 * MIB),
     )(columns, in_hbm(stiff[0]))
     blocks = in_hbm(blocks)
 
@@ -451,28 +459,21 @@
     cols = pltpu.VMEM((OWN, 16, LANES), BF16)
     rows = pltpu.VMEM((SLAB_ROWS, 16, LANES), BF16)
     acc = pltpu.VMEM((SLAB_ROWS, 8, LANES), F32)
-    stored = [pltpu.VMEM((STORED, BLOCK, LANES), BF16), pltpu.SemaphoreType.DMA((STEPS,))]
+    stored = [pltpu.VMEM((STORED, LANES, LANES), BF16), pltpu.SemaphoreType.DMA((STEPS,))]
 
     def all_rows(parts, near, far, sums=()):
         near, far = exchanged(near, far)
-        parts = parts.reshape(z_count, 2 * CHUNK, LANES)
-        arrived = lax.all_to_all(parts, "dom_0", 0, 0, tiled=True)
-        depth = 2 * CHUNK + 8 * len(sums)
-        (mine,) = call(
-            summed,
+        parts = parts.reshape(domains, CHUNK, LANES)
+        arrived = lax.all_to_all(parts, DOM, 0, 0, tiled=True)
+        depth = CHUNK + 8 * len(sums)
+        copies, near, far = call(
+            settled,
             [place, live],
             [arrived, near, far, faces, *sums],
-            [shaped(depth, LANES)],
-        )
-        other = lax.ppermute(mine, "dom_1", swap)
-        copies, near, far = call(
-            finished,
-            [place, live],
-            [mine, other, faces],
-            [shaped(z_count, depth, LANES), face, face],
+            [shaped(domains, depth, LANES), face, face],
             [pltpu.VMEM((CHUNK, LANES), F32)],
         )
-        full = lax.all_to_all(copies, "dom_0", 0, 0, tiled=True)
+        full = lax.all_to_all(copies, DOM, 0, 0, tiled=True)
         near, far = exchanged(near, far)
         return full, near, far
 
@@ -495,7 +496,7 @@
     )
     full, near, far = all_rows(parts, near, far, [sums])
     full, near, far = lax.optimization_barrier((full, near, far))
-    sums = jnp.sum(full[:, 2 * CHUNK :], axis=0)
+    sums = jnp.sum(full[:, CHUNK:], axis=0)
     sums = lax.all_to_all(
         jnp.broadcast_to(sums[None], (slabs, *sums.shape)), SLAB, 0, 0, tiled=True
     )

time: 156 us -> 149 us (0.955)
  waiting for transfers between devices: 68.5 us -> 62.7 us
  Pallas kernels: 41.4 us -> 36.1 us
  starting transfers between devices: 43.7 us -> 47.5 us
    ppermute x2 -> x0, starting transfers between devices: 5.35 us -> none  [all_rows(): other = lax.ppermute(mine, 'dom_1', swap)]
    ppermute x2 -> x0, waiting for transfers between devices: 4.21 us -> none  [all_rows(): other = lax.ppermute(mine, 'dom_1', swap)]
    all_to_all x4, starting transfers between devices: 18.8 us -> 22.9 us  [the longest x2 15 us: all_rows(): arrived = lax.all_to_all(parts, DOM, 0, 0, tiled=True)]
    all_to_all x1, starting transfers between devices: 6.76 us -> 10.6 us  [body(): lax.all_to_all(jnp.broadcast_to(sums[None], (slabs, *sums.shape)), SLAB,...]
    pallas_call x9 -> x7, Pallas kernels: 31.1 us -> 28.1 us  [call(): pl.pallas_call(kernel, in_specs=[SMEM] * len(scalars) + [VMEM] * held + [...]
    pallas_call x1, Pallas kernels: 10.2 us -> 7.98 us  [body(): pl.pallas_call(stiff_prep, in_specs=[SMEM, hbm], out_specs=(hbm, VMEM), o...]
    all_to_all x4, waiting for transfers between devices: 50.5 us -> 48.8 us  [the longest x2 26.9 us: all_rows(): arrived = lax.all_to_all(parts, DOM, 0, 0, tiled=True)]
  transfers between devices with their start and end apart: 17 -> 15, of which waited for: 15 -> 13; matrix products, arithmetic and copies ran while one was open for 0% -> 0% of each run, Pallas kernels for 10% -> 8%
where the time goes in v4:
time: 149 us; the launch traced here: 148 us
  waiting for transfers between devices  62.7 us (42%)
  starting transfers between devices  47.5 us (32%)
  Pallas kernels  36.1 us (24%)
    pallas_call x7, Pallas kernels, call(): pl.pallas_call(kernel, in_specs=[SMEM] * len(scalars) + [VMEM] * held + [...  28.1 us
    all_to_all x2, waiting for transfers between devices, all_rows(): arrived = lax.all_to_all(parts, DOM, 0, 0, tiled=True)  26.9 us
    all_to_all x2, waiting for transfers between devices, all_rows(): full = lax.all_to_all(copies, DOM, 0, 0, tiled=True)  21.9 us
    all_to_all x2, starting transfers between devices, all_rows(): arrived = lax.all_to_all(parts, DOM, 0, 0, tiled=True)  15 us
    ppermute x10, starting transfers between devices, exchanged(): return (lax.ppermute(near, 'slab_2', swap), lax.ppermute(far, SLAB, across))  14 us
    ppermute x10, waiting for transfers between devices, exchanged(): return (lax.ppermute(near, 'slab_2', swap), lax.ppermute(far, SLAB, across))  12.7 us
    all_to_all x1, starting transfers between devices, body(): lax.all_to_all(jnp.broadcast_to(sums[None], (slabs, *sums.shape)), SLAB,...  10.6 us
    pallas_call x1, Pallas kernels, body(): pl.pallas_call(stiff_prep, in_specs=[SMEM, hbm], out_specs=(hbm, VMEM), o...  7.98 us
  transfers between devices with their start and end apart: 15, of which 13 were waited for; matrix products, arithmetic and copies ran while one was open for 0% of the time, Pallas kernels for 8%

profile of v4, /device:TPU:1, one launch (start us, length us, event | category | flops | bytes accessed | tf_op | source)
XLA Modules:
  0.0 147.8 jit_solution(16153139319339233933)
XLA Ops:
  0.6 1.2 shard_map.87
  1.8 2.8 %collective-permute-start.1 = (f32[8,384]{1,0:T(8,128)S(1)}, f32[8,384]{1,0:T(8,128)S(1)}, u32[]{:S(2)}, u32[]{:S(2)}) collective-permute-start(f32[8,384]{1,0:T(8,128)S(1)} %get-tuple-element.50), channel_id=1, source_target_pairs={{0,240},{16,32},{32,16},{48,64},{64,48},{80,96},{96,80},{112,128},... | collective-permute-start | bytes 36872 | tf_op jit(solution)/shard_map/ppermute | solution.py:427
  4.6 2.0 %collective-permute-start = (f32[8,384]{1,0:T(8,128)S(1)}, f32[8,384]{1,0:T(8,128)S(1)}, u32[]{:S(2)}, u32[]{:S(2)}) collective-permute-start(f32[8,384]{1,0:T(8,128)S(1)} %get-tuple-element.51), channel_id=1, source_target_pairs={{0,16},{16,0},{1,17},{17,1},{2,18},{18,2},{3,19},{19,3},{4,20},{20... | collective-permute-start | bytes 36872 | tf_op jit(solution)/shard_map/ppermute | solution.py:427
  6.6 8.0 %shard_map.86 = (bf16[256,96,128]{2,1,0:T(8,128)(2,1)}, f32[8,1536]{1,0:T(8,128)S(1)}) custom-call(s32[256]{0:T(256)} %bitcast.18, bf16[256,9216]{1,0:T(8,128)(2,1)} %bitcast.16), custom_call_target="tpu_custom_call" | custom-call | tf_op jit(solution)/shard_map/pallas_call | solution.py:441
  14.6 0.0 collective-permute-done.1.far_ref
  14.7 0.0 collective-permute-done.near_ref
  14.7 6.9 %shard_map.88 = (f32[1152,128]{1,0:T(8,128)}, f32[8,1536]{1,0:T(8,128)S(1)}, f32[8,1536]{1,0:T(8,128)S(1)}, f32[8,384]{1,0:T(8,128)S(1)}, f32[8,384]{1,0:T(8,128)S(1)}) custom-call(s32[256]{0:T(256)} %bitcast.19, s32[256]{0:T(256)} %bitcast.22, s32[1]{0:T(128)} %bitcast.at_ref, f32[6,1,1536]{2,1,0:T(1,128)} %rhs_ref.5, f32[1,1536]{1,0:T(1,128)} %shift_ref.5, ...), custom_call_target="tpu_custom_call" | custom-call | tf_op jit(solution)/shard_map/pallas_call | solution.py:398
  21.6 10.6 %all-to-all-start = ((f32[16,72,128]{2,1,0:T(8,128)}), f32[16,72,128]{2,1,0:T(8,128)S(1)}, u32[]{:S(2)}, u32[]{:S(2)}) async-start(f32[16,72,128]{2,1,0:T(8,128)} %bitcast.8), calls=%async_computation | async-start | bytes 1179648 | tf_op jit(solution)/shard_map/all_to_all | solution.py:467
  32.2 0.4 collective-permute-start.2
  32.6 0.0 collective-permute-start.3
  32.6 0.9 collective-permute-done.2.near_ref
  33.5 2.2 %collective-permute-done.3.far_ref = f32[8,384]{1,0:T(8,128)S(1)} collective-permute-done((f32[8,384]{1,0:T(8,128)S(1)}, f32[8,384]{1,0:T(8,128)S(1)}, u32[]{:S(2)}, u32[]{:S(2)}) %collective-permute-start.3) | collective-permute-done | bytes 12320 | tf_op jit(solution)/shard_map/ppermute | solution.py:427
  35.7 15.6 %all-to-all-done.y_ref = f32[16,72,128]{2,1,0:T(8,128)S(1)} async-done(((f32[16,72,128]{2,1,0:T(8,128)}), f32[16,72,128]{2,1,0:T(8,128)S(1)}, u32[]{:S(2)}, u32[]{:S(2)}) %all-to-all-start) | async-done | bytes 589856 | tf_op jit(solution)/shard_map/all_to_all | solution.py:467
  51.3 2.1 %shard_map.89 = (f32[16,72,128]{2,1,0:T(8,128)}, f32[8,384]{1,0:T(8,128)S(1)}, f32[8,384]{1,0:T(8,128)S(1)}) custom-call(s32[1]{0:T(128)} %bitcast.at_ref, s32[2]{0:T(128)} %bitcast.26, f32[16,72,128]{2,1,0:T(8,128)S(1)} %all-to-all-done.y_ref, f32[8,384]{1,0:T(8,128)S(1)} %collective-permute-done.2.near_ref, f32[8,384]{1,0:T(8,128)S(1)} %collective-permute-done.3.far_ref, ...), custom_call_target="tpu_custom_call" | custom-call | tf_op jit(solution)/shard_map/pallas_call | solution.py:398
  53.3 4.3 %all-to-all-start.1 = ((f32[16,72,128]{2,1,0:T(8,128)}), f32[16,72,128]{2,1,0:T(8,128)S(1)}, u32[]{:S(2)}, u32[]{:S(2)}) async-start(f32[16,72,128]{2,1,0:T(8,128)} %get-tuple-element.33), calls=%async_computation.1 | async-start | bytes 1179648 | tf_op jit(solution)/shard_map/all_to_all | solution.py:476
  57.6 2.0 %collective-permute-start.4 = (f32[8,384]{1,0:T(8,128)S(1)}, f32[8,384]{1,0:T(8,128)S(1)}, u32[]{:S(2)}, u32[]{:S(2)}) collective-permute-start(f32[8,384]{1,0:T(8,128)S(1)} %get-tuple-element.36), channel_id=1, source_target_pairs={{0,16},{16,0},{1,17},{17,1},{2,18},{18,2},{3,19},{19,3},{4,20},{20... | collective-permute-start | bytes 36872 | tf_op jit(solution)/shard_map/ppermute | solution.py:427
  59.7 0.0 collective-permute-start.5
  59.7 0.8 collective-permute-done.4.near_ref
  60.5 2.3 %collective-permute-done.5.far_ref = f32[8,384]{1,0:T(8,128)S(1)} collective-permute-done((f32[8,384]{1,0:T(8,128)S(1)}, f32[8,384]{1,0:T(8,128)S(1)}, u32[]{:S(2)}, u32[]{:S(2)}) %collective-permute-start.5) | collective-permute-done | bytes 12320 | tf_op jit(solution)/shard_map/ppermute | solution.py:427
  62.8 12.6 %all-to-all-done.1 = f32[16,72,128]{2,1,0:T(8,128)S(1)} async-done(((f32[16,72,128]{2,1,0:T(8,128)}), f32[16,72,128]{2,1,0:T(8,128)S(1)}, u32[]{:S(2)}, u32[]{:S(2)}) %all-to-all-start.1) | async-done | bytes 589856 | tf_op jit(solution)/shard_map/all_to_all | solution.py:476
  75.4 9.8 %shard_map.90 = (f32[1152,128]{1,0:T(8,128)}, f32[8,1536]{1,0:T(8,128)S(1)}, f32[8,1536]{1,0:T(8,128)S(1)}, f32[8,128]{1,0:T(8,128)S(1)}, f32[8,384]{1,0:T(8,128)S(1)}, /*index=5*/f32[8,384]{1,0:T(8,128)S(1)}) custom-call(s32[256]{0:T(256)} %bitcast.20, s32[256]{0:T(256)} %bitcast.23, s32[1]{0:T(128)} %bitcast.at_ref, f32[1152,128]{1,0:T(8,128)S(1)} %bitcast.15, ...), custom_call_target="tpu_custom_call" | custom-call | tf_op jit(solution)/shard_map/pallas_call | solution.py:398
  85.2 4.4 %all-to-all-start.2 = ((f32[16,72,128]{2,1,0:T(8,128)}), f32[16,72,128]{2,1,0:T(8,128)S(1)}, u32[]{:S(2)}, u32[]{:S(2)}) async-start(f32[16,72,128]{2,1,0:T(8,128)} %bitcast.10), calls=%async_computation.2 | async-start | bytes 1179648 | tf_op jit(solution)/shard_map/all_to_all | solution.py:467
  89.6 2.9 %collective-permute-start.6 = (f32[8,384]{1,0:T(8,128)S(1)}, f32[8,384]{1,0:T(8,128)S(1)}, u32[]{:S(2)}, u32[]{:S(2)}) collective-permute-start(f32[8,384]{1,0:T(8,128)S(1)} %get-tuple-element.39), channel_id=1, source_target_pairs={{0,16},{16,0},{1,17},{17,1},{2,18},{18,2},{3,19},{19,3},{4,20},{20... | collective-permute-start | bytes 36872 | tf_op jit(solution)/shard_map/ppermute | solution.py:427
  92.5 0.0 collective-permute-start.7
  92.5 0.8 collective-permute-done.6.near_ref
  93.3 2.5 %collective-permute-done.7.far_ref = f32[8,384]{1,0:T(8,128)S(1)} collective-permute-done((f32[8,384]{1,0:T(8,128)S(1)}, f32[8,384]{1,0:T(8,128)S(1)}, u32[]{:S(2)}, u32[]{:S(2)}) %collective-permute-start.7) | collective-permute-done | bytes 12320 | tf_op jit(solution)/shard_map/ppermute | solution.py:427
  95.8 11.3 %all-to-all-done.2.y_ref = f32[16,72,128]{2,1,0:T(8,128)S(1)} async-done(((f32[16,72,128]{2,1,0:T(8,128)}), f32[16,72,128]{2,1,0:T(8,128)S(1)}, u32[]{:S(2)}, u32[]{:S(2)}) %all-to-all-start.2) | async-done | bytes 589856 | tf_op jit(solution)/shard_map/all_to_all | solution.py:467
  107.1 2.0 %shard_map.91 = (f32[16,80,128]{2,1,0:T(8,128)}, f32[8,384]{1,0:T(8,128)S(1)}, f32[8,384]{1,0:T(8,128)S(1)}) custom-call(s32[1]{0:T(128)} %bitcast.at_ref, s32[2]{0:T(128)} %bitcast.27, f32[16,72,128]{2,1,0:T(8,128)S(1)} %all-to-all-done.2.y_ref, f32[8,384]{1,0:T(8,128)S(1)} %collective-permute-done.6.near_ref, f32[8,384]{1,0:T(8,128)S(1)} %collective-permute-done.7.far_ref, ...), custom_call_target="tpu_custom_call" | custom-call | tf_op jit(solution)/shard_map/pallas_call | solution.py:398
  109.1 3.6 %all-to-all-start.3 = ((f32[16,80,128]{2,1,0:T(8,128)}), f32[16,80,128]{2,1,0:T(8,128)S(1)}, u32[]{:S(2)}, u32[]{:S(2)}) async-start(f32[16,80,128]{2,1,0:T(8,128)} %get-tuple-element.42), calls=%async_computation.3 | async-start | bytes 1310720 | tf_op jit(solution)/shard_map/all_to_all | solution.py:476
  112.7 4.0 %collective-permute-start.8 = (f32[8,384]{1,0:T(8,128)S(1)}, f32[8,384]{1,0:T(8,128)S(1)}, u32[]{:S(2)}, u32[]{:S(2)}) collective-permute-start(f32[8,384]{1,0:T(8,128)S(1)} %get-tuple-element.43), channel_id=1, source_target_pairs={{0,16},{16,0},{1,17},{17,1},{2,18},{18,2},{3,19},{19,3},{4,20},{20... | collective-permute-start | bytes 36872 | tf_op jit(solution)/shard_map/ppermute | solution.py:427
  116.6 0.0 collective-permute-start.9
  116.6 0.8 collective-permute-done.8.near_ref
  117.5 2.3 %collective-permute-done.9.far_ref = f32[8,384]{1,0:T(8,128)S(1)} collective-permute-done((f32[8,384]{1,0:T(8,128)S(1)}, f32[8,384]{1,0:T(8,128)S(1)}, u32[]{:S(2)}, u32[]{:S(2)}) %collective-permute-start.9) | collective-permute-done | bytes 12320 | tf_op jit(solution)/shard_map/ppermute | solution.py:427
  119.7 9.3 %all-to-all-done.3 = f32[16,80,128]{2,1,0:T(8,128)S(1)} async-done(((f32[16,80,128]{2,1,0:T(8,128)}), f32[16,80,128]{2,1,0:T(8,128)S(1)}, u32[]{:S(2)}, u32[]{:S(2)}) %all-to-all-start.3) | async-done | bytes 655392 | tf_op jit(solution)/shard_map/all_to_all | solution.py:476
  129.1 0.6 broadcast_in_dim.2
  129.7 10.6 %all-to-all-start.4 = ((f32[16,8,128]{2,1,0:T(8,128)}), f32[16,8,128]{2,1,0:T(8,128)S(1)}, u32[]{:S(2)}, u32[]{:S(2)}) async-start(f32[16,8,128]{2,1,0:T(8,128)} %broadcast_in_dim.2), calls=%async_computation.4 | async-start | bytes 131072 | tf_op jit(solution)/shard_map/all_to_all | solution.py:500
  140.3 4.6 %shard_map.92.second_ref = f32[8,1536]{1,0:T(8,128)S(1)} custom-call(s32[256]{0:T(256)} %bitcast.21, s32[256]{0:T(256)} %bitcast.24, s32[1]{0:T(128)} %bitcast.at_ref, f32[1280,128]{1,0:T(8,128)S(1)} %bitcast.14, f32[1,1536]{1,0:T(1,128)} %shift_ref.5, f32[8,1536]{1,0:T(8,128)S(1)} %get-tuple-element.47.v_ref.w_ref, ...), custom_call_target="tpu_custom_call" | custom-call | tf_op jit(solution)/shard_map/pallas_call | solution.py:398
  144.9 1.3 all-to-all-done.4.sums_ref
  146.2 1.6 %shard_map.93 = (f32[6,1,1536]{2,1,0:T(1,128)}, f32[6,1,1536]{2,1,0:T(1,128)}) custom-call(f32[16,8,128]{2,1,0:T(8,128)S(1)} %all-to-all-done.4.sums_ref, f32[6,1,1536]{2,1,0:T(1,128)} %rhs_ref.5, f32[8,1536]{1,0:T(8,128)S(1)} %get-tuple-element.35.v_ref, f32[8,1536]{1,0:T(8,128)S(1)} %get-tuple-element.46.image_ref, ...), custom_call_target="tpu_custom_call" | custom-call | tf_op jit(solution)/shard_map/pallas_call | solution.py:398
  (2 shorter events, 0.0 us)
Async XLA Ops:
  1.8 12.8 %collective-permute-start.1 = (f32[8,384]{1,0:T(8,128)S(1)}, f32[8,384]{1,0:T(8,128)S(1)}, u32[]{:S(2)}, u32[]{:S(2)}) collective-permute-start(f32[8,384]{1,0:T(8,128)S(1)} %get-tuple-element.50), channel_id=1, source_target_pairs={{0,240},{16,32},{32,16},{48,64},{64,48},{80,96},{96,80},{112,128},... | collective-permute-start | bytes 36872 | tf_op jit(solution)/shard_map/ppermute | solution.py:427
  4.6 10.0 %collective-permute-start = (f32[8,384]{1,0:T(8,128)S(1)}, f32[8,384]{1,0:T(8,128)S(1)}, u32[]{:S(2)}, u32[]{:S(2)}) collective-permute-start(f32[8,384]{1,0:T(8,128)S(1)} %get-tuple-element.51), channel_id=1, source_target_pairs={{0,16},{16,0},{1,17},{17,1},{2,18},{18,2},{3,19},{19,3},{4,20},{20... | collective-permute-start | bytes 36872 | tf_op jit(solution)/shard_map/ppermute | solution.py:427
  21.6 29.7 %all-to-all-start = ((f32[16,72,128]{2,1,0:T(8,128)}), f32[16,72,128]{2,1,0:T(8,128)S(1)}, u32[]{:S(2)}, u32[]{:S(2)}) async-start(f32[16,72,128]{2,1,0:T(8,128)} %bitcast.8), calls=%async_computation | async-start | bytes 1179648 | tf_op jit(solution)/shard_map/all_to_all | solution.py:467
  32.2 1.3 collective-permute-start.2
  32.6 3.1 %collective-permute-start.3 = (f32[8,384]{1,0:T(8,128)S(1)}, f32[8,384]{1,0:T(8,128)S(1)}, u32[]{:S(2)}, u32[]{:S(2)}) collective-permute-start(f32[8,384]{1,0:T(8,128)S(1)} %get-tuple-element.31), channel_id=1, source_target_pairs={{0,240},{16,32},{32,16},{48,64},{64,48},{80,96},{96,80},{112,128},... | collective-permute-start | bytes 36872 | tf_op jit(solution)/shard_map/ppermute | solution.py:427
  53.3 22.1 %all-to-all-start.1 = ((f32[16,72,128]{2,1,0:T(8,128)}), f32[16,72,128]{2,1,0:T(8,128)S(1)}, u32[]{:S(2)}, u32[]{:S(2)}) async-start(f32[16,72,128]{2,1,0:T(8,128)} %get-tuple-element.33), calls=%async_computation.1 | async-start | bytes 1179648 | tf_op jit(solution)/shard_map/all_to_all | solution.py:476
  57.6 2.9 %collective-permute-start.4 = (f32[8,384]{1,0:T(8,128)S(1)}, f32[8,384]{1,0:T(8,128)S(1)}, u32[]{:S(2)}, u32[]{:S(2)}) collective-permute-start(f32[8,384]{1,0:T(8,128)S(1)} %get-tuple-element.36), channel_id=1, source_target_pairs={{0,16},{16,0},{1,17},{17,1},{2,18},{18,2},{3,19},{19,3},{4,20},{20... | collective-permute-start | bytes 36872 | tf_op jit(solution)/shard_map/ppermute | solution.py:427
  59.7 3.2 %collective-permute-start.5 = (f32[8,384]{1,0:T(8,128)S(1)}, f32[8,384]{1,0:T(8,128)S(1)}, u32[]{:S(2)}, u32[]{:S(2)}) collective-permute-start(f32[8,384]{1,0:T(8,128)S(1)} %get-tuple-element.37), channel_id=1, source_target_pairs={{0,240},{16,32},{32,16},{48,64},{64,48},{80,96},{96,80},{112,128},... | collective-permute-start | bytes 36872 | tf_op jit(solution)/shard_map/ppermute | solution.py:427
  85.2 21.9 %all-to-all-start.2 = ((f32[16,72,128]{2,1,0:T(8,128)}), f32[16,72,128]{2,1,0:T(8,128)S(1)}, u32[]{:S(2)}, u32[]{:S(2)}) async-start(f32[16,72,128]{2,1,0:T(8,128)} %bitcast.10), calls=%async_computation.2 | async-start | bytes 1179648 | tf_op jit(solution)/shard_map/all_to_all | solution.py:467
  89.6 3.7 %collective-permute-start.6 = (f32[8,384]{1,0:T(8,128)S(1)}, f32[8,384]{1,0:T(8,128)S(1)}, u32[]{:S(2)}, u32[]{:S(2)}) collective-permute-start(f32[8,384]{1,0:T(8,128)S(1)} %get-tuple-element.39), channel_id=1, source_target_pairs={{0,16},{16,0},{1,17},{17,1},{2,18},{18,2},{3,19},{19,3},{4,20},{20... | collective-permute-start | bytes 36872 | tf_op jit(solution)/shard_map/ppermute | solution.py:427
  92.5 3.3 %collective-permute-start.7 = (f32[8,384]{1,0:T(8,128)S(1)}, f32[8,384]{1,0:T(8,128)S(1)}, u32[]{:S(2)}, u32[]{:S(2)}) collective-permute-start(f32[8,384]{1,0:T(8,128)S(1)} %get-tuple-element.40), channel_id=1, source_target_pairs={{0,240},{16,32},{32,16},{48,64},{64,48},{80,96},{96,80},{112,128},... | collective-permute-start | bytes 36872 | tf_op jit(solution)/shard_map/ppermute | solution.py:427
  109.1 20.0 %all-to-all-start.3 = ((f32[16,80,128]{2,1,0:T(8,128)}), f32[16,80,128]{2,1,0:T(8,128)S(1)}, u32[]{:S(2)}, u32[]{:S(2)}) async-start(f32[16,80,128]{2,1,0:T(8,128)} %get-tuple-element.42), calls=%async_computation.3 | async-start | bytes 1310720 | tf_op jit(solution)/shard_map/all_to_all | solution.py:476
  112.7 4.8 %collective-permute-start.8 = (f32[8,384]{1,0:T(8,128)S(1)}, f32[8,384]{1,0:T(8,128)S(1)}, u32[]{:S(2)}, u32[]{:S(2)}) collective-permute-start(f32[8,384]{1,0:T(8,128)S(1)} %get-tuple-element.43), channel_id=1, source_target_pairs={{0,16},{16,0},{1,17},{17,1},{2,18},{18,2},{3,19},{19,3},{4,20},{20... | collective-permute-start | bytes 36872 | tf_op jit(solution)/shard_map/ppermute | solution.py:427
  116.6 3.1 %collective-permute-start.9 = (f32[8,384]{1,0:T(8,128)S(1)}, f32[8,384]{1,0:T(8,128)S(1)}, u32[]{:S(2)}, u32[]{:S(2)}) collective-permute-start(f32[8,384]{1,0:T(8,128)S(1)} %get-tuple-element.44), channel_id=1, source_target_pairs={{0,240},{16,32},{32,16},{48,64},{64,48},{80,96},{96,80},{112,128},... | collective-permute-start | bytes 36872 | tf_op jit(solution)/shard_map/ppermute | solution.py:427
  129.7 16.4 %all-to-all-start.4 = ((f32[16,8,128]{2,1,0:T(8,128)}), f32[16,8,128]{2,1,0:T(8,128)S(1)}, u32[]{:S(2)}, u32[]{:S(2)}) async-start(f32[16,8,128]{2,1,0:T(8,128)} %broadcast_in_dim.2), calls=%async_computation.4 | async-start | bytes 131072 | tf_op jit(solution)/shard_map/all_to_all | solution.py:500

commit v5 on v4

--- a/solution.py
+++ b/solution.py
@@ -279,33 +279,36 @@
 
 
 def middle_product(
-    col_ref, row_ref, at_ref, y_ref, rhs_ref, shift_ref, inverse_ref, v_ref, near_ref, far_ref,
-    k_any, out_ref, image_ref, w_ref, sums_ref, near_out, far_out, held, rows, cols, acc,
-    k_ref, sems,
+    col_ref, row_ref, at_ref, y_ref, shift_ref, inverse_ref, v_ref, near_ref, far_ref, k_any,
+    out_ref, image_ref, w_ref, near_out, far_out, rows, cols, acc, k_ref, sems,
 ):
     fetch(k_any, k_ref, sems)
     core = at_ref[0]
     wait = functools.partial(fetched, k_any, k_ref, sems)
     tiles = adjoint(col_ref, row_ref, y_ref, k_ref, rows, acc, wait)
     tiles = image_tiles(core, tiles, v_ref, shift_ref, near_ref, far_ref)
-    held[...] = jnp.zeros_like(held)
-    for c in range(CASES):
-        held[c : c + 1, :] = rhs_ref[c]
-    sums = [jnp.zeros((8, LANES), F32) for _ in range(4)]
     second = []
     for t, image in enumerate(tiles):
         image_ref[:, tile_at(t)] = image
         w = inverse_ref[:, tile_at(t)] * image
         w_ref[:, tile_at(t)] = w
         second.append(w)
-        v = v_ref[:, tile_at(t)]
-        sums[0] = sums[0] + held[:, tile_at(t)] * v
+    send_sides(core, second[:3], second[9:], near_out, far_out)
+    forward(col_ref, row_ref, second, k_ref, out_ref, cols, acc)
+
+
+def inner_products(rhs_ref, shift_ref, v_ref, image_ref, w_ref, sums_ref, held_ref):
+    held_ref[...] = jnp.zeros_like(held_ref)
+    for c in range(CASES):
+        held_ref[c : c + 1, :] = rhs_ref[c]
+    sums = [jnp.zeros((8, LANES), F32) for _ in range(4)]
+    for t in range(TILES):
+        v, w, image = (ref[:, tile_at(t)] for ref in (v_ref, w_ref, image_ref))
+        sums[0] = sums[0] + held_ref[:, tile_at(t)] * v
         sums[1] = sums[1] + v * image
         sums[2] = sums[2] + image * w
         sums[3] = sums[3] + shift_ref[:, tile_at(t)] * w * w
     sums_ref[...] = placed_sums(enumerate(sums))
-    send_sides(core, second[:3], second[9:], near_out, far_out)
-    forward(col_ref, row_ref, second, k_ref, out_ref, cols, acc)
 
 
 def last_product(
@@ -319,12 +322,7 @@
         image_ref[:, tile_at(t)] = tile
 
 
-def settled(at_ref, live_ref, y_ref, near_ref, far_ref, k_ref, *rest):
-    out_ref, near_out, far_out, held = rest[-4:]
-    whole = y_ref[0]
-    for d in range(1, y_ref.shape[0]):
-        whole = whole + y_ref[d]
-    held[...] = whole
+def face_terms(at_ref, live_ref, near_ref, far_ref, k_ref, out_ref):
     for k, face in enumerate(both_sides(at_ref[0], near_ref, far_ref)):
         terms = []
         for i, v in enumerate(spread(*face)):
@@ -335,22 +333,37 @@
             term = jnp.where(rows_live((8, BLOCK), 1, live_ref[k], i), term, 0.0)
             terms.append(jnp.concatenate([term, jnp.zeros((8, LANES - BLOCK), F32)], axis=1))
         for t, tile in enumerate(packed(*terms)):
+            out_ref[k, :, tile_at(t)] = tile
+
+
+def settled(y_ref, terms_ref, *rest):
+    out_ref, own_ref = rest[-2:]
+    whole = y_ref[0]
+    for d in range(1, y_ref.shape[0]):
+        whole = whole + y_ref[d]
+    own_ref[...] = whole
+    for k in range(2):
+        for t in range(3):
             at = (k * 9 + t) * CASES
-            held[at : at + CASES, :] = held[at : at + CASES, :] + tile[:CASES]
-    own = held[...]
+            term = terms_ref[k, :, tile_at(t)]
+            own_ref[at : at + CASES, :] = own_ref[at : at + CASES, :] + term[:CASES]
+    own = own_ref[...]
     for d in range(out_ref.shape[0]):
         out_ref[d, :CHUNK] = own
-    if len(rest) > 4:
+    if len(rest) > 2:
         square = jnp.zeros((8, LANES), F32)
         for t in range(TILES):
-            tile = eight(held, t * CASES)
+            tile = eight(own_ref, t * CASES)
             square = square + tile * tile
         sums = rest[0][...] + placed_sums([(3, square)])
         for d in range(out_ref.shape[0]):
             out_ref[d, CHUNK:] = sums
+
+
+def back_faces(at_ref, live_ref, own_ref, k_ref, near_out, far_out):
     backs = []
     for k in range(2):
-        tiles = [eight(held, (k * 9 + t) * CASES) for t in range(3)]
+        tiles = [eight(own_ref, (k * 9 + t) * CASES) for t in range(3)]
         terms = []
         for i, v in enumerate(spread(*tiles)):
             v = jnp.where(rows_live((8, LANES), 1, live_ref[k], i), v, 0.0)
@@ -378,7 +391,7 @@
     change = on_second * second_ref[:CASES, :] - on_first * image_ref[:CASES, :]
     for c in range(CASES):
         sol_ref[c] = sol[c : c + 1]
-        res_ref[c] = rhs_ref[c] + change[c : c + 1]
+        res_ref[c] = rhs_ref[c : c + 1, :] + change[c : c + 1]
 
 
 SMEM = pl.BlockSpec(memory_space=pltpu.SMEM)
@@ -466,14 +479,15 @@
         parts = parts.reshape(domains, CHUNK, LANES)
         arrived = lax.all_to_all(parts, DOM, 0, 0, tiled=True)
         depth = CHUNK + 8 * len(sums)
-        copies, near, far = call(
+        (terms,) = call(face_terms, [place, live], [near, far, faces], [shaped(2, 8, face_len)])
+        copies, own = call(
             settled,
-            [place, live],
-            [arrived, near, far, faces, *sums],
-            [shaped(domains, depth, LANES), face, face],
-            [pltpu.VMEM((CHUNK, LANES), F32)],
+            [],
+            [arrived, terms, *sums],
+            [shaped(domains, depth, LANES), shaped(CHUNK, LANES)],
         )
         full = lax.all_to_all(copies, DOM, 0, 0, tiled=True)
+        near, far = call(back_faces, [place, live], [own, faces], [face, face])
         near, far = exchanged(near, far)
         return full, near, far
 
@@ -486,13 +500,16 @@
         stays=1,
     )
     full, near, far = all_rows(parts, near, far)
-    parts, image, second, sums, near, far = call(
+    parts, image, second, near, far = call(
         middle_product,
         [columns, targets, place],
-        [full.reshape(-1, LANES), rhs, dshift, inverse, first, near, far, blocks],
-        [shaped(OWN * CHUNK, LANES), vector, vector, shaped(8, LANES), face, face],
-        [held, rows, cols, acc, *stored],
+        [full.reshape(-1, LANES), dshift, inverse, first, near, far, blocks],
+        [shaped(OWN * CHUNK, LANES), vector, vector, face, face],
+        [rows, cols, acc, *stored],
         stays=1,
+    )
+    sums, whole_rhs = call(
+        inner_products, [], [rhs, dshift, first, image, second], [shaped(8, LANES), vector]
     )
     full, near, far = all_rows(parts, near, far, [sums])
     full, near, far = lax.optimization_barrier((full, near, far))
@@ -509,7 +526,7 @@
         stays=1,
     )
     out = shaped(CASES, 1, span)
-    return call(combined, [], [sums, rhs, first, image, second, second_image], [out, out])
+    return call(combined, [], [sums, whole_rhs, first, image, second, second_image], [out, out])
 
 
 def solution(mesh):

time: 149 us -> 146 us (0.980)
  waiting for transfers between devices: 62.7 us -> 58 us
  Pallas kernels: 36.1 us -> 37.7 us
    all_to_all x2, waiting for transfers between devices: 21.9 us -> 19.5 us  [all_rows(): full = lax.all_to_all(copies, DOM, 0, 0, tiled=True)]
    all_to_all x2, waiting for transfers between devices: 26.9 us -> 24.9 us  [all_rows(): arrived = lax.all_to_all(parts, DOM, 0, 0, tiled=True)]
    pallas_call x7 -> x12, Pallas kernels: 28.1 us -> 29.8 us  [call(): pl.pallas_call(kernel, in_specs=[SMEM] * len(scalars) + [VMEM] * held + [...]
  transfers between devices with their start and end apart: 15 -> 15, of which waited for: 13 -> 12; matrix products, arithmetic and copies ran while one was open for 0% -> 0% of each run, Pallas kernels for 8% -> 12%
where the time goes in v5:
time: 146 us; the launch traced here: 145 us
  waiting for transfers between devices  58 us (40%)
  starting transfers between devices  47.7 us (33%)
  Pallas kernels  37.7 us (26%)
    pallas_call x12, Pallas kernels, call(): pl.pallas_call(kernel, in_specs=[SMEM] * len(scalars) + [VMEM] * held + [...  29.8 us
    all_to_all x2, waiting for transfers between devices, all_rows(): arrived = lax.all_to_all(parts, DOM, 0, 0, tiled=True)  24.9 us
    all_to_all x2, waiting for transfers between devices, all_rows(): full = lax.all_to_all(copies, DOM, 0, 0, tiled=True)  19.5 us
    all_to_all x2, starting transfers between devices, all_rows(): arrived = lax.all_to_all(parts, DOM, 0, 0, tiled=True)  15 us
    ppermute x10, starting transfers between devices, exchanged(): return (lax.ppermute(near, 'slab_2', swap), lax.ppermute(far, SLAB, across))  14 us
    ppermute x10, waiting for transfers between devices, exchanged(): return (lax.ppermute(near, 'slab_2', swap), lax.ppermute(far, SLAB, across))  12.4 us
    all_to_all x1, starting transfers between devices, body(): lax.all_to_all(jnp.broadcast_to(sums[None], (slabs, *sums.shape)), SLAB,...  10.8 us
    pallas_call x1, Pallas kernels, body(): pl.pallas_call(stiff_prep, in_specs=[SMEM, hbm], out_specs=(hbm, VMEM), o...  7.97 us
  transfers between devices with their start and end apart: 15, of which 12 were waited for; matrix products, arithmetic and copies ran while one was open for 0% of the time, Pallas kernels for 12%

profile of v5, /device:TPU:1, one launch (start us, length us, event | category | flops | bytes accessed | tf_op | source)
XLA Modules:
  0.0 144.9 jit_solution(5736888180054933089)
XLA Ops:
  0.6 1.2 shard_map.87
  1.8 2.8 %collective-permute-start.1 = (f32[8,384]{1,0:T(8,128)S(1)}, f32[8,384]{1,0:T(8,128)S(1)}, u32[]{:S(2)}, u32[]{:S(2)}) collective-permute-start(f32[8,384]{1,0:T(8,128)S(1)} %get-tuple-element.56), channel_id=1, source_target_pairs={{0,240},{16,32},{32,16},{48,64},{64,48},{80,96},{96,80},{112,128},... | collective-permute-start | bytes 36872 | tf_op jit(solution)/shard_map/ppermute | solution.py:440
  4.6 2.0 %collective-permute-start = (f32[8,384]{1,0:T(8,128)S(1)}, f32[8,384]{1,0:T(8,128)S(1)}, u32[]{:S(2)}, u32[]{:S(2)}) collective-permute-start(f32[8,384]{1,0:T(8,128)S(1)} %get-tuple-element.57), channel_id=1, source_target_pairs={{0,16},{16,0},{1,17},{17,1},{2,18},{18,2},{3,19},{19,3},{4,20},{20... | collective-permute-start | bytes 36872 | tf_op jit(solution)/shard_map/ppermute | solution.py:440
  6.6 8.0 %shard_map.86 = (bf16[256,96,128]{2,1,0:T(8,128)(2,1)}, f32[8,1536]{1,0:T(8,128)S(1)}) custom-call(s32[256]{0:T(256)} %bitcast.18, bf16[256,9216]{1,0:T(8,128)(2,1)} %bitcast.16), custom_call_target="tpu_custom_call" | custom-call | tf_op jit(solution)/shard_map/pallas_call | solution.py:454
  14.6 0.0 collective-permute-done.1.far_ref
  14.6 0.0 collective-permute-done.near_ref
  14.7 6.9 %shard_map.88 = (f32[1152,128]{1,0:T(8,128)}, f32[8,1536]{1,0:T(8,128)S(1)}, f32[8,1536]{1,0:T(8,128)S(1)}, f32[8,384]{1,0:T(8,128)S(1)}, f32[8,384]{1,0:T(8,128)S(1)}) custom-call(s32[256]{0:T(256)} %bitcast.19, s32[256]{0:T(256)} %bitcast.27, s32[1]{0:T(128)} %bitcast.2.at_ref, f32[6,1,1536]{2,1,0:T(1,128)} %rhs_ref.3, f32[1,1536]{1,0:T(1,128)} %shift_ref.7, ...), custom_call_target="tpu_custom_call" | custom-call | tf_op jit(solution)/shard_map/pallas_call | solution.py:411
  21.6 10.6 %all-to-all-start = ((f32[16,72,128]{2,1,0:T(8,128)}), f32[16,72,128]{2,1,0:T(8,128)S(1)}, u32[]{:S(2)}, u32[]{:S(2)}) async-start(f32[16,72,128]{2,1,0:T(8,128)} %bitcast.8), calls=%async_computation | async-start | bytes 1179648 | tf_op jit(solution)/shard_map/all_to_all | solution.py:480
  32.2 0.4 collective-permute-start.2
  32.6 0.0 collective-permute-start.3
  32.6 0.9 collective-permute-done.2.near_ref
  33.5 2.2 %collective-permute-done.3.far_ref = f32[8,384]{1,0:T(8,128)S(1)} collective-permute-done((f32[8,384]{1,0:T(8,128)S(1)}, f32[8,384]{1,0:T(8,128)S(1)}, u32[]{:S(2)}, u32[]{:S(2)}) %collective-permute-start.3) | collective-permute-done | bytes 12320 | tf_op jit(solution)/shard_map/ppermute | solution.py:440
  35.7 1.0 shard_map.89.terms_ref
  36.7 14.6 %all-to-all-done.y_ref = f32[16,72,128]{2,1,0:T(8,128)S(1)} async-done(((f32[16,72,128]{2,1,0:T(8,128)}), f32[16,72,128]{2,1,0:T(8,128)S(1)}, u32[]{:S(2)}, u32[]{:S(2)}) %all-to-all-start) | async-done | bytes 589856 | tf_op jit(solution)/shard_map/all_to_all | solution.py:480
  51.3 0.9 shard_map.90
  52.2 4.3 %all-to-all-start.1 = ((f32[16,72,128]{2,1,0:T(8,128)}), f32[16,72,128]{2,1,0:T(8,128)S(1)}, u32[]{:S(2)}, u32[]{:S(2)}) async-start(f32[16,72,128]{2,1,0:T(8,128)} %get-tuple-element.36), calls=%async_computation.1 | async-start | bytes 1179648 | tf_op jit(solution)/shard_map/all_to_all | solution.py:489
  56.5 0.9 shard_map.91
  57.4 2.0 %collective-permute-start.4 = (f32[8,384]{1,0:T(8,128)S(1)}, f32[8,384]{1,0:T(8,128)S(1)}, u32[]{:S(2)}, u32[]{:S(2)}) collective-permute-start(f32[8,384]{1,0:T(8,128)S(1)} %get-tuple-element.40), channel_id=1, source_target_pairs={{0,16},{16,0},{1,17},{17,1},{2,18},{18,2},{3,19},{19,3},{4,20},{20... | collective-permute-start | bytes 36872 | tf_op jit(solution)/shard_map/ppermute | solution.py:440
  59.5 0.0 collective-permute-start.5
  59.5 0.8 collective-permute-done.4.near_ref
  60.3 2.6 %collective-permute-done.5.far_ref = f32[8,384]{1,0:T(8,128)S(1)} collective-permute-done((f32[8,384]{1,0:T(8,128)S(1)}, f32[8,384]{1,0:T(8,128)S(1)}, u32[]{:S(2)}, u32[]{:S(2)}) %collective-permute-start.5) | collective-permute-done | bytes 12320 | tf_op jit(solution)/shard_map/ppermute | solution.py:440
  62.9 11.4 %all-to-all-done.1 = f32[16,72,128]{2,1,0:T(8,128)S(1)} async-done(((f32[16,72,128]{2,1,0:T(8,128)}), f32[16,72,128]{2,1,0:T(8,128)S(1)}, u32[]{:S(2)}, u32[]{:S(2)}) %all-to-all-start.1) | async-done | bytes 589856 | tf_op jit(solution)/shard_map/all_to_all | solution.py:489
  74.3 9.6 %shard_map.92 = (f32[1152,128]{1,0:T(8,128)}, f32[8,1536]{1,0:T(8,128)S(1)}, f32[8,1536]{1,0:T(8,128)S(1)}, f32[8,384]{1,0:T(8,128)S(1)}, f32[8,384]{1,0:T(8,128)S(1)}) custom-call(s32[256]{0:T(256)} %bitcast.20, s32[256]{0:T(256)} %bitcast.28, s32[1]{0:T(128)} %bitcast.2.at_ref, f32[1152,128]{1,0:T(8,128)S(1)} %bitcast.15, f32[1,1536]{1,0:T(1,128)} %shift_ref.7, ...), custom_call_target="tpu_custom_call" | custom-call | tf_op jit(solution)/shard_map/pallas_call | solution.py:411
  83.9 4.4 %all-to-all-start.2 = ((f32[16,72,128]{2,1,0:T(8,128)}), f32[16,72,128]{2,1,0:T(8,128)S(1)}, u32[]{:S(2)}, u32[]{:S(2)}) async-start(f32[16,72,128]{2,1,0:T(8,128)} %bitcast.10), calls=%async_computation.2 | async-start | bytes 1179648 | tf_op jit(solution)/shard_map/all_to_all | solution.py:480
  88.3 2.8 %collective-permute-start.6 = (f32[8,384]{1,0:T(8,128)S(1)}, f32[8,384]{1,0:T(8,128)S(1)}, u32[]{:S(2)}, u32[]{:S(2)}) collective-permute-start(f32[8,384]{1,0:T(8,128)S(1)} %get-tuple-element.43), channel_id=1, source_target_pairs={{0,16},{16,0},{1,17},{17,1},{2,18},{18,2},{3,19},{19,3},{4,20},{20... | collective-permute-start | bytes 36872 | tf_op jit(solution)/shard_map/ppermute | solution.py:440
  91.1 0.0 collective-permute-start.7
  91.1 0.9 shard_map.94
  92.0 0.0 collective-permute-done.6.near_ref
  92.0 2.4 %collective-permute-done.7.far_ref = f32[8,384]{1,0:T(8,128)S(1)} collective-permute-done((f32[8,384]{1,0:T(8,128)S(1)}, f32[8,384]{1,0:T(8,128)S(1)}, u32[]{:S(2)}, u32[]{:S(2)}) %collective-permute-start.7) | collective-permute-done | bytes 12320 | tf_op jit(solution)/shard_map/ppermute | solution.py:440
  94.4 1.0 shard_map.93.terms_ref
  95.4 10.4 %all-to-all-done.2.y_ref = f32[16,72,128]{2,1,0:T(8,128)S(1)} async-done(((f32[16,72,128]{2,1,0:T(8,128)}), f32[16,72,128]{2,1,0:T(8,128)S(1)}, u32[]{:S(2)}, u32[]{:S(2)}) %all-to-all-start.2) | async-done | bytes 589856 | tf_op jit(solution)/shard_map/all_to_all | solution.py:480
  105.8 1.0 shard_map.95
  106.8 3.6 %all-to-all-start.3 = ((f32[16,80,128]{2,1,0:T(8,128)}), f32[16,80,128]{2,1,0:T(8,128)S(1)}, u32[]{:S(2)}, u32[]{:S(2)}) async-start(f32[16,80,128]{2,1,0:T(8,128)} %get-tuple-element.48), calls=%async_computation.3 | async-start | bytes 1310720 | tf_op jit(solution)/shard_map/all_to_all | solution.py:489
  110.4 0.9 shard_map.96
  111.3 4.0 %collective-permute-start.8 = (f32[8,384]{1,0:T(8,128)S(1)}, f32[8,384]{1,0:T(8,128)S(1)}, u32[]{:S(2)}, u32[]{:S(2)}) collective-permute-start(f32[8,384]{1,0:T(8,128)S(1)} %get-tuple-element.50), channel_id=1, source_target_pairs={{0,16},{16,0},{1,17},{17,1},{2,18},{18,2},{3,19},{19,3},{4,20},{20... | collective-permute-start | bytes 36872 | tf_op jit(solution)/shard_map/ppermute | solution.py:440
  115.3 0.0 collective-permute-start.9
  115.3 0.8 collective-permute-done.8.near_ref
  116.1 2.6 %collective-permute-done.9.far_ref = f32[8,384]{1,0:T(8,128)S(1)} collective-permute-done((f32[8,384]{1,0:T(8,128)S(1)}, f32[8,384]{1,0:T(8,128)S(1)}, u32[]{:S(2)}, u32[]{:S(2)}) %collective-permute-start.9) | collective-permute-done | bytes 12320 | tf_op jit(solution)/shard_map/ppermute | solution.py:440
  118.7 8.1 %all-to-all-done.3 = f32[16,80,128]{2,1,0:T(8,128)S(1)} async-done(((f32[16,80,128]{2,1,0:T(8,128)}), f32[16,80,128]{2,1,0:T(8,128)S(1)}, u32[]{:S(2)}, u32[]{:S(2)}) %all-to-all-start.3) | async-done | bytes 655392 | tf_op jit(solution)/shard_map/all_to_all | solution.py:489
  126.8 0.6 broadcast_in_dim.2
  127.4 10.8 %all-to-all-start.4 = ((f32[16,8,128]{2,1,0:T(8,128)}), f32[16,8,128]{2,1,0:T(8,128)S(1)}, u32[]{:S(2)}, u32[]{:S(2)}) async-start(f32[16,8,128]{2,1,0:T(8,128)} %broadcast_in_dim.2), calls=%async_computation.4 | async-start | bytes 131072 | tf_op jit(solution)/shard_map/all_to_all | solution.py:517
  138.2 4.6 %shard_map.97.second_ref = f32[8,1536]{1,0:T(8,128)S(1)} custom-call(s32[256]{0:T(256)} %bitcast.21, s32[256]{0:T(256)} %bitcast.29, s32[1]{0:T(128)} %bitcast.2.at_ref, f32[1280,128]{1,0:T(8,128)S(1)} %bitcast.14, f32[1,1536]{1,0:T(1,128)} %shift_ref.7, f32[8,1536]{1,0:T(8,128)S(1)} %get-tuple-element.46.w_ref.v_ref, ...), custom_call_target="tpu_custom_call" | custom-call | tf_op jit(solution)/shard_map/pallas_call | solution.py:411
  142.8 1.3 all-to-all-done.4.sums_ref
  144.1 0.8 shard_map.98
  (2 shorter events, 0.0 us)
Async XLA Ops:
  1.8 12.8 %collective-permute-start.1 = (f32[8,384]{1,0:T(8,128)S(1)}, f32[8,384]{1,0:T(8,128)S(1)}, u32[]{:S(2)}, u32[]{:S(2)}) collective-permute-start(f32[8,384]{1,0:T(8,128)S(1)} %get-tuple-element.56), channel_id=1, source_target_pairs={{0,240},{16,32},{32,16},{48,64},{64,48},{80,96},{96,80},{112,128},... | collective-permute-start | bytes 36872 | tf_op jit(solution)/shard_map/ppermute | solution.py:440
  4.6 10.0 %collective-permute-start = (f32[8,384]{1,0:T(8,128)S(1)}, f32[8,384]{1,0:T(8,128)S(1)}, u32[]{:S(2)}, u32[]{:S(2)}) collective-permute-start(f32[8,384]{1,0:T(8,128)S(1)} %get-tuple-element.57), channel_id=1, source_target_pairs={{0,16},{16,0},{1,17},{17,1},{2,18},{18,2},{3,19},{19,3},{4,20},{20... | collective-permute-start | bytes 36872 | tf_op jit(solution)/shard_map/ppermute | solution.py:440
  21.6 29.7 %all-to-all-start = ((f32[16,72,128]{2,1,0:T(8,128)}), f32[16,72,128]{2,1,0:T(8,128)S(1)}, u32[]{:S(2)}, u32[]{:S(2)}) async-start(f32[16,72,128]{2,1,0:T(8,128)} %bitcast.8), calls=%async_computation | async-start | bytes 1179648 | tf_op jit(solution)/shard_map/all_to_all | solution.py:480
  32.2 1.3 collective-permute-start.2
  32.6 3.1 %collective-permute-start.3 = (f32[8,384]{1,0:T(8,128)S(1)}, f32[8,384]{1,0:T(8,128)S(1)}, u32[]{:S(2)}, u32[]{:S(2)}) collective-permute-start(f32[8,384]{1,0:T(8,128)S(1)} %get-tuple-element.34), channel_id=1, source_target_pairs={{0,240},{16,32},{32,16},{48,64},{64,48},{80,96},{96,80},{112,128},... | collective-permute-start | bytes 36872 | tf_op jit(solution)/shard_map/ppermute | solution.py:440
  52.2 22.1 %all-to-all-start.1 = ((f32[16,72,128]{2,1,0:T(8,128)}), f32[16,72,128]{2,1,0:T(8,128)S(1)}, u32[]{:S(2)}, u32[]{:S(2)}) async-start(f32[16,72,128]{2,1,0:T(8,128)} %get-tuple-element.36), calls=%async_computation.1 | async-start | bytes 1179648 | tf_op jit(solution)/shard_map/all_to_all | solution.py:489
  57.4 2.9 %collective-permute-start.4 = (f32[8,384]{1,0:T(8,128)S(1)}, f32[8,384]{1,0:T(8,128)S(1)}, u32[]{:S(2)}, u32[]{:S(2)}) collective-permute-start(f32[8,384]{1,0:T(8,128)S(1)} %get-tuple-element.40), channel_id=1, source_target_pairs={{0,16},{16,0},{1,17},{17,1},{2,18},{18,2},{3,19},{19,3},{4,20},{20... | collective-permute-start | bytes 36872 | tf_op jit(solution)/shard_map/ppermute | solution.py:440
  59.5 3.4 %collective-permute-start.5 = (f32[8,384]{1,0:T(8,128)S(1)}, f32[8,384]{1,0:T(8,128)S(1)}, u32[]{:S(2)}, u32[]{:S(2)}) collective-permute-start(f32[8,384]{1,0:T(8,128)S(1)} %get-tuple-element.41), channel_id=1, source_target_pairs={{0,240},{16,32},{32,16},{48,64},{64,48},{80,96},{96,80},{112,128},... | collective-permute-start | bytes 36872 | tf_op jit(solution)/shard_map/ppermute | solution.py:440
  83.9 21.9 %all-to-all-start.2 = ((f32[16,72,128]{2,1,0:T(8,128)}), f32[16,72,128]{2,1,0:T(8,128)S(1)}, u32[]{:S(2)}, u32[]{:S(2)}) async-start(f32[16,72,128]{2,1,0:T(8,128)} %bitcast.10), calls=%async_computation.2 | async-start | bytes 1179648 | tf_op jit(solution)/shard_map/all_to_all | solution.py:480
  88.3 3.7 %collective-permute-start.6 = (f32[8,384]{1,0:T(8,128)S(1)}, f32[8,384]{1,0:T(8,128)S(1)}, u32[]{:S(2)}, u32[]{:S(2)}) collective-permute-start(f32[8,384]{1,0:T(8,128)S(1)} %get-tuple-element.43), channel_id=1, source_target_pairs={{0,16},{16,0},{1,17},{17,1},{2,18},{18,2},{3,19},{19,3},{4,20},{20... | collective-permute-start | bytes 36872 | tf_op jit(solution)/shard_map/ppermute | solution.py:440
  91.1 3.3 %collective-permute-start.7 = (f32[8,384]{1,0:T(8,128)S(1)}, f32[8,384]{1,0:T(8,128)S(1)}, u32[]{:S(2)}, u32[]{:S(2)}) collective-permute-start(f32[8,384]{1,0:T(8,128)S(1)} %get-tuple-element.44), channel_id=1, source_target_pairs={{0,240},{16,32},{32,16},{48,64},{64,48},{80,96},{96,80},{112,128},... | collective-permute-start | bytes 36872 | tf_op jit(solution)/shard_map/ppermute | solution.py:440
  106.8 20.0 %all-to-all-start.3 = ((f32[16,80,128]{2,1,0:T(8,128)}), f32[16,80,128]{2,1,0:T(8,128)S(1)}, u32[]{:S(2)}, u32[]{:S(2)}) async-start(f32[16,80,128]{2,1,0:T(8,128)} %get-tuple-element.48), calls=%async_computation.3 | async-start | bytes 1310720 | tf_op jit(solution)/shard_map/all_to_all | solution.py:489
  111.3 4.8 %collective-permute-start.8 = (f32[8,384]{1,0:T(8,128)S(1)}, f32[8,384]{1,0:T(8,128)S(1)}, u32[]{:S(2)}, u32[]{:S(2)}) collective-permute-start(f32[8,384]{1,0:T(8,128)S(1)} %get-tuple-element.50), channel_id=1, source_target_pairs={{0,16},{16,0},{1,17},{17,1},{2,18},{18,2},{3,19},{19,3},{4,20},{20... | collective-permute-start | bytes 36872 | tf_op jit(solution)/shard_map/ppermute | solution.py:440
  115.3 3.4 %collective-permute-start.9 = (f32[8,384]{1,0:T(8,128)S(1)}, f32[8,384]{1,0:T(8,128)S(1)}, u32[]{:S(2)}, u32[]{:S(2)}) collective-permute-start(f32[8,384]{1,0:T(8,128)S(1)} %get-tuple-element.51), channel_id=1, source_target_pairs={{0,240},{16,32},{32,16},{48,64},{64,48},{80,96},{96,80},{112,128},... | collective-permute-start | bytes 36872 | tf_op jit(solution)/shard_map/ppermute | solution.py:440
  127.4 16.7 %all-to-all-start.4 = ((f32[16,8,128]{2,1,0:T(8,128)}), f32[16,8,128]{2,1,0:T(8,128)S(1)}, u32[]{:S(2)}, u32[]{:S(2)}) async-start(f32[16,8,128]{2,1,0:T(8,128)} %broadcast_in_dim.2), calls=%async_computation.4 | async-start | bytes 131072 | tf_op jit(solution)/shard_map/all_to_all | solution.py:517

commit v6 on v5

--- a/solution.py
+++ b/solution.py
@@ -91,12 +91,14 @@
             sq_ref[k, :, t * LANES : (t + 1) * LANES] = tile
 
 
-def stiff_prep(col_ref, x_any, k_any, diag_ref, x_ref, k_ref, held, acc, came, left):
+def stiff_prep(col_ref, x_any, k_any, diag_ref, k_ref, x_ref, held, acc, came, left):
     def arriving(g):
         return pltpu.make_async_copy(x_any.at[part(g)], x_ref.at[part(g)], came.at[g])
 
     def leaving(g):
-        return pltpu.make_async_copy(k_ref.at[part(g)], k_any.at[part(g)], left.at[g])
+        return pltpu.make_async_copy(
+            k_ref.at[part(g), pl.ds(0, BLOCK)], k_any.at[part(g)], left.at[g]
+        )
 
     for g in range(STEPS):
         arriving(g).start()
@@ -112,7 +114,7 @@
                 ].astype(F32)
             for e in range(16):
                 whole = block_of(held, e, 48)
-                k_ref[base + e] = whole.astype(BF16)
+                k_ref[base + e, :BLOCK] = whole.astype(BF16)
                 total = jnp.sum((whole * whole).reshape(12, 8, LANES), axis=0)
                 j = col_ref[base + e]
                 acc[j] = acc[j] + total
@@ -232,10 +234,9 @@
 
 
 def first_product(
-    col_ref, row_ref, at_ref, rhs_ref, shift_ref, diag_ref, near_ref, far_ref, k_any,
-    out_ref, inverse_ref, v_ref, near_out, far_out, held, cols, acc, k_ref, sems,
+    col_ref, row_ref, at_ref, rhs_ref, shift_ref, diag_ref, near_ref, far_ref, k_ref,
+    out_ref, inverse_ref, v_ref, near_out, far_out, held, cols, acc,
 ):
-    fetch(k_any, k_ref, sems)
     core = at_ref[0]
     held[...] = jnp.zeros_like(held)
     for c in range(CASES):
@@ -254,8 +255,7 @@
         v_ref[:, tile_at(t)] = tile
         tiles.append(tile)
     send_sides(core, tiles[:3], tiles[9:], near_out, far_out)
-    wait = functools.partial(fetched, k_any, k_ref, sems)
-    forward(col_ref, row_ref, tiles, k_ref, out_ref, cols, acc, wait)
+    forward(col_ref, row_ref, tiles, k_ref, out_ref, cols, acc)
 
 
 def image_tiles(core, tiles, v_ref, shift_ref, near_ref, far_ref):
@@ -451,14 +451,17 @@
     )
 
     hbm = pl.BlockSpec(memory_space=pltpu.HBM)
-    blocks, inner = pl.pallas_call(
+    blocks, inner, near_blocks = pl.pallas_call(
         stiff_prep,
         in_specs=[SMEM, hbm],
-        out_specs=(hbm, VMEM),
-        out_shape=(pltpu.HBM((STORED, BLOCK, LANES), BF16), vector),
+        out_specs=(hbm, VMEM, VMEM),
+        out_shape=(
+            pltpu.HBM((STORED, BLOCK, LANES), BF16),
+            vector,
+            pltpu.VMEM((STORED, LANES, LANES), BF16),
+        ),
         scratch_shapes=[
             pltpu.VMEM((STORED, BLOCK * BLOCK), BF16),
-            pltpu.VMEM((STORED, BLOCK, LANES), BF16),
             pltpu.VMEM((CHUNK * 16, LANES), F32),
             pltpu.VMEM((OWN, 8, LANES), F32),
             pltpu.SemaphoreType.DMA((STEPS,)),
@@ -467,6 +470,7 @@
         compiler_params=pltpu.CompilerParams(vmem_limit_bytes=20 * MIB),
     )(columns, in_hbm(stiff[0]))
     blocks = in_hbm(blocks)
+    near_blocks = pltpu.with_memory_space_constraint(near_blocks, pltpu.VMEM)
 
     held = pltpu.VMEM((8, span), F32)
     cols = pltpu.VMEM((OWN, 16, LANES), BF16)
@@ -494,10 +498,9 @@
     parts, inverse, first, near, far = call(
         first_product,
         [columns, targets, place],
-        [rhs, dshift, inner, sq_near, sq_far, blocks],
+        [rhs, dshift, inner, sq_near, sq_far, near_blocks],
         [shaped(OWN * CHUNK, LANES), vector, vector, face, face],
-        [held, cols, acc, *stored],
-        stays=1,
+        [held, cols, acc],
     )
     full, near, far = all_rows(parts, near, far)
     parts, image, second, near, far = call(

time: 146 us -> 145 us (level)
  no operation moved by 1% of the time
where the time goes in v6:
time: 145 us; the launch traced here: 144 us
  waiting for transfers between devices  58.1 us (40%)
  starting transfers between devices  47.8 us (33%)
  Pallas kernels  36.6 us (25%)
    pallas_call x12, Pallas kernels, call(): pl.pallas_call(kernel, in_specs=[SMEM] * len(scalars) + [VMEM] * held + [...  28.6 us
    all_to_all x2, waiting for transfers between devices, all_rows(): arrived = lax.all_to_all(parts, DOM, 0, 0, tiled=True)  25 us
    all_to_all x2, waiting for transfers between devices, all_rows(): full = lax.all_to_all(copies, DOM, 0, 0, tiled=True)  19.4 us
    all_to_all x2, starting transfers between devices, all_rows(): arrived = lax.all_to_all(parts, DOM, 0, 0, tiled=True)  15 us
    ppermute x10, starting transfers between devices, exchanged(): return (lax.ppermute(near, 'slab_2', swap), lax.ppermute(far, SLAB, across))  14 us
    ppermute x10, waiting for transfers between devices, exchanged(): return (lax.ppermute(near, 'slab_2', swap), lax.ppermute(far, SLAB, across))  12.3 us
    all_to_all x1, starting transfers between devices, body(): lax.all_to_all(jnp.broadcast_to(sums[None], (slabs, *sums.shape)), SLAB,...  10.8 us
    pallas_call x1, Pallas kernels, body(): pl.pallas_call(stiff_prep, in_specs=[SMEM, hbm], out_specs=(hbm, VMEM, VM...  7.99 us
  transfers between devices with their start and end apart: 15, of which 12 were waited for; matrix products, arithmetic and copies ran while one was open for 0% of the time, Pallas kernels for 12%

profile of v6, /device:TPU:1, one launch (start us, length us, event | category | flops | bytes accessed | tf_op | source)
XLA Modules:
  0.0 143.8 jit_solution(1286393885083342470)
XLA Ops:
  0.6 1.2 shard_map.87
  1.8 2.8 %collective-permute-start.1 = (f32[8,384]{1,0:T(8,128)S(1)}, f32[8,384]{1,0:T(8,128)S(1)}, u32[]{:S(2)}, u32[]{:S(2)}) collective-permute-start(f32[8,384]{1,0:T(8,128)S(1)} %get-tuple-element.58), channel_id=1, source_target_pairs={{0,240},{16,32},{32,16},{48,64},{64,48},{80,96},{96,80},{112,128},... | collective-permute-start | bytes 36872 | tf_op jit(solution)/shard_map/ppermute | solution.py:440
  4.6 2.0 %collective-permute-start = (f32[8,384]{1,0:T(8,128)S(1)}, f32[8,384]{1,0:T(8,128)S(1)}, u32[]{:S(2)}, u32[]{:S(2)}) collective-permute-start(f32[8,384]{1,0:T(8,128)S(1)} %get-tuple-element.59), channel_id=1, source_target_pairs={{0,16},{16,0},{1,17},{17,1},{2,18},{18,2},{3,19},{19,3},{4,20},{20... | collective-permute-start | bytes 36872 | tf_op jit(solution)/shard_map/ppermute | solution.py:440
  6.6 8.0 %shard_map.86 = (bf16[256,96,128]{2,1,0:T(8,128)(2,1)}, f32[8,1536]{1,0:T(8,128)S(1)}, bf16[256,128,128]{2,1,0:T(8,128)(2,1)S(1)}) custom-call(s32[256]{0:T(256)} %bitcast.18, bf16[256,9216]{1,0:T(8,128)(2,1)} %bitcast.16), custom_call_target="tpu_custom_call" | custom-call | tf_op jit(solution)/shard_map/pallas_call | solution.py:454
  14.6 0.0 collective-permute-done.1.far_ref
  14.7 0.0 collective-permute-done.near_ref
  14.7 5.8 %shard_map.88 = (f32[1152,128]{1,0:T(8,128)}, f32[8,1536]{1,0:T(8,128)S(1)}, f32[8,1536]{1,0:T(8,128)S(1)}, f32[8,384]{1,0:T(8,128)S(1)}, f32[8,384]{1,0:T(8,128)S(1)}) custom-call(s32[256]{0:T(256)} %bitcast.19, s32[256]{0:T(256)} %bitcast.27, s32[1]{0:T(128)} %bitcast.2.at_ref, f32[6,1,1536]{2,1,0:T(1,128)} %rhs_ref.3, f32[1,1536]{1,0:T(1,128)} %shift_ref.7, ...), custom_call_target="tpu_custom_call" | custom-call | tf_op jit(solution)/shard_map/pallas_call | solution.py:411
  20.5 10.6 %all-to-all-start = ((f32[16,72,128]{2,1,0:T(8,128)}), f32[16,72,128]{2,1,0:T(8,128)S(1)}, u32[]{:S(2)}, u32[]{:S(2)}) async-start(f32[16,72,128]{2,1,0:T(8,128)} %bitcast.8), calls=%async_computation | async-start | bytes 1179648 | tf_op jit(solution)/shard_map/all_to_all | solution.py:484
  31.1 0.4 collective-permute-start.2
  31.5 0.0 collective-permute-start.3
  31.5 0.9 collective-permute-done.2.near_ref
  32.4 2.2 %collective-permute-done.3.far_ref = f32[8,384]{1,0:T(8,128)S(1)} collective-permute-done((f32[8,384]{1,0:T(8,128)S(1)}, f32[8,384]{1,0:T(8,128)S(1)}, u32[]{:S(2)}, u32[]{:S(2)}) %collective-permute-start.3) | collective-permute-done | bytes 12320 | tf_op jit(solution)/shard_map/ppermute | solution.py:440
  34.6 1.0 shard_map.89.terms_ref
  35.6 14.6 %all-to-all-done.y_ref = f32[16,72,128]{2,1,0:T(8,128)S(1)} async-done(((f32[16,72,128]{2,1,0:T(8,128)}), f32[16,72,128]{2,1,0:T(8,128)S(1)}, u32[]{:S(2)}, u32[]{:S(2)}) %all-to-all-start) | async-done | bytes 589856 | tf_op jit(solution)/shard_map/all_to_all | solution.py:484
  50.1 0.9 shard_map.90
  51.1 4.3 %all-to-all-start.1 = ((f32[16,72,128]{2,1,0:T(8,128)}), f32[16,72,128]{2,1,0:T(8,128)S(1)}, u32[]{:S(2)}, u32[]{:S(2)}) async-start(f32[16,72,128]{2,1,0:T(8,128)} %get-tuple-element.37), calls=%async_computation.1 | async-start | bytes 1179648 | tf_op jit(solution)/shard_map/all_to_all | solution.py:493
  55.4 0.9 shard_map.91
  56.3 2.0 %collective-permute-start.4 = (f32[8,384]{1,0:T(8,128)S(1)}, f32[8,384]{1,0:T(8,128)S(1)}, u32[]{:S(2)}, u32[]{:S(2)}) collective-permute-start(f32[8,384]{1,0:T(8,128)S(1)} %get-tuple-element.41), channel_id=1, source_target_pairs={{0,16},{16,0},{1,17},{17,1},{2,18},{18,2},{3,19},{19,3},{4,20},{20... | collective-permute-start | bytes 36872 | tf_op jit(solution)/shard_map/ppermute | solution.py:440
  58.3 0.0 collective-permute-start.5
  58.3 0.8 collective-permute-done.4.near_ref
  59.2 2.6 %collective-permute-done.5.far_ref = f32[8,384]{1,0:T(8,128)S(1)} collective-permute-done((f32[8,384]{1,0:T(8,128)S(1)}, f32[8,384]{1,0:T(8,128)S(1)}, u32[]{:S(2)}, u32[]{:S(2)}) %collective-permute-start.5) | collective-permute-done | bytes 12320 | tf_op jit(solution)/shard_map/ppermute | solution.py:440
  61.7 11.4 %all-to-all-done.1 = f32[16,72,128]{2,1,0:T(8,128)S(1)} async-done(((f32[16,72,128]{2,1,0:T(8,128)}), f32[16,72,128]{2,1,0:T(8,128)S(1)}, u32[]{:S(2)}, u32[]{:S(2)}) %all-to-all-start.1) | async-done | bytes 589856 | tf_op jit(solution)/shard_map/all_to_all | solution.py:493
  73.1 9.6 %shard_map.92 = (f32[1152,128]{1,0:T(8,128)}, f32[8,1536]{1,0:T(8,128)S(1)}, f32[8,1536]{1,0:T(8,128)S(1)}, f32[8,384]{1,0:T(8,128)S(1)}, f32[8,384]{1,0:T(8,128)S(1)}) custom-call(s32[256]{0:T(256)} %bitcast.20, s32[256]{0:T(256)} %bitcast.28, s32[1]{0:T(128)} %bitcast.2.at_ref, f32[1152,128]{1,0:T(8,128)S(1)} %bitcast.15, f32[1,1536]{1,0:T(1,128)} %shift_ref.7, ...), custom_call_target="tpu_custom_call" | custom-call | tf_op jit(solution)/shard_map/pallas_call | solution.py:411
  82.7 4.4 %all-to-all-start.2 = ((f32[16,72,128]{2,1,0:T(8,128)}), f32[16,72,128]{2,1,0:T(8,128)S(1)}, u32[]{:S(2)}, u32[]{:S(2)}) async-start(f32[16,72,128]{2,1,0:T(8,128)} %bitcast.10), calls=%async_computation.2 | async-start | bytes 1179648 | tf_op jit(solution)/shard_map/all_to_all | solution.py:484
  87.2 2.8 %collective-permute-start.6 = (f32[8,384]{1,0:T(8,128)S(1)}, f32[8,384]{1,0:T(8,128)S(1)}, u32[]{:S(2)}, u32[]{:S(2)}) collective-permute-start(f32[8,384]{1,0:T(8,128)S(1)} %get-tuple-element.45), channel_id=1, source_target_pairs={{0,16},{16,0},{1,17},{17,1},{2,18},{18,2},{3,19},{19,3},{4,20},{20... | collective-permute-start | bytes 36872 | tf_op jit(solution)/shard_map/ppermute | solution.py:440
  90.0 0.0 collective-permute-start.7
  90.0 0.9 shard_map.94
  90.9 0.0 collective-permute-done.6.near_ref
  90.9 2.3 %collective-permute-done.7.far_ref = f32[8,384]{1,0:T(8,128)S(1)} collective-permute-done((f32[8,384]{1,0:T(8,128)S(1)}, f32[8,384]{1,0:T(8,128)S(1)}, u32[]{:S(2)}, u32[]{:S(2)}) %collective-permute-start.7) | collective-permute-done | bytes 12320 | tf_op jit(solution)/shard_map/ppermute | solution.py:440
  93.2 1.0 shard_map.93.terms_ref
  94.2 10.4 %all-to-all-done.2.y_ref = f32[16,72,128]{2,1,0:T(8,128)S(1)} async-done(((f32[16,72,128]{2,1,0:T(8,128)}), f32[16,72,128]{2,1,0:T(8,128)S(1)}, u32[]{:S(2)}, u32[]{:S(2)}) %all-to-all-start.2) | async-done | bytes 589856 | tf_op jit(solution)/shard_map/all_to_all | solution.py:484
  104.6 1.0 shard_map.95
  105.6 3.6 %all-to-all-start.3 = ((f32[16,80,128]{2,1,0:T(8,128)}), f32[16,80,128]{2,1,0:T(8,128)S(1)}, u32[]{:S(2)}, u32[]{:S(2)}) async-start(f32[16,80,128]{2,1,0:T(8,128)} %get-tuple-element.50), calls=%async_computation.3 | async-start | bytes 1310720 | tf_op jit(solution)/shard_map/all_to_all | solution.py:493
  109.2 0.9 shard_map.96
  110.2 4.0 %collective-permute-start.8 = (f32[8,384]{1,0:T(8,128)S(1)}, f32[8,384]{1,0:T(8,128)S(1)}, u32[]{:S(2)}, u32[]{:S(2)}) collective-permute-start(f32[8,384]{1,0:T(8,128)S(1)} %get-tuple-element.52), channel_id=1, source_target_pairs={{0,16},{16,0},{1,17},{17,1},{2,18},{18,2},{3,19},{19,3},{4,20},{20... | collective-permute-start | bytes 36872 | tf_op jit(solution)/shard_map/ppermute | solution.py:440
  114.1 0.0 collective-permute-start.9
  114.1 0.8 collective-permute-done.8.near_ref
  115.0 2.6 %collective-permute-done.9.far_ref = f32[8,384]{1,0:T(8,128)S(1)} collective-permute-done((f32[8,384]{1,0:T(8,128)S(1)}, f32[8,384]{1,0:T(8,128)S(1)}, u32[]{:S(2)}, u32[]{:S(2)}) %collective-permute-start.9) | collective-permute-done | bytes 12320 | tf_op jit(solution)/shard_map/ppermute | solution.py:440
  117.6 8.0 %all-to-all-done.3 = f32[16,80,128]{2,1,0:T(8,128)S(1)} async-done(((f32[16,80,128]{2,1,0:T(8,128)}), f32[16,80,128]{2,1,0:T(8,128)S(1)}, u32[]{:S(2)}, u32[]{:S(2)}) %all-to-all-start.3) | async-done | bytes 655392 | tf_op jit(solution)/shard_map/all_to_all | solution.py:493
  125.7 0.6 broadcast_in_dim.2
  126.3 10.8 %all-to-all-start.4 = ((f32[16,8,128]{2,1,0:T(8,128)}), f32[16,8,128]{2,1,0:T(8,128)S(1)}, u32[]{:S(2)}, u32[]{:S(2)}) async-start(f32[16,8,128]{2,1,0:T(8,128)} %broadcast_in_dim.2), calls=%async_computation.4 | async-start | bytes 131072 | tf_op jit(solution)/shard_map/all_to_all | solution.py:520
  137.1 4.6 %shard_map.97.second_ref = f32[8,1536]{1,0:T(8,128)S(1)} custom-call(s32[256]{0:T(256)} %bitcast.21, s32[256]{0:T(256)} %bitcast.29, s32[1]{0:T(128)} %bitcast.2.at_ref, f32[1280,128]{1,0:T(8,128)S(1)} %bitcast.14, f32[1,1536]{1,0:T(1,128)} %shift_ref.7, f32[8,1536]{1,0:T(8,128)S(1)} %get-tuple-element.48.w_ref.v_ref, ...), custom_call_target="tpu_custom_call" | custom-call | tf_op jit(solution)/shard_map/pallas_call | solution.py:411
  141.7 1.3 all-to-all-done.4.sums_ref
  143.0 0.8 shard_map.98
  (2 shorter events, 0.0 us)
Async XLA Ops:
  1.8 12.8 %collective-permute-start.1 = (f32[8,384]{1,0:T(8,128)S(1)}, f32[8,384]{1,0:T(8,128)S(1)}, u32[]{:S(2)}, u32[]{:S(2)}) collective-permute-start(f32[8,384]{1,0:T(8,128)S(1)} %get-tuple-element.58), channel_id=1, source_target_pairs={{0,240},{16,32},{32,16},{48,64},{64,48},{80,96},{96,80},{112,128},... | collective-permute-start | bytes 36872 | tf_op jit(solution)/shard_map/ppermute | solution.py:440
  4.6 10.0 %collective-permute-start = (f32[8,384]{1,0:T(8,128)S(1)}, f32[8,384]{1,0:T(8,128)S(1)}, u32[]{:S(2)}, u32[]{:S(2)}) collective-permute-start(f32[8,384]{1,0:T(8,128)S(1)} %get-tuple-element.59), channel_id=1, source_target_pairs={{0,16},{16,0},{1,17},{17,1},{2,18},{18,2},{3,19},{19,3},{4,20},{20... | collective-permute-start | bytes 36872 | tf_op jit(solution)/shard_map/ppermute | solution.py:440
  20.5 29.7 %all-to-all-start = ((f32[16,72,128]{2,1,0:T(8,128)}), f32[16,72,128]{2,1,0:T(8,128)S(1)}, u32[]{:S(2)}, u32[]{:S(2)}) async-start(f32[16,72,128]{2,1,0:T(8,128)} %bitcast.8), calls=%async_computation | async-start | bytes 1179648 | tf_op jit(solution)/shard_map/all_to_all | solution.py:484
  31.1 1.3 collective-permute-start.2
  31.5 3.1 %collective-permute-start.3 = (f32[8,384]{1,0:T(8,128)S(1)}, f32[8,384]{1,0:T(8,128)S(1)}, u32[]{:S(2)}, u32[]{:S(2)}) collective-permute-start(f32[8,384]{1,0:T(8,128)S(1)} %get-tuple-element.35), channel_id=1, source_target_pairs={{0,240},{16,32},{32,16},{48,64},{64,48},{80,96},{96,80},{112,128},... | collective-permute-start | bytes 36872 | tf_op jit(solution)/shard_map/ppermute | solution.py:440
  51.1 22.1 %all-to-all-start.1 = ((f32[16,72,128]{2,1,0:T(8,128)}), f32[16,72,128]{2,1,0:T(8,128)S(1)}, u32[]{:S(2)}, u32[]{:S(2)}) async-start(f32[16,72,128]{2,1,0:T(8,128)} %get-tuple-element.37), calls=%async_computation.1 | async-start | bytes 1179648 | tf_op jit(solution)/shard_map/all_to_all | solution.py:493
  56.3 2.9 %collective-permute-start.4 = (f32[8,384]{1,0:T(8,128)S(1)}, f32[8,384]{1,0:T(8,128)S(1)}, u32[]{:S(2)}, u32[]{:S(2)}) collective-permute-start(f32[8,384]{1,0:T(8,128)S(1)} %get-tuple-element.41), channel_id=1, source_target_pairs={{0,16},{16,0},{1,17},{17,1},{2,18},{18,2},{3,19},{19,3},{4,20},{20... | collective-permute-start | bytes 36872 | tf_op jit(solution)/shard_map/ppermute | solution.py:440
  58.3 3.4 %collective-permute-start.5 = (f32[8,384]{1,0:T(8,128)S(1)}, f32[8,384]{1,0:T(8,128)S(1)}, u32[]{:S(2)}, u32[]{:S(2)}) collective-permute-start(f32[8,384]{1,0:T(8,128)S(1)} %get-tuple-element.42), channel_id=1, source_target_pairs={{0,240},{16,32},{32,16},{48,64},{64,48},{80,96},{96,80},{112,128},... | collective-permute-start | bytes 36872 | tf_op jit(solution)/shard_map/ppermute | solution.py:440
  82.7 21.9 %all-to-all-start.2 = ((f32[16,72,128]{2,1,0:T(8,128)}), f32[16,72,128]{2,1,0:T(8,128)S(1)}, u32[]{:S(2)}, u32[]{:S(2)}) async-start(f32[16,72,128]{2,1,0:T(8,128)} %bitcast.10), calls=%async_computation.2 | async-start | bytes 1179648 | tf_op jit(solution)/shard_map/all_to_all | solution.py:484
  87.2 3.7 %collective-permute-start.6 = (f32[8,384]{1,0:T(8,128)S(1)}, f32[8,384]{1,0:T(8,128)S(1)}, u32[]{:S(2)}, u32[]{:S(2)}) collective-permute-start(f32[8,384]{1,0:T(8,128)S(1)} %get-tuple-element.45), channel_id=1, source_target_pairs={{0,16},{16,0},{1,17},{17,1},{2,18},{18,2},{3,19},{19,3},{4,20},{20... | collective-permute-start | bytes 36872 | tf_op jit(solution)/shard_map/ppermute | solution.py:440
  90.0 3.2 %collective-permute-start.7 = (f32[8,384]{1,0:T(8,128)S(1)}, f32[8,384]{1,0:T(8,128)S(1)}, u32[]{:S(2)}, u32[]{:S(2)}) collective-permute-start(f32[8,384]{1,0:T(8,128)S(1)} %get-tuple-element.46), channel_id=1, source_target_pairs={{0,240},{16,32},{32,16},{48,64},{64,48},{80,96},{96,80},{112,128},... | collective-permute-start | bytes 36872 | tf_op jit(solution)/shard_map/ppermute | solution.py:440
  105.6 20.0 %all-to-all-start.3 = ((f32[16,80,128]{2,1,0:T(8,128)}), f32[16,80,128]{2,1,0:T(8,128)S(1)}, u32[]{:S(2)}, u32[]{:S(2)}) async-start(f32[16,80,128]{2,1,0:T(8,128)} %get-tuple-element.50), calls=%async_computation.3 | async-start | bytes 1310720 | tf_op jit(solution)/shard_map/all_to_all | solution.py:493
  110.2 4.8 %collective-permute-start.8 = (f32[8,384]{1,0:T(8,128)S(1)}, f32[8,384]{1,0:T(8,128)S(1)}, u32[]{:S(2)}, u32[]{:S(2)}) collective-permute-start(f32[8,384]{1,0:T(8,128)S(1)} %get-tuple-element.52), channel_id=1, source_target_pairs={{0,16},{16,0},{1,17},{17,1},{2,18},{18,2},{3,19},{19,3},{4,20},{20... | collective-permute-start | bytes 36872 | tf_op jit(solution)/shard_map/ppermute | solution.py:440
  114.1 3.4 %collective-permute-start.9 = (f32[8,384]{1,0:T(8,128)S(1)}, f32[8,384]{1,0:T(8,128)S(1)}, u32[]{:S(2)}, u32[]{:S(2)}) collective-permute-start(f32[8,384]{1,0:T(8,128)S(1)} %get-tuple-element.53), channel_id=1, source_target_pairs={{0,240},{16,32},{32,16},{48,64},{64,48},{80,96},{96,80},{112,128},... | collective-permute-start | bytes 36872 | tf_op jit(solution)/shard_map/ppermute | solution.py:440
  126.3 16.7 %all-to-all-start.4 = ((f32[16,8,128]{2,1,0:T(8,128)}), f32[16,8,128]{2,1,0:T(8,128)S(1)}, u32[]{:S(2)}, u32[]{:S(2)}) async-start(f32[16,8,128]{2,1,0:T(8,128)} %broadcast_in_dim.2), calls=%async_computation.4 | async-start | bytes 131072 | tf_op jit(solution)/shard_map/all_to_all | solution.py:520

commit v7 on v6

--- a/solution.py
+++ b/solution.py
@@ -18,10 +18,11 @@
 OWN = 16
 STORED = 256
 SLAB_ROWS = 256
-GROUP = 32
+GROUP = 64
 STEPS = STORED // GROUP
 CHUNK = 72
 TILES = 12
+PITCH = 17
 FACE = 4
 MIB = 1024 * 1024
 
@@ -109,11 +110,11 @@
         for half in range(GROUP // 16):
             base = g * GROUP + half * 16
             for t in range(CHUNK):
-                held[t * 16 : (t + 1) * 16, :] = x_ref[
+                held[t * PITCH : t * PITCH + 16, :] = x_ref[
                     pl.ds(pl.multiple_of(base, 16), 16), tile_at(t)
                 ].astype(F32)
             for e in range(16):
-                whole = block_of(held, e, 48)
+                whole = block_of(held, e, 3 * PITCH)
                 k_ref[base + e, :BLOCK] = whole.astype(BF16)
                 total = jnp.sum((whole * whole).reshape(12, 8, LANES), axis=0)
                 j = col_ref[base + e]
@@ -462,7 +463,7 @@
         ),
         scratch_shapes=[
             pltpu.VMEM((STORED, BLOCK * BLOCK), BF16),
-            pltpu.VMEM((CHUNK * 16, LANES), F32),
+            pltpu.VMEM((CHUNK * PITCH, LANES), F32),
             pltpu.VMEM((OWN, 8, LANES), F32),
             pltpu.SemaphoreType.DMA((STEPS,)),
             pltpu.SemaphoreType.DMA((STEPS,)),

time: 145 us -> 143 us (0.986)
  no operation moved by 1% of the time
where the time goes in v7:
time: 143 us; the launch traced here: 142 us
  waiting for transfers between devices  58.2 us (41%)
  starting transfers between devices  47.7 us (33%)
  Pallas kernels  35.2 us (25%)
    pallas_call x12, Pallas kernels, call(): pl.pallas_call(kernel, in_specs=[SMEM] * len(scalars) + [VMEM] * held + [...  27.4 us
    all_to_all x2, waiting for transfers between devices, all_rows(): arrived = lax.all_to_all(parts, DOM, 0, 0, tiled=True)  25.1 us
    all_to_all x2, waiting for transfers between devices, all_rows(): full = lax.all_to_all(copies, DOM, 0, 0, tiled=True)  19.4 us
    all_to_all x2, starting transfers between devices, all_rows(): arrived = lax.all_to_all(parts, DOM, 0, 0, tiled=True)  15 us
    ppermute x10, starting transfers between devices, exchanged(): return (lax.ppermute(near, 'slab_2', swap), lax.ppermute(far, SLAB, across))  14 us
    ppermute x10, waiting for transfers between devices, exchanged(): return (lax.ppermute(near, 'slab_2', swap), lax.ppermute(far, SLAB, across))  12.3 us
    all_to_all x1, starting transfers between devices, body(): lax.all_to_all(jnp.broadcast_to(sums[None], (slabs, *sums.shape)), SLAB,...  10.8 us
    all_to_all x2, starting transfers between devices, all_rows(): full = lax.all_to_all(copies, DOM, 0, 0, tiled=True)  7.88 us
  transfers between devices with their start and end apart: 15, of which 12 were waited for; matrix products, arithmetic and copies ran while one was open for 0% of the time, Pallas kernels for 12%

profile of v7, /device:TPU:1, one launch (start us, length us, event | category | flops | bytes accessed | tf_op | source)
XLA Modules:
  0.0 142.5 jit_solution(16587224112733089484)
XLA Ops:
  0.6 1.2 shard_map.87
  1.8 2.8 %collective-permute-start.1 = (f32[8,384]{1,0:T(8,128)S(1)}, f32[8,384]{1,0:T(8,128)S(1)}, u32[]{:S(2)}, u32[]{:S(2)}) collective-permute-start(f32[8,384]{1,0:T(8,128)S(1)} %get-tuple-element.58), channel_id=1, source_target_pairs={{0,240},{16,32},{32,16},{48,64},{64,48},{80,96},{96,80},{112,128},... | collective-permute-start | bytes 36872 | tf_op jit(solution)/shard_map/ppermute | solution.py:441
  4.6 2.0 %collective-permute-start = (f32[8,384]{1,0:T(8,128)S(1)}, f32[8,384]{1,0:T(8,128)S(1)}, u32[]{:S(2)}, u32[]{:S(2)}) collective-permute-start(f32[8,384]{1,0:T(8,128)S(1)} %get-tuple-element.59), channel_id=1, source_target_pairs={{0,16},{16,0},{1,17},{17,1},{2,18},{18,2},{3,19},{19,3},{4,20},{20... | collective-permute-start | bytes 36872 | tf_op jit(solution)/shard_map/ppermute | solution.py:441
  6.6 7.8 %shard_map.86 = (bf16[256,96,128]{2,1,0:T(8,128)(2,1)}, f32[8,1536]{1,0:T(8,128)S(1)}, bf16[256,128,128]{2,1,0:T(8,128)(2,1)S(1)}) custom-call(s32[256]{0:T(256)} %bitcast.18, bf16[256,9216]{1,0:T(8,128)(2,1)} %bitcast.16), custom_call_target="tpu_custom_call" | custom-call | tf_op jit(solution)/shard_map/pallas_call | solution.py:455
  14.5 0.0 collective-permute-done.1.far_ref
  14.5 0.0 collective-permute-done.near_ref
  14.5 5.4 %shard_map.88 = (f32[1152,128]{1,0:T(8,128)}, f32[8,1536]{1,0:T(8,128)S(1)}, f32[8,1536]{1,0:T(8,128)S(1)}, f32[8,384]{1,0:T(8,128)S(1)}, f32[8,384]{1,0:T(8,128)S(1)}) custom-call(s32[256]{0:T(256)} %bitcast.19, s32[256]{0:T(256)} %bitcast.27, s32[1]{0:T(128)} %bitcast.2.at_ref, f32[6,1,1536]{2,1,0:T(1,128)} %rhs_ref.3, f32[1,1536]{1,0:T(1,128)} %shift_ref.7, ...), custom_call_target="tpu_custom_call" | custom-call | tf_op jit(solution)/shard_map/pallas_call | solution.py:412
  19.9 10.6 %all-to-all-start = ((f32[16,72,128]{2,1,0:T(8,128)}), f32[16,72,128]{2,1,0:T(8,128)S(1)}, u32[]{:S(2)}, u32[]{:S(2)}) async-start(f32[16,72,128]{2,1,0:T(8,128)} %bitcast.8), calls=%async_computation | async-start | bytes 1179648 | tf_op jit(solution)/shard_map/all_to_all | solution.py:485
  30.5 0.4 collective-permute-start.2
  30.9 0.0 collective-permute-start.3
  30.9 0.9 collective-permute-done.2.near_ref
  31.8 2.2 %collective-permute-done.3.far_ref = f32[8,384]{1,0:T(8,128)S(1)} collective-permute-done((f32[8,384]{1,0:T(8,128)S(1)}, f32[8,384]{1,0:T(8,128)S(1)}, u32[]{:S(2)}, u32[]{:S(2)}) %collective-permute-start.3) | collective-permute-done | bytes 12320 | tf_op jit(solution)/shard_map/ppermute | solution.py:441
  34.0 1.0 shard_map.89.terms_ref
  35.0 14.6 %all-to-all-done.y_ref = f32[16,72,128]{2,1,0:T(8,128)S(1)} async-done(((f32[16,72,128]{2,1,0:T(8,128)}), f32[16,72,128]{2,1,0:T(8,128)S(1)}, u32[]{:S(2)}, u32[]{:S(2)}) %all-to-all-start) | async-done | bytes 589856 | tf_op jit(solution)/shard_map/all_to_all | solution.py:485
  49.5 0.9 shard_map.90
  50.5 4.3 %all-to-all-start.1 = ((f32[16,72,128]{2,1,0:T(8,128)}), f32[16,72,128]{2,1,0:T(8,128)S(1)}, u32[]{:S(2)}, u32[]{:S(2)}) async-start(f32[16,72,128]{2,1,0:T(8,128)} %get-tuple-element.37), calls=%async_computation.1 | async-start | bytes 1179648 | tf_op jit(solution)/shard_map/all_to_all | solution.py:494
  54.8 0.9 shard_map.91
  55.7 2.0 %collective-permute-start.4 = (f32[8,384]{1,0:T(8,128)S(1)}, f32[8,384]{1,0:T(8,128)S(1)}, u32[]{:S(2)}, u32[]{:S(2)}) collective-permute-start(f32[8,384]{1,0:T(8,128)S(1)} %get-tuple-element.41), channel_id=1, source_target_pairs={{0,16},{16,0},{1,17},{17,1},{2,18},{18,2},{3,19},{19,3},{4,20},{20... | collective-permute-start | bytes 36872 | tf_op jit(solution)/shard_map/ppermute | solution.py:441
  57.7 0.0 collective-permute-start.5
  57.7 0.8 collective-permute-done.4.near_ref
  58.6 2.6 %collective-permute-done.5.far_ref = f32[8,384]{1,0:T(8,128)S(1)} collective-permute-done((f32[8,384]{1,0:T(8,128)S(1)}, f32[8,384]{1,0:T(8,128)S(1)}, u32[]{:S(2)}, u32[]{:S(2)}) %collective-permute-start.5) | collective-permute-done | bytes 12320 | tf_op jit(solution)/shard_map/ppermute | solution.py:441
  61.1 11.4 %all-to-all-done.1 = f32[16,72,128]{2,1,0:T(8,128)S(1)} async-done(((f32[16,72,128]{2,1,0:T(8,128)}), f32[16,72,128]{2,1,0:T(8,128)S(1)}, u32[]{:S(2)}, u32[]{:S(2)}) %all-to-all-start.1) | async-done | bytes 589856 | tf_op jit(solution)/shard_map/all_to_all | solution.py:494
  72.5 8.9 %shard_map.92 = (f32[1152,128]{1,0:T(8,128)}, f32[8,1536]{1,0:T(8,128)S(1)}, f32[8,1536]{1,0:T(8,128)S(1)}, f32[8,384]{1,0:T(8,128)S(1)}, f32[8,384]{1,0:T(8,128)S(1)}) custom-call(s32[256]{0:T(256)} %bitcast.20, s32[256]{0:T(256)} %bitcast.28, s32[1]{0:T(128)} %bitcast.2.at_ref, f32[1152,128]{1,0:T(8,128)S(1)} %bitcast.15, f32[1,1536]{1,0:T(1,128)} %shift_ref.7, ...), custom_call_target="tpu_custom_call" | custom-call | tf_op jit(solution)/shard_map/pallas_call | solution.py:412
  81.5 4.4 %all-to-all-start.2 = ((f32[16,72,128]{2,1,0:T(8,128)}), f32[16,72,128]{2,1,0:T(8,128)S(1)}, u32[]{:S(2)}, u32[]{:S(2)}) async-start(f32[16,72,128]{2,1,0:T(8,128)} %bitcast.10), calls=%async_computation.2 | async-start | bytes 1179648 | tf_op jit(solution)/shard_map/all_to_all | solution.py:485
  85.9 2.9 %collective-permute-start.6 = (f32[8,384]{1,0:T(8,128)S(1)}, f32[8,384]{1,0:T(8,128)S(1)}, u32[]{:S(2)}, u32[]{:S(2)}) collective-permute-start(f32[8,384]{1,0:T(8,128)S(1)} %get-tuple-element.45), channel_id=1, source_target_pairs={{0,16},{16,0},{1,17},{17,1},{2,18},{18,2},{3,19},{19,3},{4,20},{20... | collective-permute-start | bytes 36872 | tf_op jit(solution)/shard_map/ppermute | solution.py:441
  88.8 0.0 collective-permute-start.7
  88.8 0.9 shard_map.94
  89.6 0.0 collective-permute-done.6.near_ref
  89.6 2.3 %collective-permute-done.7.far_ref = f32[8,384]{1,0:T(8,128)S(1)} collective-permute-done((f32[8,384]{1,0:T(8,128)S(1)}, f32[8,384]{1,0:T(8,128)S(1)}, u32[]{:S(2)}, u32[]{:S(2)}) %collective-permute-start.7) | collective-permute-done | bytes 12320 | tf_op jit(solution)/shard_map/ppermute | solution.py:441
  91.9 1.0 shard_map.93.terms_ref
  92.9 10.5 %all-to-all-done.2.y_ref = f32[16,72,128]{2,1,0:T(8,128)S(1)} async-done(((f32[16,72,128]{2,1,0:T(8,128)}), f32[16,72,128]{2,1,0:T(8,128)S(1)}, u32[]{:S(2)}, u32[]{:S(2)}) %all-to-all-start.2) | async-done | bytes 589856 | tf_op jit(solution)/shard_map/all_to_all | solution.py:485
  103.4 1.0 shard_map.95
  104.4 3.6 %all-to-all-start.3 = ((f32[16,80,128]{2,1,0:T(8,128)}), f32[16,80,128]{2,1,0:T(8,128)S(1)}, u32[]{:S(2)}, u32[]{:S(2)}) async-start(f32[16,80,128]{2,1,0:T(8,128)} %get-tuple-element.50), calls=%async_computation.3 | async-start | bytes 1310720 | tf_op jit(solution)/shard_map/all_to_all | solution.py:494
  108.0 0.9 shard_map.96
  108.9 4.0 %collective-permute-start.8 = (f32[8,384]{1,0:T(8,128)S(1)}, f32[8,384]{1,0:T(8,128)S(1)}, u32[]{:S(2)}, u32[]{:S(2)}) collective-permute-start(f32[8,384]{1,0:T(8,128)S(1)} %get-tuple-element.52), channel_id=1, source_target_pairs={{0,16},{16,0},{1,17},{17,1},{2,18},{18,2},{3,19},{19,3},{4,20},{20... | collective-permute-start | bytes 36872 | tf_op jit(solution)/shard_map/ppermute | solution.py:441
  112.9 0.0 collective-permute-start.9
  112.9 0.8 collective-permute-done.8.near_ref
  113.7 2.7 %collective-permute-done.9.far_ref = f32[8,384]{1,0:T(8,128)S(1)} collective-permute-done((f32[8,384]{1,0:T(8,128)S(1)}, f32[8,384]{1,0:T(8,128)S(1)}, u32[]{:S(2)}, u32[]{:S(2)}) %collective-permute-start.9) | collective-permute-done | bytes 12320 | tf_op jit(solution)/shard_map/ppermute | solution.py:441
  116.4 8.0 %all-to-all-done.3 = f32[16,80,128]{2,1,0:T(8,128)S(1)} async-done(((f32[16,80,128]{2,1,0:T(8,128)}), f32[16,80,128]{2,1,0:T(8,128)S(1)}, u32[]{:S(2)}, u32[]{:S(2)}) %all-to-all-start.3) | async-done | bytes 655392 | tf_op jit(solution)/shard_map/all_to_all | solution.py:494
  124.4 0.6 broadcast_in_dim.2
  125.0 10.8 %all-to-all-start.4 = ((f32[16,8,128]{2,1,0:T(8,128)}), f32[16,8,128]{2,1,0:T(8,128)S(1)}, u32[]{:S(2)}, u32[]{:S(2)}) async-start(f32[16,8,128]{2,1,0:T(8,128)} %broadcast_in_dim.2), calls=%async_computation.4 | async-start | bytes 131072 | tf_op jit(solution)/shard_map/all_to_all | solution.py:521
  135.8 4.4 %shard_map.97.second_ref = f32[8,1536]{1,0:T(8,128)S(1)} custom-call(s32[256]{0:T(256)} %bitcast.21, s32[256]{0:T(256)} %bitcast.29, s32[1]{0:T(128)} %bitcast.2.at_ref, f32[1280,128]{1,0:T(8,128)S(1)} %bitcast.14, f32[1,1536]{1,0:T(1,128)} %shift_ref.7, f32[8,1536]{1,0:T(8,128)S(1)} %get-tuple-element.48.w_ref.v_ref, ...), custom_call_target="tpu_custom_call" | custom-call | tf_op jit(solution)/shard_map/pallas_call | solution.py:412
  140.2 1.4 %all-to-all-done.4.sums_ref = f32[16,8,128]{2,1,0:T(8,128)S(1)} async-done(((f32[16,8,128]{2,1,0:T(8,128)}), f32[16,8,128]{2,1,0:T(8,128)S(1)}, u32[]{:S(2)}, u32[]{:S(2)}) %all-to-all-start.4) | async-done | bytes 65568 | tf_op jit(solution)/shard_map/all_to_all | solution.py:521
  141.7 0.8 shard_map.98
  (2 shorter events, 0.0 us)
Async XLA Ops:
  1.8 12.6 %collective-permute-start.1 = (f32[8,384]{1,0:T(8,128)S(1)}, f32[8,384]{1,0:T(8,128)S(1)}, u32[]{:S(2)}, u32[]{:S(2)}) collective-permute-start(f32[8,384]{1,0:T(8,128)S(1)} %get-tuple-element.58), channel_id=1, source_target_pairs={{0,240},{16,32},{32,16},{48,64},{64,48},{80,96},{96,80},{112,128},... | collective-permute-start | bytes 36872 | tf_op jit(solution)/shard_map/ppermute | solution.py:441
  4.6 9.9 %collective-permute-start = (f32[8,384]{1,0:T(8,128)S(1)}, f32[8,384]{1,0:T(8,128)S(1)}, u32[]{:S(2)}, u32[]{:S(2)}) collective-permute-start(f32[8,384]{1,0:T(8,128)S(1)} %get-tuple-element.59), channel_id=1, source_target_pairs={{0,16},{16,0},{1,17},{17,1},{2,18},{18,2},{3,19},{19,3},{4,20},{20... | collective-permute-start | bytes 36872 | tf_op jit(solution)/shard_map/ppermute | solution.py:441
  19.9 29.7 %all-to-all-start = ((f32[16,72,128]{2,1,0:T(8,128)}), f32[16,72,128]{2,1,0:T(8,128)S(1)}, u32[]{:S(2)}, u32[]{:S(2)}) async-start(f32[16,72,128]{2,1,0:T(8,128)} %bitcast.8), calls=%async_computation | async-start | bytes 1179648 | tf_op jit(solution)/shard_map/all_to_all | solution.py:485
  30.5 1.3 collective-permute-start.2
  30.9 3.1 %collective-permute-start.3 = (f32[8,384]{1,0:T(8,128)S(1)}, f32[8,384]{1,0:T(8,128)S(1)}, u32[]{:S(2)}, u32[]{:S(2)}) collective-permute-start(f32[8,384]{1,0:T(8,128)S(1)} %get-tuple-element.35), channel_id=1, source_target_pairs={{0,240},{16,32},{32,16},{48,64},{64,48},{80,96},{96,80},{112,128},... | collective-permute-start | bytes 36872 | tf_op jit(solution)/shard_map/ppermute | solution.py:441
  50.5 22.1 %all-to-all-start.1 = ((f32[16,72,128]{2,1,0:T(8,128)}), f32[16,72,128]{2,1,0:T(8,128)S(1)}, u32[]{:S(2)}, u32[]{:S(2)}) async-start(f32[16,72,128]{2,1,0:T(8,128)} %get-tuple-element.37), calls=%async_computation.1 | async-start | bytes 1179648 | tf_op jit(solution)/shard_map/all_to_all | solution.py:494
  55.7 2.9 %collective-permute-start.4 = (f32[8,384]{1,0:T(8,128)S(1)}, f32[8,384]{1,0:T(8,128)S(1)}, u32[]{:S(2)}, u32[]{:S(2)}) collective-permute-start(f32[8,384]{1,0:T(8,128)S(1)} %get-tuple-element.41), channel_id=1, source_target_pairs={{0,16},{16,0},{1,17},{17,1},{2,18},{18,2},{3,19},{19,3},{4,20},{20... | collective-permute-start | bytes 36872 | tf_op jit(solution)/shard_map/ppermute | solution.py:441
  57.7 3.4 %collective-permute-start.5 = (f32[8,384]{1,0:T(8,128)S(1)}, f32[8,384]{1,0:T(8,128)S(1)}, u32[]{:S(2)}, u32[]{:S(2)}) collective-permute-start(f32[8,384]{1,0:T(8,128)S(1)} %get-tuple-element.42), channel_id=1, source_target_pairs={{0,240},{16,32},{32,16},{48,64},{64,48},{80,96},{96,80},{112,128},... | collective-permute-start | bytes 36872 | tf_op jit(solution)/shard_map/ppermute | solution.py:441
  81.5 21.9 %all-to-all-start.2 = ((f32[16,72,128]{2,1,0:T(8,128)}), f32[16,72,128]{2,1,0:T(8,128)S(1)}, u32[]{:S(2)}, u32[]{:S(2)}) async-start(f32[16,72,128]{2,1,0:T(8,128)} %bitcast.10), calls=%async_computation.2 | async-start | bytes 1179648 | tf_op jit(solution)/shard_map/all_to_all | solution.py:485
  85.9 3.7 %collective-permute-start.6 = (f32[8,384]{1,0:T(8,128)S(1)}, f32[8,384]{1,0:T(8,128)S(1)}, u32[]{:S(2)}, u32[]{:S(2)}) collective-permute-start(f32[8,384]{1,0:T(8,128)S(1)} %get-tuple-element.45), channel_id=1, source_target_pairs={{0,16},{16,0},{1,17},{17,1},{2,18},{18,2},{3,19},{19,3},{4,20},{20... | collective-permute-start | bytes 36872 | tf_op jit(solution)/shard_map/ppermute | solution.py:441
  88.8 3.1 %collective-permute-start.7 = (f32[8,384]{1,0:T(8,128)S(1)}, f32[8,384]{1,0:T(8,128)S(1)}, u32[]{:S(2)}, u32[]{:S(2)}) collective-permute-start(f32[8,384]{1,0:T(8,128)S(1)} %get-tuple-element.46), channel_id=1, source_target_pairs={{0,240},{16,32},{32,16},{48,64},{64,48},{80,96},{96,80},{112,128},... | collective-permute-start | bytes 36872 | tf_op jit(solution)/shard_map/ppermute | solution.py:441
  104.4 20.0 %all-to-all-start.3 = ((f32[16,80,128]{2,1,0:T(8,128)}), f32[16,80,128]{2,1,0:T(8,128)S(1)}, u32[]{:S(2)}, u32[]{:S(2)}) async-start(f32[16,80,128]{2,1,0:T(8,128)} %get-tuple-element.50), calls=%async_computation.3 | async-start | bytes 1310720 | tf_op jit(solution)/shard_map/all_to_all | solution.py:494
  108.9 4.8 %collective-permute-start.8 = (f32[8,384]{1,0:T(8,128)S(1)}, f32[8,384]{1,0:T(8,128)S(1)}, u32[]{:S(2)}, u32[]{:S(2)}) collective-permute-start(f32[8,384]{1,0:T(8,128)S(1)} %get-tuple-element.52), channel_id=1, source_target_pairs={{0,16},{16,0},{1,17},{17,1},{2,18},{18,2},{3,19},{19,3},{4,20},{20... | collective-permute-start | bytes 36872 | tf_op jit(solution)/shard_map/ppermute | solution.py:441
  112.9 3.5 %collective-permute-start.9 = (f32[8,384]{1,0:T(8,128)S(1)}, f32[8,384]{1,0:T(8,128)S(1)}, u32[]{:S(2)}, u32[]{:S(2)}) collective-permute-start(f32[8,384]{1,0:T(8,128)S(1)} %get-tuple-element.53), channel_id=1, source_target_pairs={{0,240},{16,32},{32,16},{48,64},{64,48},{80,96},{96,80},{112,128},... | collective-permute-start | bytes 36872 | tf_op jit(solution)/shard_map/ppermute | solution.py:441
  125.0 16.6 %all-to-all-start.4 = ((f32[16,8,128]{2,1,0:T(8,128)}), f32[16,8,128]{2,1,0:T(8,128)S(1)}, u32[]{:S(2)}, u32[]{:S(2)}) async-start(f32[16,8,128]{2,1,0:T(8,128)} %broadcast_in_dim.2), calls=%async_computation.4 | async-start | bytes 131072 | tf_op jit(solution)/shard_map/all_to_all | solution.py:521

commit v8 on v7

--- a/solution.py
+++ b/solution.py
@@ -18,7 +18,7 @@
 OWN = 16
 STORED = 256
 SLAB_ROWS = 256
-GROUP = 64
+GROUP = 128
 STEPS = STORED // GROUP
 CHUNK = 72
 TILES = 12

time: 143 us -> 144 us (level)
  no operation moved by 1% of the time
where the time goes in v8:
time: 144 us; the launch traced here: 143 us
  waiting for transfers between devices  57.9 us (40%)
  starting transfers between devices  47.9 us (33%)
  Pallas kernels  36 us (25%)
    pallas_call x12, Pallas kernels, call(): pl.pallas_call(kernel, in_specs=[SMEM] * len(scalars) + [VMEM] * held + [...  27.6 us
    all_to_all x2, waiting for transfers between devices, all_rows(): arrived = lax.all_to_all(parts, DOM, 0, 0, tiled=True)  25.1 us
    all_to_all x2, waiting for transfers between devices, all_rows(): full = lax.all_to_all(copies, DOM, 0, 0, tiled=True)  19.4 us
    all_to_all x2, starting transfers between devices, all_rows(): arrived = lax.all_to_all(parts, DOM, 0, 0, tiled=True)  15.1 us
    ppermute x10, starting transfers between devices, exchanged(): return (lax.ppermute(near, 'slab_2', swap), lax.ppermute(far, SLAB, across))  14 us
    ppermute x10, waiting for transfers between devices, exchanged(): return (lax.ppermute(near, 'slab_2', swap), lax.ppermute(far, SLAB, across))  12.3 us
    all_to_all x1, starting transfers between devices, body(): lax.all_to_all(jnp.broadcast_to(sums[None], (slabs, *sums.shape)), SLAB,...  10.8 us
    pallas_call x1, Pallas kernels, body(): pl.pallas_call(stiff_prep, in_specs=[SMEM, hbm], out_specs=(hbm, VMEM, VM...  8.4 us
  transfers between devices with their start and end apart: 15, of which 12 were waited for; matrix products, arithmetic and copies ran while one was open for 0% of the time, Pallas kernels for 12%

profile of v8, /device:TPU:1, one launch (start us, length us, event | category | flops | bytes accessed | tf_op | source)
XLA Modules:
  0.0 143.2 jit_solution(18207704164548579789)
XLA Ops:
  0.6 1.2 shard_map.87
  1.8 2.8 %collective-permute-start.1 = (f32[8,384]{1,0:T(8,128)S(1)}, f32[8,384]{1,0:T(8,128)S(1)}, u32[]{:S(2)}, u32[]{:S(2)}) collective-permute-start(f32[8,384]{1,0:T(8,128)S(1)} %get-tuple-element.58), channel_id=1, source_target_pairs={{0,240},{16,32},{32,16},{48,64},{64,48},{80,96},{96,80},{112,128},... | collective-permute-start | bytes 36872 | tf_op jit(solution)/shard_map/ppermute | solution.py:441
  4.6 2.0 %collective-permute-start = (f32[8,384]{1,0:T(8,128)S(1)}, f32[8,384]{1,0:T(8,128)S(1)}, u32[]{:S(2)}, u32[]{:S(2)}) collective-permute-start(f32[8,384]{1,0:T(8,128)S(1)} %get-tuple-element.59), channel_id=1, source_target_pairs={{0,16},{16,0},{1,17},{17,1},{2,18},{18,2},{3,19},{19,3},{4,20},{20... | collective-permute-start | bytes 36872 | tf_op jit(solution)/shard_map/ppermute | solution.py:441
  6.6 8.4 %shard_map.86 = (bf16[256,96,128]{2,1,0:T(8,128)(2,1)}, f32[8,1536]{1,0:T(8,128)S(1)}, bf16[256,128,128]{2,1,0:T(8,128)(2,1)S(1)}) custom-call(s32[256]{0:T(256)} %bitcast.18, bf16[256,9216]{1,0:T(8,128)(2,1)} %bitcast.16), custom_call_target="tpu_custom_call" | custom-call | tf_op jit(solution)/shard_map/pallas_call | solution.py:455
  15.1 0.0 collective-permute-done.1.far_ref
  15.1 0.0 collective-permute-done.near_ref
  15.1 5.1 %shard_map.88 = (f32[1152,128]{1,0:T(8,128)}, f32[8,1536]{1,0:T(8,128)S(1)}, f32[8,1536]{1,0:T(8,128)S(1)}, f32[8,384]{1,0:T(8,128)S(1)}, f32[8,384]{1,0:T(8,128)S(1)}) custom-call(s32[256]{0:T(256)} %bitcast.19, s32[256]{0:T(256)} %bitcast.27, s32[1]{0:T(128)} %bitcast.2.at_ref, f32[6,1,1536]{2,1,0:T(1,128)} %rhs_ref.3, f32[1,1536]{1,0:T(1,128)} %shift_ref.7, ...), custom_call_target="tpu_custom_call" | custom-call | tf_op jit(solution)/shard_map/pallas_call | solution.py:412
  20.2 10.6 %all-to-all-start = ((f32[16,72,128]{2,1,0:T(8,128)}), f32[16,72,128]{2,1,0:T(8,128)S(1)}, u32[]{:S(2)}, u32[]{:S(2)}) async-start(f32[16,72,128]{2,1,0:T(8,128)} %bitcast.8), calls=%async_computation | async-start | bytes 1179648 | tf_op jit(solution)/shard_map/all_to_all | solution.py:485
  30.9 0.4 collective-permute-start.2
  31.2 0.0 collective-permute-start.3
  31.2 0.9 collective-permute-done.2.near_ref
  32.1 2.2 %collective-permute-done.3.far_ref = f32[8,384]{1,0:T(8,128)S(1)} collective-permute-done((f32[8,384]{1,0:T(8,128)S(1)}, f32[8,384]{1,0:T(8,128)S(1)}, u32[]{:S(2)}, u32[]{:S(2)}) %collective-permute-start.3) | collective-permute-done | bytes 12320 | tf_op jit(solution)/shard_map/ppermute | solution.py:441
  34.4 1.0 shard_map.89.terms_ref
  35.3 14.6 %all-to-all-done.y_ref = f32[16,72,128]{2,1,0:T(8,128)S(1)} async-done(((f32[16,72,128]{2,1,0:T(8,128)}), f32[16,72,128]{2,1,0:T(8,128)S(1)}, u32[]{:S(2)}, u32[]{:S(2)}) %all-to-all-start) | async-done | bytes 589856 | tf_op jit(solution)/shard_map/all_to_all | solution.py:485
  49.9 0.9 shard_map.90
  50.8 4.3 %all-to-all-start.1 = ((f32[16,72,128]{2,1,0:T(8,128)}), f32[16,72,128]{2,1,0:T(8,128)S(1)}, u32[]{:S(2)}, u32[]{:S(2)}) async-start(f32[16,72,128]{2,1,0:T(8,128)} %get-tuple-element.37), calls=%async_computation.1 | async-start | bytes 1179648 | tf_op jit(solution)/shard_map/all_to_all | solution.py:494
  55.1 0.9 shard_map.91
  56.1 2.0 %collective-permute-start.4 = (f32[8,384]{1,0:T(8,128)S(1)}, f32[8,384]{1,0:T(8,128)S(1)}, u32[]{:S(2)}, u32[]{:S(2)}) collective-permute-start(f32[8,384]{1,0:T(8,128)S(1)} %get-tuple-element.41), channel_id=1, source_target_pairs={{0,16},{16,0},{1,17},{17,1},{2,18},{18,2},{3,19},{19,3},{4,20},{20... | collective-permute-start | bytes 36872 | tf_op jit(solution)/shard_map/ppermute | solution.py:441
  58.1 0.0 collective-permute-start.5
  58.1 0.8 collective-permute-done.4.near_ref
  58.9 2.6 %collective-permute-done.5.far_ref = f32[8,384]{1,0:T(8,128)S(1)} collective-permute-done((f32[8,384]{1,0:T(8,128)S(1)}, f32[8,384]{1,0:T(8,128)S(1)}, u32[]{:S(2)}, u32[]{:S(2)}) %collective-permute-start.5) | collective-permute-done | bytes 12320 | tf_op jit(solution)/shard_map/ppermute | solution.py:441
  61.5 11.4 %all-to-all-done.1 = f32[16,72,128]{2,1,0:T(8,128)S(1)} async-done(((f32[16,72,128]{2,1,0:T(8,128)}), f32[16,72,128]{2,1,0:T(8,128)S(1)}, u32[]{:S(2)}, u32[]{:S(2)}) %all-to-all-start.1) | async-done | bytes 589856 | tf_op jit(solution)/shard_map/all_to_all | solution.py:494
  72.9 9.1 %shard_map.92 = (f32[1152,128]{1,0:T(8,128)}, f32[8,1536]{1,0:T(8,128)S(1)}, f32[8,1536]{1,0:T(8,128)S(1)}, f32[8,384]{1,0:T(8,128)S(1)}, f32[8,384]{1,0:T(8,128)S(1)}) custom-call(s32[256]{0:T(256)} %bitcast.20, s32[256]{0:T(256)} %bitcast.28, s32[1]{0:T(128)} %bitcast.2.at_ref, f32[1152,128]{1,0:T(8,128)S(1)} %bitcast.15, f32[1,1536]{1,0:T(1,128)} %shift_ref.7, ...), custom_call_target="tpu_custom_call" | custom-call | tf_op jit(solution)/shard_map/pallas_call | solution.py:412
  81.9 4.4 %all-to-all-start.2 = ((f32[16,72,128]{2,1,0:T(8,128)}), f32[16,72,128]{2,1,0:T(8,128)S(1)}, u32[]{:S(2)}, u32[]{:S(2)}) async-start(f32[16,72,128]{2,1,0:T(8,128)} %bitcast.10), calls=%async_computation.2 | async-start | bytes 1179648 | tf_op jit(solution)/shard_map/all_to_all | solution.py:485
  86.4 2.8 %collective-permute-start.6 = (f32[8,384]{1,0:T(8,128)S(1)}, f32[8,384]{1,0:T(8,128)S(1)}, u32[]{:S(2)}, u32[]{:S(2)}) collective-permute-start(f32[8,384]{1,0:T(8,128)S(1)} %get-tuple-element.45), channel_id=1, source_target_pairs={{0,16},{16,0},{1,17},{17,1},{2,18},{18,2},{3,19},{19,3},{4,20},{20... | collective-permute-start | bytes 36872 | tf_op jit(solution)/shard_map/ppermute | solution.py:441
  89.2 0.0 collective-permute-start.7
  89.2 0.9 shard_map.94
  90.1 0.0 collective-permute-done.6.near_ref
  90.1 2.3 %collective-permute-done.7.far_ref = f32[8,384]{1,0:T(8,128)S(1)} collective-permute-done((f32[8,384]{1,0:T(8,128)S(1)}, f32[8,384]{1,0:T(8,128)S(1)}, u32[]{:S(2)}, u32[]{:S(2)}) %collective-permute-start.7) | collective-permute-done | bytes 12320 | tf_op jit(solution)/shard_map/ppermute | solution.py:441
  92.4 1.0 shard_map.93.terms_ref
  93.3 10.5 %all-to-all-done.2.y_ref = f32[16,72,128]{2,1,0:T(8,128)S(1)} async-done(((f32[16,72,128]{2,1,0:T(8,128)}), f32[16,72,128]{2,1,0:T(8,128)S(1)}, u32[]{:S(2)}, u32[]{:S(2)}) %all-to-all-start.2) | async-done | bytes 589856 | tf_op jit(solution)/shard_map/all_to_all | solution.py:485
  103.9 1.0 shard_map.95
  104.9 3.8 %all-to-all-start.3 = ((f32[16,80,128]{2,1,0:T(8,128)}), f32[16,80,128]{2,1,0:T(8,128)S(1)}, u32[]{:S(2)}, u32[]{:S(2)}) async-start(f32[16,80,128]{2,1,0:T(8,128)} %get-tuple-element.50), calls=%async_computation.3 | async-start | bytes 1310720 | tf_op jit(solution)/shard_map/all_to_all | solution.py:494
  108.6 0.9 shard_map.96
  109.6 3.9 %collective-permute-start.8 = (f32[8,384]{1,0:T(8,128)S(1)}, f32[8,384]{1,0:T(8,128)S(1)}, u32[]{:S(2)}, u32[]{:S(2)}) collective-permute-start(f32[8,384]{1,0:T(8,128)S(1)} %get-tuple-element.52), channel_id=1, source_target_pairs={{0,16},{16,0},{1,17},{17,1},{2,18},{18,2},{3,19},{19,3},{4,20},{20... | collective-permute-start | bytes 36872 | tf_op jit(solution)/shard_map/ppermute | solution.py:441
  113.5 0.0 collective-permute-start.9
  113.5 0.8 collective-permute-done.8.near_ref
  114.4 2.7 %collective-permute-done.9.far_ref = f32[8,384]{1,0:T(8,128)S(1)} collective-permute-done((f32[8,384]{1,0:T(8,128)S(1)}, f32[8,384]{1,0:T(8,128)S(1)}, u32[]{:S(2)}, u32[]{:S(2)}) %collective-permute-start.9) | collective-permute-done | bytes 12320 | tf_op jit(solution)/shard_map/ppermute | solution.py:441
  117.0 8.0 %all-to-all-done.3 = f32[16,80,128]{2,1,0:T(8,128)S(1)} async-done(((f32[16,80,128]{2,1,0:T(8,128)}), f32[16,80,128]{2,1,0:T(8,128)S(1)}, u32[]{:S(2)}, u32[]{:S(2)}) %all-to-all-start.3) | async-done | bytes 655392 | tf_op jit(solution)/shard_map/all_to_all | solution.py:494
  125.1 0.6 broadcast_in_dim.2
  125.7 10.8 %all-to-all-start.4 = ((f32[16,8,128]{2,1,0:T(8,128)}), f32[16,8,128]{2,1,0:T(8,128)S(1)}, u32[]{:S(2)}, u32[]{:S(2)}) async-start(f32[16,8,128]{2,1,0:T(8,128)} %broadcast_in_dim.2), calls=%async_computation.4 | async-start | bytes 131072 | tf_op jit(solution)/shard_map/all_to_all | solution.py:521
  136.5 4.8 %shard_map.97.second_ref = f32[8,1536]{1,0:T(8,128)S(1)} custom-call(s32[256]{0:T(256)} %bitcast.21, s32[256]{0:T(256)} %bitcast.29, s32[1]{0:T(128)} %bitcast.2.at_ref, f32[1280,128]{1,0:T(8,128)S(1)} %bitcast.14, f32[1,1536]{1,0:T(1,128)} %shift_ref.7, f32[8,1536]{1,0:T(8,128)S(1)} %get-tuple-element.48.w_ref.v_ref, ...), custom_call_target="tpu_custom_call" | custom-call | tf_op jit(solution)/shard_map/pallas_call | solution.py:412
  141.2 1.1 all-to-all-done.4.sums_ref
  142.3 0.8 shard_map.98
  (2 shorter events, 0.0 us)
Async XLA Ops:
  1.8 13.2 %collective-permute-start.1 = (f32[8,384]{1,0:T(8,128)S(1)}, f32[8,384]{1,0:T(8,128)S(1)}, u32[]{:S(2)}, u32[]{:S(2)}) collective-permute-start(f32[8,384]{1,0:T(8,128)S(1)} %get-tuple-element.58), channel_id=1, source_target_pairs={{0,240},{16,32},{32,16},{48,64},{64,48},{80,96},{96,80},{112,128},... | collective-permute-start | bytes 36872 | tf_op jit(solution)/shard_map/ppermute | solution.py:441
  4.6 10.4 %collective-permute-start = (f32[8,384]{1,0:T(8,128)S(1)}, f32[8,384]{1,0:T(8,128)S(1)}, u32[]{:S(2)}, u32[]{:S(2)}) collective-permute-start(f32[8,384]{1,0:T(8,128)S(1)} %get-tuple-element.59), channel_id=1, source_target_pairs={{0,16},{16,0},{1,17},{17,1},{2,18},{18,2},{3,19},{19,3},{4,20},{20... | collective-permute-start | bytes 36872 | tf_op jit(solution)/shard_map/ppermute | solution.py:441
  20.2 29.7 %all-to-all-start = ((f32[16,72,128]{2,1,0:T(8,128)}), f32[16,72,128]{2,1,0:T(8,128)S(1)}, u32[]{:S(2)}, u32[]{:S(2)}) async-start(f32[16,72,128]{2,1,0:T(8,128)} %bitcast.8), calls=%async_computation | async-start | bytes 1179648 | tf_op jit(solution)/shard_map/all_to_all | solution.py:485
  30.9 1.3 collective-permute-start.2
  31.2 3.1 %collective-permute-start.3 = (f32[8,384]{1,0:T(8,128)S(1)}, f32[8,384]{1,0:T(8,128)S(1)}, u32[]{:S(2)}, u32[]{:S(2)}) collective-permute-start(f32[8,384]{1,0:T(8,128)S(1)} %get-tuple-element.35), channel_id=1, source_target_pairs={{0,240},{16,32},{32,16},{48,64},{64,48},{80,96},{96,80},{112,128},... | collective-permute-start | bytes 36872 | tf_op jit(solution)/shard_map/ppermute | solution.py:441
  50.8 22.1 %all-to-all-start.1 = ((f32[16,72,128]{2,1,0:T(8,128)}), f32[16,72,128]{2,1,0:T(8,128)S(1)}, u32[]{:S(2)}, u32[]{:S(2)}) async-start(f32[16,72,128]{2,1,0:T(8,128)} %get-tuple-element.37), calls=%async_computation.1 | async-start | bytes 1179648 | tf_op jit(solution)/shard_map/all_to_all | solution.py:494
  56.1 2.9 %collective-permute-start.4 = (f32[8,384]{1,0:T(8,128)S(1)}, f32[8,384]{1,0:T(8,128)S(1)}, u32[]{:S(2)}, u32[]{:S(2)}) collective-permute-start(f32[8,384]{1,0:T(8,128)S(1)} %get-tuple-element.41), channel_id=1, source_target_pairs={{0,16},{16,0},{1,17},{17,1},{2,18},{18,2},{3,19},{19,3},{4,20},{20... | collective-permute-start | bytes 36872 | tf_op jit(solution)/shard_map/ppermute | solution.py:441
  58.1 3.4 %collective-permute-start.5 = (f32[8,384]{1,0:T(8,128)S(1)}, f32[8,384]{1,0:T(8,128)S(1)}, u32[]{:S(2)}, u32[]{:S(2)}) collective-permute-start(f32[8,384]{1,0:T(8,128)S(1)} %get-tuple-element.42), channel_id=1, source_target_pairs={{0,240},{16,32},{32,16},{48,64},{64,48},{80,96},{96,80},{112,128},... | collective-permute-start | bytes 36872 | tf_op jit(solution)/shard_map/ppermute | solution.py:441
  81.9 21.9 %all-to-all-start.2 = ((f32[16,72,128]{2,1,0:T(8,128)}), f32[16,72,128]{2,1,0:T(8,128)S(1)}, u32[]{:S(2)}, u32[]{:S(2)}) async-start(f32[16,72,128]{2,1,0:T(8,128)} %bitcast.10), calls=%async_computation.2 | async-start | bytes 1179648 | tf_op jit(solution)/shard_map/all_to_all | solution.py:485
  86.4 3.7 %collective-permute-start.6 = (f32[8,384]{1,0:T(8,128)S(1)}, f32[8,384]{1,0:T(8,128)S(1)}, u32[]{:S(2)}, u32[]{:S(2)}) collective-permute-start(f32[8,384]{1,0:T(8,128)S(1)} %get-tuple-element.45), channel_id=1, source_target_pairs={{0,16},{16,0},{1,17},{17,1},{2,18},{18,2},{3,19},{19,3},{4,20},{20... | collective-permute-start | bytes 36872 | tf_op jit(solution)/shard_map/ppermute | solution.py:441
  89.2 3.1 %collective-permute-start.7 = (f32[8,384]{1,0:T(8,128)S(1)}, f32[8,384]{1,0:T(8,128)S(1)}, u32[]{:S(2)}, u32[]{:S(2)}) collective-permute-start(f32[8,384]{1,0:T(8,128)S(1)} %get-tuple-element.46), channel_id=1, source_target_pairs={{0,240},{16,32},{32,16},{48,64},{64,48},{80,96},{96,80},{112,128},... | collective-permute-start | bytes 36872 | tf_op jit(solution)/shard_map/ppermute | solution.py:441
  104.9 20.2 %all-to-all-start.3 = ((f32[16,80,128]{2,1,0:T(8,128)}), f32[16,80,128]{2,1,0:T(8,128)S(1)}, u32[]{:S(2)}, u32[]{:S(2)}) async-start(f32[16,80,128]{2,1,0:T(8,128)} %get-tuple-element.50), calls=%async_computation.3 | async-start | bytes 1310720 | tf_op jit(solution)/shard_map/all_to_all | solution.py:494
  109.6 4.8 %collective-permute-start.8 = (f32[8,384]{1,0:T(8,128)S(1)}, f32[8,384]{1,0:T(8,128)S(1)}, u32[]{:S(2)}, u32[]{:S(2)}) collective-permute-start(f32[8,384]{1,0:T(8,128)S(1)} %get-tuple-element.52), channel_id=1, source_target_pairs={{0,16},{16,0},{1,17},{17,1},{2,18},{18,2},{3,19},{19,3},{4,20},{20... | collective-permute-start | bytes 36872 | tf_op jit(solution)/shard_map/ppermute | solution.py:441
  113.5 3.5 %collective-permute-start.9 = (f32[8,384]{1,0:T(8,128)S(1)}, f32[8,384]{1,0:T(8,128)S(1)}, u32[]{:S(2)}, u32[]{:S(2)}) collective-permute-start(f32[8,384]{1,0:T(8,128)S(1)} %get-tuple-element.53), channel_id=1, source_target_pairs={{0,240},{16,32},{32,16},{48,64},{64,48},{80,96},{96,80},{112,128},... | collective-permute-start | bytes 36872 | tf_op jit(solution)/shard_map/ppermute | solution.py:441
  125.7 16.6 %all-to-all-start.4 = ((f32[16,8,128]{2,1,0:T(8,128)}), f32[16,8,128]{2,1,0:T(8,128)S(1)}, u32[]{:S(2)}, u32[]{:S(2)}) async-start(f32[16,8,128]{2,1,0:T(8,128)} %broadcast_in_dim.2), calls=%async_computation.4 | async-start | bytes 131072 | tf_op jit(solution)/shard_map/all_to_all | solution.py:521
